TPU v7x, 512 devices: a whole 4x4x16 slice. The times are simulated.
512 devices in a mesh: seq: 64 (over y, z_hi, x), tp: 8 (over z_lo, core).
Axes of the slice: x: 4, y: 4, z: 16 (z_hi: 4, z_lo: 4; z = z_hi * 4 + z_lo), core: 2. Of those that a mesh axis runs over, the one named last changes fastest.
Arguments:
- tokens: bfloat16 [8192, 4096], P('seq'), may hold values from -6 to 6
- w_value: bfloat16 [4096, 4096], P('seq', 'tp'), may hold values from -0.09375 to 0.09375
- w_gate: bfloat16 [4096, 4096], P('seq', 'tp'), may hold values from -0.09375 to 0.09375
- w_output: bfloat16 [4096, 4096], P('tp', 'seq'), may hold values from -0.09375 to 0.09375
- residues: float32 [8, 64, 8, 16], P('tp', 'seq'), may hold values from -1.5 to 1.5
- log_rates: float32 [8, 64, 8, 16], P('tp', 'seq'), as said below
- cotangent: bfloat16 [8192, 4096], P('seq'), may hold values from -6 to 6
Outputs:
- layer_out: bfloat16 [8192, 4096], P('seq', 'tp')
- token_grad: bfloat16 [8192, 4096], P('seq', 'tp')
- residue_grad: float32 [8, 64, 8, 16], P('tp', 'seq')
- log_rate_grad: float32 [8, 64, 8, 16], P('tp', 'seq')
Inputs may be any that keep to these rules, and one draw needn't show every extreme that they name: log_rates lie between log(0.5 / 8192) and log(1 / 24).
All inputs are finite; a program needn't handle non-finite values.
Results may differ from a plain program's by a relative error of at most 0.018.
Values may be sent and summed in bfloat16 or wider, within the bound.
No kernel may reach another device: no remote copies, remote signals or barrier semaphores. Data moves between devices by JAX's collectives and lax.ppermute only.
A program may use at most 64 MiB of HBM per device.

v0:
```python
import math

import jax
import jax.numpy as jnp
from jax import lax
from jax.sharding import PartitionSpec as P


def make_filter(residue_rows, log_rows, length):
    rates = jnp.exp(log_rows)
    offsets = jnp.arange(length).astype(jnp.float32)
    amplitude = residue_rows * jnp.sqrt(2.0 * rates)
    return jnp.sum(
        amplitude[:, :, None] * jnp.exp(-rates[:, :, None] * offsets[None, None, :]), axis=1
    )


def filter_pullback(residue_rows, log_rows, filter_grad, length):
    rates = jnp.exp(log_rows)
    offsets = jnp.arange(length).astype(jnp.float32)
    root = jnp.sqrt(2.0 * rates)
    decay = jnp.exp(-rates[:, :, None] * offsets[None, None, :])
    weighted = filter_grad[:, None, :] * decay
    plain_sum = jnp.sum(weighted, axis=2)
    moment_sum = jnp.sum(weighted * (0.5 - rates[:, :, None] * offsets[None, None, :]), axis=2)
    return (plain_sum * root, residue_rows * root * moment_sum)


def angle_table(rows, cols, period):
    row_ids = lax.broadcasted_iota(jnp.int32, (rows, cols), 0)
    col_ids = lax.broadcasted_iota(jnp.int32, (rows, cols), 1)
    turns = (row_ids * col_ids % period).astype(jnp.float32)
    return turns * (2.0 * math.pi / period)


def make_tables(half_rows, width):
    rows = 2 * half_rows
    first = angle_table(rows, half_rows, rows)
    first_stack = jnp.concatenate([jnp.cos(first), -jnp.sin(first)], axis=0)
    twist = angle_table(rows, width, rows * width)
    twist_cos = jnp.cos(twist)[:, None, :]
    twist_sin = jnp.sin(twist)[:, None, :]
    last = angle_table(width, width, width)
    last_cos = jnp.cos(last)
    last_sin = jnp.sin(last)
    forward_last = jnp.concatenate(
        [
            jnp.concatenate([last_cos, -last_sin], axis=1),
            jnp.concatenate([last_sin, last_cos], axis=1),
        ],
        axis=0,
    )
    inverse_last = jnp.concatenate(
        [
            jnp.concatenate([last_cos, last_sin], axis=1),
            jnp.concatenate([-last_sin, last_cos], axis=1),
        ],
        axis=0,
    )
    return (first_stack, twist_cos, twist_sin, forward_last, inverse_last)


def spectrum(signal, tables):
    first_stack, twist_cos, twist_sin, forward_last, inverse_last = tables
    channels, half_rows, width = signal.shape
    rows = 2 * half_rows
    exact = lax.Precision.HIGHEST
    flat = signal.transpose(1, 0, 2).reshape(half_rows, channels * width)
    stacked = jnp.dot(first_stack, flat, precision=exact, preferred_element_type=jnp.float32)
    a_real = stacked[:rows].reshape(rows, channels, width)
    a_imag = stacked[rows:].reshape(rows, channels, width)
    b_real = a_real * twist_cos + a_imag * twist_sin
    b_imag = a_imag * twist_cos - a_real * twist_sin
    joined = jnp.concatenate([b_real, b_imag], axis=2).reshape(rows * channels, 2 * width)
    result = jnp.dot(joined, forward_last, precision=exact, preferred_element_type=jnp.float32)
    result = result.reshape(rows, channels, 2 * width)
    return (result[:, :, :width], result[:, :, width:])


def signal_of(spec_real, spec_imag, tables):
    first_stack, twist_cos, twist_sin, forward_last, inverse_last = tables
    rows, channels, width = spec_real.shape
    half_rows = rows // 2
    exact = lax.Precision.HIGHEST
    joined = jnp.concatenate([spec_real, spec_imag], axis=2).reshape(rows * channels, 2 * width)
    turned = jnp.dot(joined, inverse_last, precision=exact, preferred_element_type=jnp.float32)
    turned = turned.reshape(rows, channels, 2 * width)
    c_real = turned[:, :, :width]
    c_imag = turned[:, :, width:]
    d_real = c_real * twist_cos - c_imag * twist_sin
    d_imag = c_imag * twist_cos + c_real * twist_sin
    stacked = jnp.concatenate([d_real, d_imag], axis=0).reshape(2 * rows, channels * width)
    result = lax.dot_general(
        first_stack,
        stacked,
        (((0,), (0,)), ((), ())),
        precision=exact,
        preferred_element_type=jnp.float32,
    )
    result = result.reshape(half_rows, channels, width).transpose(1, 0, 2)
    return result / (rows * width)


def product_of(left_real, left_imag, right_real, right_imag):
    return (
        left_real * right_real - left_imag * right_imag,
        left_real * right_imag + left_imag * right_real,
    )


def product_conj(left_real, left_imag, right_real, right_imag):
    return (
        left_real * right_real + left_imag * right_imag,
        left_imag * right_real - left_real * right_imag,
    )


def to_channels(columns):
    return lax.all_to_all(columns, "seq", split_axis=0, concat_axis=1, tiled=True)


def to_tokens(channel_rows):
    return lax.all_to_all(channel_rows, "seq", split_axis=1, concat_axis=0, tiled=True)


def sum_features(term_fn, rows_here):
    return lax.psum_scatter(
        term_fn(jnp.int32(0), rows_here * lax.axis_size("tp")).astype(jnp.bfloat16),
        "tp",
        scatter_dimension=0,
        tiled=True,
    ).astype(jnp.float32)


def local(tokens, w_value, w_gate, w_output, residues, log_rates, cotangent):
    seq_devices = lax.axis_size("seq")
    tok_rows = tokens.shape[0]
    local_width = w_value.shape[1]
    channels = local_width // seq_devices
    length = tok_rows * seq_devices
    out_rows = tokens.shape[1] // lax.axis_size("tp")
    contract_first = (((0,), (1,)), ((), ()))
    tables = make_tables(seq_devices, tok_rows)
    full_value, full_gate, full_output = (
        lax.all_gather(w_value, "seq", axis=0, tiled=True),
        lax.all_gather(w_gate, "seq", axis=0, tiled=True),
        lax.all_gather(w_output, "seq", axis=1, tiled=True),
    )
    value_cols = lax.dot_general(
        full_value, tokens, contract_first, preferred_element_type=jnp.float32
    ).astype(jnp.bfloat16)
    gate_cols = lax.dot_general(
        full_gate, tokens, contract_first, preferred_element_type=jnp.float32
    )
    value_chan = to_channels(value_cols)
    residue_rows = residues.reshape(channels, residues.shape[3])
    log_rows = log_rates.reshape(channels, log_rates.shape[3])
    filters = make_filter(residue_rows, log_rows, length)
    filter_real, filter_imag = spectrum(filters.reshape(channels, seq_devices, tok_rows), tables)
    value_real, value_imag = spectrum(
        value_chan.astype(jnp.float32).reshape(channels, seq_devices, tok_rows), tables
    )
    conv_real, conv_imag = product_of(value_real, value_imag, filter_real, filter_imag)
    conv_chan = (
        signal_of(conv_real, conv_imag, tables).reshape(channels, length).astype(jnp.bfloat16)
    )
    conv_cols = to_tokens(conv_chan)
    mixed = (gate_cols * conv_cols.astype(jnp.float32)).astype(jnp.bfloat16)

    def output_terms(first_row, row_total):
        return lax.dot_general(
            full_output, mixed, (((0,), (0,)), ((), ())), preferred_element_type=jnp.float32
        )

    layer_out = sum_features(output_terms, out_rows).astype(jnp.bfloat16).T
    back = lax.dot_general(
        full_output, cotangent, (((1,), (1,)), ((), ())), preferred_element_type=jnp.float32
    )
    gate_grad = (back * conv_cols.astype(jnp.float32)).astype(jnp.bfloat16)
    conv_grad = (back * gate_cols).astype(jnp.bfloat16)
    grad_chan = to_channels(conv_grad)
    grad_real, grad_imag = spectrum(
        grad_chan.astype(jnp.float32).reshape(channels, seq_devices, tok_rows), tables
    )
    back_real, back_imag = product_conj(grad_real, grad_imag, filter_real, filter_imag)
    value_grad_chan = (
        signal_of(back_real, back_imag, tables).reshape(channels, length).astype(jnp.bfloat16)
    )
    corr_real, corr_imag = product_conj(grad_real, grad_imag, value_real, value_imag)
    filter_grad = signal_of(corr_real, corr_imag, tables).reshape(channels, length)
    residue_grad, rate_grad = filter_pullback(residue_rows, log_rows, filter_grad, length)
    scale = length ** (-0.5)
    value_grad = to_tokens(value_grad_chan)

    def input_terms(first_row, row_total):
        summed = jnp.dot(full_value, value_grad, preferred_element_type=jnp.float32)
        return summed + jnp.dot(full_gate, gate_grad, preferred_element_type=jnp.float32)

    token_grad = sum_features(input_terms, out_rows).astype(jnp.bfloat16).T
    return (
        layer_out,
        token_grad,
        (residue_grad * scale).reshape(residues.shape),
        (rate_grad * scale).reshape(log_rates.shape),
    )


def solution(mesh):
    in_specs = (
        P("seq", None),
        P("seq", "tp"),
        P("seq", "tp"),
        P("tp", "seq"),
        P("tp", "seq", None, None),
        P("tp", "seq", None, None),
        P("seq", None),
    )
    out_specs = (
        P("seq", "tp"),
        P("seq", "tp"),
        P("tp", "seq", None, None),
        P("tp", "seq", None, None),
    )
    return jax.shard_map(local, mesh=mesh, in_specs=in_specs, out_specs=out_specs, check_vma=False)
```

profile of v0, /device:TPU:1, one launch (start us, length us, event | category | flops | bytes accessed | tf_op | source)
XLA Modules:
  0.0 615.0 jit_solution(4162731654677740279)
XLA Ops:
  7.2 0.7 all-gather.8.cloned.1.call-update
  8.0 0.7 all-gather.4.cloned.1.call-update
  8.7 0.7 all-gather.6.cloned.1.call-update
  10.1 0.7 exponential_bitcast_fusion
  10.8 1.3 bitcast_multiply_fusion.8
  12.1 145.2 %all-gather.8.cloned.1.call-done = bf16[512,4096]{0,1:T(8,128)(2,1)} async-done(((bf16[512,64]{0,1:T(8,128)(2,1)}), bf16[512,4096]{0,1:T(8,128)(2,1)}) %all-gather.8.cloned.1.call-update) | async-done | bytes 4194320 | tf_op jit(solution)/shard_map/all_gather | solution.py:147
  157.3 3.8 fusion.110
  161.1 136.8 %all-gather.4.cloned.1.call-done = bf16[4096,512]{1,0:T(8,128)(2,1)} async-done(((bf16[64,512]{1,0:T(8,128)(2,1)}), bf16[4096,512]{1,0:T(8,128)(2,1)}) %all-gather.4.cloned.1.call-update) | async-done | bytes 4194320 | tf_op jit(solution)/shard_map/all_gather | solution.py:146
  297.9 3.5 fusion.109
  301.4 0.7 copy-done.2
  302.1 0.7 fusion.55
  302.8 13.0 %all-to-all-start.2 = ((bf16[64,8,128]{2,1,0:T(8,128)(2,1)}), bf16[64,8,128]{2,1,0:T(8,128)(2,1)S(1)}, u32[]{:S(2)}, u32[]{:S(2)}) async-start(bf16[64,8,128]{2,1,0:T(8,128)(2,1)} %fusion.55), calls=%async_computation.3 | async-start | bytes 262144 | tf_op jit(solution)/shard_map/all_to_all | solution.py:119
  315.8 0.6 iota_convert_fusion
  316.7 122.9 %all-gather.6.cloned.1.call-done = bf16[4096,512]{1,0:T(8,128)(2,1)} async-done(((bf16[64,512]{1,0:T(8,128)(2,1)}), bf16[4096,512]{1,0:T(8,128)(2,1)}) %all-gather.6.cloned.1.call-update) | async-done | bytes 4194320 | tf_op jit(solution)/shard_map/all_gather | solution.py:145
  439.6 4.1 fusion.8
  443.8 13.3 %all-to-all-start = ((bf16[64,8,128]{2,1,0:T(8,128)(2,1)}), bf16[64,8,128]{2,1,0:T(8,128)(2,1)}, u32[]{:S(2)}, u32[]{:S(2)}) async-start(bf16[64,8,128]{2,1,0:T(8,128)(2,1)} %fusion.8), calls=%async_computation | async-start | bytes 262144 | tf_op jit(solution)/shard_map/all_to_all | solution.py:119
  457.3 0.6 fusion.58
  458.8 14.2 %all-to-all-done = bf16[64,8,128]{2,1,0:T(8,128)(2,1)} async-done(((bf16[64,8,128]{2,1,0:T(8,128)(2,1)}), bf16[64,8,128]{2,1,0:T(8,128)(2,1)}, u32[]{:S(2)}, u32[]{:S(2)}) %all-to-all-start) | async-done | bytes 131104 | tf_op jit(solution)/shard_map/all_to_all | solution.py:119
  473.0 1.5 fusion.61
  474.9 1.0 fusion.11
  475.9 1.0 fusion.23
  477.1 1.0 fusion.31
  478.2 1.1 pad_maximum_fusion.2
  479.3 2.5 copy.78
  481.8 2.3 fusion.5
  484.3 3.0 multiply_reduce_fusion
  487.3 1.0 fusion.44
  488.4 1.1 fusion.107
  489.5 2.0 copy.64
  491.5 2.0 copy.65
  493.5 2.0 copy.62
  495.6 2.1 copy.63
  497.6 1.3 multiply_add_fusion.7
  499.0 1.0 fusion.15
  500.3 1.2 fusion.27
  501.5 1.0 fusion.19
  502.5 1.3 multiply_subtract_fusion.2
  504.2 0.3 copy-done.9
  504.6 1.1 fusion.10
  505.8 21.1 %all_to_all.52 = bf16[8,64,128]{2,0,1:T(8,128)(2,1)S(1)} all-to-all(bf16[8,64,128]{2,0,1:T(8,128)(2,1)S(1)} %copy.69), channel_id=1, replica_groups=mesh['seq'=64,'tp'=8] {'seq'}, dimensions={1} | all-to-all | bytes 262144 | tf_op jit(solution)/shard_map/all_to_all | solution.py:123
  526.9 4.7 fusion.1
  532.2 1.1 fusion.9
  533.4 21.2 %all_to_all.53 = bf16[8,64,128]{2,0,1:T(8,128)(2,1)S(1)} all-to-all(bf16[8,64,128]{2,0,1:T(8,128)(2,1)S(1)} %copy.77), channel_id=1, replica_groups=mesh['seq'=64,'tp'=8] {'seq'}, dimensions={1} | all-to-all | bytes 262144 | tf_op jit(solution)/shard_map/all_to_all | solution.py:123
  554.6 3.7 fusion.64
  558.4 2.5 fusion.2
  560.9 0.6 fusion.92
  561.5 3.1 reduce-scatter.3.cloned.1.call-done
  564.6 43.9 %reduce-scatter.5.cloned.1.call-done = bf16[512,128]{0,1:T(8,128)(2,1)} async-done(((bf16[4096,128]{0,1:T(8,128)(2,1)}), bf16[512,128]{0,1:T(8,128)(2,1)}) %reduce-scatter.5.cloned.1.call-update) | async-done | bytes 131088 | tf_op jit(solution)/shard_map/reduce_scatter | solution.py:127
  (59 shorter events, 4.4 us)
Async XLA Ops:
  7.2 290.7 %copy-start = (bf16[128,4096]{1,0:T(8,128)(2,1)S(1)}, bf16[128,4096]{1,0:T(8,128)(2,1)}, u32[]{:S(2)}) copy-start(bf16[128,4096]{1,0:T(8,128)(2,1)} %param.7) | copy-start | bytes 3145732
  7.2 150.2 %all-gather.8.cloned.1.call-start = ((), (), s32[]{:S(2)}) async-start(), calls=%async_computation.8 | async-start | bytes 4259840 | tf_op jit(solution)/shard_map/all_gather | solution.py:147
  7.9 290.0 %all-gather.4.cloned.1.call-start = ((), (), s32[]{:S(2)}) async-start(), calls=%async_computation.6 | async-start | bytes 4259840 | tf_op jit(solution)/shard_map/all_gather | solution.py:146
  8.7 431.0 %all-gather.6.cloned.1.call-start = ((), (), s32[]{:S(2)}) async-start(), calls=%async_computation.7 | async-start | bytes 4259840 | tf_op jit(solution)/shard_map/all_gather | solution.py:145
  9.8 477.5 %copy-start.8 = (f32[128,64]{0,1:T(8,128)}, f32[128,64]{0,1:T(8,128)S(1)}, u32[]{:S(2)}) copy-start(f32[128,64]{0,1:T(8,128)S(1)} %get-tuple-element.41) | copy-start | bytes 98308
  9.8 477.5 %copy-start.10 = (f32[128,64]{0,1:T(8,128)}, f32[128,64]{0,1:T(8,128)S(1)}, u32[]{:S(2)}) copy-start(f32[128,64]{0,1:T(8,128)S(1)} %get-tuple-element.42) | copy-start | bytes 98308
  161.1 282.7 %copy-start.4 = (f32[512,128]{1,0:T(8,128)}, f32[512,128]{1,0:T(8,128)S(1)}, u32[]{:S(2)}) copy-start(f32[512,128]{1,0:T(8,128)S(1)} %fusion.110) | copy-start | bytes 786436
  301.4 0.7 copy-start.2
  302.8 141.0 %all-to-all-start.2 = ((bf16[64,8,128]{2,1,0:T(8,128)(2,1)}), bf16[64,8,128]{2,1,0:T(8,128)(2,1)S(1)}, u32[]{:S(2)}, u32[]{:S(2)}) async-start(bf16[64,8,128]{2,1,0:T(8,128)(2,1)} %fusion.55), calls=%async_computation.3 | async-start | bytes 262144 | tf_op jit(solution)/shard_map/all_to_all | solution.py:119
  443.8 29.2 %all-to-all-start = ((bf16[64,8,128]{2,1,0:T(8,128)(2,1)}), bf16[64,8,128]{2,1,0:T(8,128)(2,1)}, u32[]{:S(2)}, u32[]{:S(2)}) async-start(bf16[64,8,128]{2,1,0:T(8,128)(2,1)} %fusion.8), calls=%async_computation | async-start | bytes 262144 | tf_op jit(solution)/shard_map/all_to_all | solution.py:119
  457.1 107.5 %reduce-scatter.3.cloned.1.call-start = ((), (), s32[]{:S(2)}) async-start(), calls=%async_computation.9 | async-start | bytes 1179648 | tf_op jit(solution)/shard_map/reduce_scatter | solution.py:127
  502.5 24.3 %copy-start.3 = (f32[512,128]{1,0:T(8,128)S(1)}, f32[512,128]{1,0:T(8,128)}, u32[]{:S(2)}) copy-start(f32[512,128]{1,0:T(8,128)} %copy-done.2) | copy-start | bytes 786436
  503.8 0.8 copy-start.9
  503.8 0.8 copy-start.11
  504.6 27.1 %copy-start.6 = (f32[128,8,128]{2,0,1:T(8,128)S(1)}, f32[128,8,128]{2,0,1:T(8,128)}, u32[]{:S(2)}) copy-start(f32[128,8,128]{2,0,1:T(8,128)} %get-tuple-element.13) | copy-start | bytes 1572868
  504.6 27.1 %copy-start.7 = (f32[128,8,128]{2,0,1:T(8,128)S(1)}, f32[128,8,128]{2,0,1:T(8,128)}, u32[]{:S(2)}) copy-start(f32[128,8,128]{2,0,1:T(8,128)} %get-tuple-element.14) | copy-start | bytes 1572868
  526.9 4.8 copy-start.12
  531.6 76.8 %reduce-scatter.5.cloned.1.call-start = ((), (), s32[]{:S(2)}) async-start(), calls=%async_computation.10 | async-start | bytes 1179648 | tf_op jit(solution)/shard_map/reduce_scatter | solution.py:127
  532.1 26.2 %copy-start.1 = (bf16[4096,512]{1,0:T(8,128)(2,1)S(1)}, bf16[4096,512]{1,0:T(8,128)(2,1)}, u32[]{:S(2)}) copy-start(bf16[4096,512]{1,0:T(8,128)(2,1)} %all-gather.4.cloned.1.call-done) | copy-start | bytes 12582916
  532.1 26.2 %copy-start.5 = (f32[512,128]{1,0:T(8,128)S(1)}, f32[512,128]{1,0:T(8,128)}, u32[]{:S(2)}) copy-start(f32[512,128]{1,0:T(8,128)} %copy-done.4) | copy-start | bytes 786436
  532.1 26.2 %copy-start.13 = (bf16[8,64,128]{2,0,1:T(8,128)(2,1)S(1)}, bf16[8,64,128]{2,0,1:T(8,128)(2,1)}, u32[]{:S(2)}) copy-start(bf16[8,64,128]{2,0,1:T(8,128)(2,1)} %copy-done.12) | copy-start | bytes 393220
  558.3 2.5 copy-start.14
  558.3 2.5 copy-start.15
Sparse Core Ops, SparseCore 0:
  12.2 145.1 all-gather.7
  161.5 136.3 all-gather.3
  302.1 137.4 all-gather.5
  531.7 32.8 reduce-scatter.2
  567.8 40.5 reduce-scatter.4
where the time goes:
time: 618 us; the launch traced here: 615 us
  waiting for transfers between devices  468 us (76%)
  blocking collectives  42.3 us (7%)
  matrix products  36.2 us (6%)
  starting transfers between devices  26.7 us (4%)
  local copies, waits for them, and re-layouts  15.5 us (3%)
  between operations  14.2 us (2%)
  other arithmetic  11.9 us (2%)
    all_gather x1, waiting for transfers between devices, local(): lax.all_gather(w_output, 'seq', axis=1, tiled=True)  145 us
    all_gather x1, waiting for transfers between devices, local(): lax.all_gather(w_gate, 'seq', axis=0, tiled=True)  137 us
    all_gather x1, waiting for transfers between devices, local(): lax.all_gather(w_value, 'seq', axis=0, tiled=True)  123 us
    reduce_scatter x2, waiting for transfers between devices, sum_features(): lax.psum_scatter(term_fn(jnp.int32(0), rows_here * lax.axis_size('tp')).a...  47 us
    all_to_all x2, blocking collectives, to_tokens(): lax.all_to_all(channel_rows, 'seq', split_axis=1, concat_axis=0, tiled=True)  42.3 us
    all_to_all x2, starting transfers between devices, to_channels(): lax.all_to_all(columns, 'seq', split_axis=0, concat_axis=1, tiled=True)  26.3 us
    all_to_all x2, waiting for transfers between devices, to_channels(): lax.all_to_all(columns, 'seq', split_axis=0, concat_axis=1, tiled=True)  14.2 us
  transfers between devices with their start and end apart: 7, of which 6 were waited for; matrix products, arithmetic and copies ran while one was open for 4% of the time, Pallas kernels for 0%

commit v1 on v0

v1 whole, which is shorter than its diff:
```python
import jax
import jax.numpy as jnp
from jax import lax
from jax.experimental import pallas as pl
from jax.experimental.pallas import tpu as pltpu
from jax.sharding import PartitionSpec as P

EXACT = lax.Precision.HIGHEST
VMEM_GRANT = 56 * 2**20


def groups_along(sizes, picked):
    groups = {}
    total = 1
    for size in sizes:
        total *= size
    for index in range(total):
        rest, coords = index, []
        for size in reversed(sizes):
            coords.append(rest % size)
            rest //= size
        coords.reverse()
        key = tuple(c for axis, c in enumerate(coords) if axis not in picked)
        groups.setdefault(key, []).append(index)
    return list(groups.values())


def exchange(blocks, axis, groups=None):
    return lax.all_to_all(
        blocks, axis, split_axis=0, concat_axis=0, tiled=True, axis_index_groups=groups
    )


def batched(spec, left, right):
    return jnp.einsum(spec, left, right, precision=EXACT, preferred_element_type=jnp.float32)


def mode_tables(residue_rows, log_rows, chunks, width):
    rates = jnp.exp(log_rows)
    root = jnp.sqrt(2.0 * rates)
    amplitude = residue_rows * root
    channels, modes = rates.shape
    steps = jnp.arange(width).astype(jnp.float32)
    lag = steps[None, :] - steps[:, None]
    to_end = width - 1.0 - steps
    grow = jnp.exp(rates[:, :, None] * steps[None, None, :])
    fade = jnp.exp(-rates[:, :, None] * steps[None, None, :])
    near = batched("cru,crt->cut", amplitude[:, :, None] * grow, fade)
    near = jnp.where((lag >= 0.0)[None], near, 0.0)
    into = jnp.exp(-rates[:, :, None] * to_end[None, None, :])
    out_of = jnp.exp(-rates[:, :, None] * (steps + 1.0)[None, None, :])

    def wide(table):
        own = jnp.eye(channels, dtype=jnp.float32)[:, :, None, None]
        return (own * table[None]).reshape(channels, channels * modes, width)

    filters = jnp.stack(
        [
            wide(into).swapaxes(1, 2),
            wide(out_of).swapaxes(1, 2),
            near,
            near.swapaxes(1, 2),
            wide(amplitude[:, :, None] * out_of),
            wide(amplitude[:, :, None] * into),
        ]
    )
    high = lax.reduce_precision(filters, 8, 7)
    low = (filters - high).astype(jnp.bfloat16)
    spans = width * 2.0 ** jnp.arange(8).astype(jnp.float32)
    hops = jnp.exp(-rates.reshape(1, -1) * spans[:, None])
    return {
        "rates": rates,
        "root": root,
        "grow": grow,
        "fade": fade,
        "into": into,
        "out_of": out_of,
        "high": high.astype(jnp.bfloat16),
        "low": low,
        "hops": hops,
    }


def filter_kernel(signal, high, low, hops, filtered, states):
    channels, chunks = signal.shape[1:3]
    modes = hops.shape[1]

    def dot(left, right):
        return jnp.dot(left, right, preferred_element_type=jnp.float32)

    def times(left, table, c):
        return dot(left, high[table, c]) + dot(left, low[table, c])

    head = jnp.zeros((chunks, modes), jnp.float32)
    tail = jnp.zeros((chunks, modes), jnp.float32)
    for c in range(channels):
        head = head + times(signal[0, c], 0, c)
        tail = tail + times(signal[1, c], 1, c)
    place = lax.broadcasted_iota(jnp.int32, (chunks, modes), 0)

    def later(array, step):
        return jnp.where(place >= step, pltpu.roll(array, step, 0), 0.0)

    def earlier(array, step):
        return jnp.where(place < chunks - step, pltpu.roll(array, chunks - step, 0), 0.0)

    ahead, behind = later(head, 1), earlier(tail, 1)
    step, level = 1, 0
    while step < chunks:
        hop = hops[level : level + 1, :]
        ahead = ahead + hop * later(ahead, step)
        behind = behind + hop * earlier(behind, step)
        step, level = 2 * step, level + 1
    states[0], states[1], states[2] = head, tail, ahead
    for which, state in ((0, ahead), (1, behind)):
        rough = state.astype(jnp.bfloat16)
        fine = (state - rough.astype(jnp.float32)).astype(jnp.bfloat16)
        for c in range(channels):
            far = times(rough, 4 + which, c) + dot(fine, high[4 + which, c])
            filtered[which, c] = (times(signal[which, c], 2 + which, c) + far).astype(jnp.bfloat16)


def filter_both(signal, tables):
    channels, chunks = signal.shape[1:3]
    modes = tables["hops"].shape[1]
    return pl.pallas_call(
        filter_kernel,
        out_shape=(
            jax.ShapeDtypeStruct(signal.shape, jnp.bfloat16),
            jax.ShapeDtypeStruct((3, chunks, modes), jnp.float32),
        ),
        in_specs=[pl.BlockSpec(memory_space=pltpu.VMEM)] * 4,
        out_specs=(pl.BlockSpec(memory_space=pltpu.VMEM),) * 2,
        compiler_params=pltpu.CompilerParams(vmem_limit_bytes=24 * 2**20),
        cost_estimate=pl.CostEstimate(flops=200_000_000, bytes_accessed=4_000_000, transcendentals=0),
    )(signal, tables["high"], tables["low"], tables["hops"])


def fetch(weights, held, arrived):
    side_y, _, side_z = weights.shape[:3]
    copies = [
        pltpu.make_async_copy(
            weights.at[i // side_z, :, i % side_z], held.at[i], arrived.at[i]
        )
        for i in range(side_y * side_z)
    ]
    for copy in copies:
        copy.start()

    def block(i):
        copies[i].wait()
        return held[i].reshape(-1, held.shape[3])

    return block


def project_kernel(
    tokens, cotangent, weights, gates, back, sent, held, arrived, total, back_total
):
    width = gates.shape[0]
    block = fetch(weights, held, arrived)
    depth = held.shape[1] * held.shape[2]
    for i in range(held.shape[0]):
        rows = block(i)
        columns = slice(i * depth, (i + 1) * depth)
        term = jnp.dot(
            tokens[:, columns], rows[:, : 2 * width], preferred_element_type=jnp.float32
        )
        back_term = jnp.dot(
            cotangent[:, columns], rows[:, 2 * width :], preferred_element_type=jnp.float32
        )
        if i == 0:
            total[...] = term
            back_total[...] = back_term
        else:
            total[...] += term
            back_total[...] += back_term
    gates[...] = total[:, width:].T
    back[...] = back_total[...].T
    sent[0] = total[:, :width].T.astype(jnp.bfloat16)
    sent[1] = (back[...] * gates[...]).astype(jnp.bfloat16)


def held_blocks(weights):
    side_y, side_x, side_z, deep, wide = weights.shape
    return [
        pltpu.VMEM((side_y * side_z, side_x, deep, wide), weights.dtype),
        pltpu.SemaphoreType.DMA((side_y * side_z,)),
    ]


def project(tokens, cotangent, weights):
    rows = tokens.shape[0]
    width = weights.shape[4] // 3
    here = pl.BlockSpec(memory_space=pltpu.VMEM)
    return pl.pallas_call(
        project_kernel,
        out_shape=(
            jax.ShapeDtypeStruct((width, rows), jnp.float32),
            jax.ShapeDtypeStruct((width, rows), jnp.float32),
            jax.ShapeDtypeStruct((2, width, rows), jnp.bfloat16),
        ),
        in_specs=[here, here, pl.BlockSpec(memory_space=pl.ANY)],
        out_specs=(here, here, here),
        scratch_shapes=held_blocks(weights)
        + [
            pltpu.VMEM((rows, 2 * width), jnp.float32),
            pltpu.VMEM((rows, width), jnp.float32),
        ],
        compiler_params=pltpu.CompilerParams(vmem_limit_bytes=VMEM_GRANT),
    )(tokens, cotangent, weights)


def out_kernel(gates, back, filtered, weights, parts, held, arrived, mixed, grads):
    width = gates.shape[0]
    block = fetch(weights, held, arrived)
    conv = filtered[0].astype(jnp.float32)
    mixed[...] = (gates[...] * conv).astype(jnp.bfloat16)
    grads[:width] = filtered[1]
    grads[width:] = (back[...] * conv).astype(jnp.bfloat16)
    side_y, side_z = weights.shape[0], weights.shape[2]
    depth = held.shape[1] * held.shape[2]
    for i in range(side_y * side_z):
        y, z = i // side_z, i % side_z
        rows = block(i)
        columns = slice(z % 2 * depth, (z % 2 + 1) * depth)
        out = jnp.dot(rows[:, 2 * width :], mixed[...], preferred_element_type=jnp.float32)
        parts[z // 2, y, 0, :, columns] = out.T.astype(jnp.bfloat16)
        out = jnp.dot(rows[:, : 2 * width], grads[...], preferred_element_type=jnp.float32)
        parts[z // 2, y, 1, :, columns] = out.T.astype(jnp.bfloat16)


def project_back(gates, back, filtered, weights):
    width, rows = gates.shape
    side_y, side_x, side_z, deep, _ = weights.shape
    here = pl.BlockSpec(memory_space=pltpu.VMEM)
    return pl.pallas_call(
        out_kernel,
        out_shape=jax.ShapeDtypeStruct(
            (side_z // 2, side_y, 2, rows, 2 * side_x * deep), jnp.bfloat16
        ),
        in_specs=[here, here, here, pl.BlockSpec(memory_space=pl.ANY)],
        out_specs=here,
        scratch_shapes=held_blocks(weights)
        + [
            pltpu.VMEM((width, rows), jnp.bfloat16),
            pltpu.VMEM((2 * width, rows), jnp.bfloat16),
        ],
        compiler_params=pltpu.CompilerParams(vmem_limit_bytes=VMEM_GRANT),
    )(gates, back, filtered, weights)


def by_chunk(states):
    return states.reshape(-1, states.shape[2]).T


def parameter_grads(signal, grad, head, tail, ahead, residue_rows, tables):
    chunks, width = signal.shape[1:]
    steps = jnp.arange(width).astype(jnp.float32)
    lag = jnp.maximum(steps[None, :] - steps[:, None], -1.0)[None]
    overlap = jnp.where(lag >= 0.0, batched("cku,ckt->cut", signal, grad), 0.0)
    grow, fade = tables["grow"], tables["fade"]
    shape = residue_rows.shape
    plain = jnp.sum(batched("cut,crt->cru", overlap, fade) * grow, axis=2)
    plain = plain + jnp.sum(ahead * tail, axis=0).reshape(shape)
    into_moment = tables["into"] * (width - 1.0 - steps)[None, None, :]
    out_moment = tables["out_of"] * (steps + 1.0)[None, None, :]
    head_moment = by_chunk(batched("cku,cru->crk", signal, into_moment))
    tail_moment = by_chunk(batched("ckt,crt->crk", grad, out_moment))
    blocks = jnp.arange(chunks).astype(jnp.float32)
    gap = (blocks[:, None] - blocks[None, :] - 1.0)[:, :, None]
    hop = width * jnp.maximum(gap, 0.0)
    carry = jnp.where(gap >= 0.0, jnp.exp(-tables["rates"].reshape(1, 1, -1) * hop), 0.0)
    ahead_moment = jnp.sum(carry * (head_moment[None] + hop * head[None]), axis=1)
    far = jnp.sum(ahead * tail_moment + ahead_moment * tail, axis=0).reshape(shape)
    moment = jnp.sum(batched("cut,crt->cru", overlap * lag, fade) * grow, axis=2) + far
    root = tables["root"]
    return plain * root, residue_rows * root * (0.5 * plain - tables["rates"] * moment)


def local(tokens, w_value, w_gate, w_output, residues, log_rates, cotangent):
    seq_devices, tp_devices = lax.axis_size("seq"), lax.axis_size("tp")
    side = 4
    sizes, tp_sizes = (side, side, seq_devices // side**2), (tp_devices // 2, 2)
    z_groups, yx_groups = groups_along(sizes, (1,)), groups_along(sizes, (0, 2))
    core_groups, line_groups = groups_along(tp_sizes, (1,)), groups_along(tp_sizes, (0,))
    rows, model = tokens.shape
    block, width = w_value.shape
    channels = width // seq_devices
    half = jnp.bfloat16

    weights = jnp.concatenate([w_value, w_gate, w_output.T], axis=1)
    along_z = lax.all_gather(weights, "seq", axis=0, tiled=True, axis_index_groups=z_groups)

    along_z, residues, log_rates = lax.optimization_barrier((along_z, residues, log_rates))
    full = lax.all_gather(along_z, "seq", axis=0, tiled=True, axis_index_groups=yx_groups)
    residue_rows = residues.reshape(channels, residues.shape[3])
    log_rows = log_rates.reshape(channels, log_rates.shape[3])
    tables = mode_tables(residue_rows, log_rows, seq_devices, rows)
    full, tables = lax.optimization_barrier((full, tables))
    full = full.reshape(side, side, side, block, 3 * width)

    gates, back, sent = project(tokens, cotangent, full)
    sent = sent.reshape(2, seq_devices, channels, rows).swapaxes(0, 1)
    got = exchange(sent, "seq").transpose(1, 2, 0, 3)
    filtered, states = filter_both(got, tables)
    got_back = exchange(filtered.transpose(2, 0, 1, 3), "seq")
    got_back = got_back.swapaxes(0, 1).reshape(2, width, rows)
    parts = project_back(gates, back, got_back, full)

    pair = exchange(parts, "tp", core_groups).astype(jnp.float32)
    pair = (pair[0] + pair[1]).astype(half)
    pair, got, states = lax.optimization_barrier((pair, got, states))
    line = exchange(pair, "tp", line_groups).astype(jnp.float32)
    summed = ((line[0] + line[1]) + (line[2] + line[3])).astype(half)
    result = summed.reshape(2, rows, model // tp_devices)

    signal, grad = got[0].astype(jnp.float32), got[1].astype(jnp.float32)
    residue_grad, rate_grad = parameter_grads(
        signal, grad, states[0], states[1], states[2], residue_rows, tables
    )
    scale = (rows * seq_devices) ** (-0.5)
    return (
        result[0],
        result[1],
        (residue_grad * scale).reshape(residues.shape),
        (rate_grad * scale).reshape(log_rates.shape),
    )


def solution(mesh):
    in_specs = (
        P("seq", None),
        P("seq", "tp"),
        P("seq", "tp"),
        P("tp", "seq"),
        P("tp", "seq", None, None),
        P("tp", "seq", None, None),
        P("seq", None),
    )
    out_specs = (
        P("seq", "tp"),
        P("seq", "tp"),
        P("tp", "seq", None, None),
        P("tp", "seq", None, None),
    )
    return jax.shard_map(local, mesh=mesh, in_specs=in_specs, out_specs=out_specs, check_vma=False)
```

time: 618 us -> 290 us (0.47)
  waiting for transfers between devices: 468 us -> 113 us
  blocking collectives: 42.3 us -> 114 us
  matrix products: 36.2 us -> 4.79 us
  starting transfers between devices: 26.7 us -> 4.4 us
  Pallas kernels: 0 us -> 19.3 us
  local copies, waits for them, and re-layouts: 15.5 us -> 3.64 us
    all_gather x3 -> x1, waiting for transfers between devices: 405 us -> 93.9 us  [local(): lax.all_gather(along_z, 'seq', axis=0, tiled=True, axis_index_groups=yx_g...]
    reduce_scatter x2 -> x0, waiting for transfers between devices: 47 us -> none  [sum_features(): lax.psum_scatter(term_fn(jnp.int32(0), rows_here * lax.axis_size('tp')).a...]
    all_gather x0 -> x1, blocking collectives: none -> 39.1 us  [local(): lax.all_gather(weights, 'seq', axis=0, tiled=True, axis_index_groups=z_gr...]
    all_to_all x2 -> x3, blocking collectives: 42.3 us -> 74.7 us  [exchange(): lax.all_to_all(blocks, axis, split_axis=0, concat_axis=0, tiled=True, axi...]
    dot_general x18 -> x6, matrix products: 36.2 us -> 4.79 us  [batched(): jnp.einsum(spec, left, right, precision=EXACT, preferred_element_type=jnp...]
    all_to_all x2 -> x1, starting transfers between devices: 26.3 us -> 4.36 us  [exchange(): lax.all_to_all(blocks, axis, split_axis=0, concat_axis=0, tiled=True, axi...]
    pallas_call x0 -> x3, Pallas kernels: none -> 19.3 us  [the longest x1 10.6 us: project_back(): pl.pallas_call(out_kernel, out_shape=jax.ShapeDtypeStruct((side_z // 2, s...]
    all_to_all x2 -> x1, waiting for transfers between devices: 14.2 us -> 19.5 us  [exchange(): lax.all_to_all(blocks, axis, split_axis=0, concat_axis=0, tiled=True, axi...]
  transfers between devices with their start and end apart: 7 -> 2, of which waited for: 6 -> 2; matrix products, arithmetic and copies ran while one was open for 4% -> 6% of each run, Pallas kernels for 0% -> 0%
where the time goes in v1:
time: 290 us; the launch traced here: 289 us
  blocking collectives  114 us (39%)
  waiting for transfers between devices  113 us (39%)
  Pallas kernels  19.3 us (7%)
  other arithmetic  15.5 us (5%)
  between operations  14.2 us (5%)
  matrix products  4.79 us (2%)
  starting transfers between devices  4.4 us (2%)
  local copies, waits for them, and re-layouts  3.64 us (1%)
    all_gather x1, waiting for transfers between devices, local(): lax.all_gather(along_z, 'seq', axis=0, tiled=True, axis_index_groups=yx_g...  93.9 us
    all_to_all x3, blocking collectives, exchange(): lax.all_to_all(blocks, axis, split_axis=0, concat_axis=0, tiled=True, axi...  74.7 us
    all_gather x1, blocking collectives, local(): lax.all_gather(weights, 'seq', axis=0, tiled=True, axis_index_groups=z_gr...  39.1 us
    all_to_all x1, waiting for transfers between devices, exchange(): lax.all_to_all(blocks, axis, split_axis=0, concat_axis=0, tiled=True, axi...  19.5 us
    pallas_call x1, Pallas kernels, project_back(): pl.pallas_call(out_kernel, out_shape=jax.ShapeDtypeStruct((side_z // 2, s...  10.6 us
    pallas_call x1, Pallas kernels, project(): pl.pallas_call(project_kernel, out_shape=(jax.ShapeDtypeStruct((width, ro...  7.52 us
  transfers between devices with their start and end apart: 2, of which 2 were waited for; matrix products, arithmetic and copies ran while one was open for 6% of the time, Pallas kernels for 0%

profile of v1, /device:TPU:1, one launch (start us, length us, event | category | flops | bytes accessed | tf_op | source)
XLA Modules:
  0.0 289.1 jit_solution(16091952333231970066)
XLA Ops:
  7.2 0.9 pad_maximum_fusion
  8.1 39.1 %all_gather.6 = bf16[256,1536]{1,0:T(8,128)(2,1)} all-gather(bf16[64,1536]{1,0:T(8,128)(2,1)S(1)} %pad_maximum_fusion), channel_id=1, replica_groups={{0,32,64,96},{8,40,72,104},{16,48,80,112},{24,56,88,120},{128,160,192,2..., dimensions={0}, use_global_device_ids=true | all-gather | bytes 983040 | tf_op jit(solution)/shard_map/all_gather | solution.py:293
  47.3 0.7 sqrt_multiply_fusion
  48.0 0.1 neg.35
  48.1 0.1 mul.394
  48.2 0.1 mul.374
  48.3 0.7 multiply_sqrt_fusion
  49.0 0.1 broadcast_compare_fusion
  49.2 0.1 exponential_multiply_fusion
  49.3 0.9 multiply_dynamic-update-slice_fusion.3
  50.2 0.9 multiply_dynamic-update-slice_fusion.2
  51.0 1.9 bitcast_dynamic-update-slice_fusion.1
  52.9 0.2 copy.27
  53.2 0.8 multiply_exponential_fusion
  54.0 0.8 bitcast_dynamic-update-slice_fusion
  54.8 1.0 multiply_dynamic-update-slice_fusion.1
  55.8 1.0 multiply_dynamic-update-slice_fusion
  56.8 2.8 fusion
  59.6 93.9 %all-gather.2.cloned.1.call-done = bf16[4096,1536]{1,0:T(8,128)(2,1)} async-done(((bf16[256,1536]{1,0:T(8,128)(2,1)}), bf16[4096,1536]{1,0:T(8,128)(2,1)}) %all-gather.2.cloned.1.call-update) | async-done | bytes 12582928 | tf_op jit(solution)/shard_map/all_gather | solution.py:296
  153.5 7.5 %shard_map.102 = (f32[512,128]{1,0:T(8,128)}, f32[512,128]{1,0:T(8,128)}, bf16[2,512,128]{2,1,0:T(8,128)(2,1)}) custom-call(bf16[128,4096]{1,0:T(8,128)(2,1)} %tokens.1, bf16[128,4096]{1,0:T(8,128)(2,1)} %cotangent.1, bf16[4,4,4,64,1536]{4,3,2,1,0:T(8,128)(2,1)} %bitcast.93), custom_call_target="tpu_custom_call" | custom-call | tf_op jit(solution)/shard_map/pallas_call | solution.py:196
  161.0 1.0 copy.28
  162.0 35.6 %all_to_all.20 = bf16[64,2,8,128]{3,2,1,0:T(8,128)(2,1)S(1)} all-to-all(bf16[64,2,8,128]{3,2,1,0:T(8,128)(2,1)S(1)} %copy.28), channel_id=1, replica_groups=mesh['seq'=64,'tp'=8] {'seq'}, dimensions={0} | all-to-all | bytes 524288 | tf_op jit(solution)/shard_map/all_to_all | solution.py:29
  197.7 1.2 shard_map.103
  199.0 0.2 copy.30
  199.2 29.0 %all_to_all.21 = bf16[64,2,8,128]{3,2,1,0:T(8,128)(2,1)S(1)} all-to-all(bf16[64,2,8,128]{3,2,1,0:T(8,128)(2,1)S(1)} %copy.30), channel_id=1, replica_groups=mesh['seq'=64,'tp'=8] {'seq'}, dimensions={0} | all-to-all | bytes 524288 | tf_op jit(solution)/shard_map/all_to_all | solution.py:29
  228.1 0.7 copy_bitcast_fusion.filtered
  228.9 10.6 %shard_map.104 = bf16[2,4,2,128,512]{4,3,2,1,0:T(8,128)(2,1)} custom-call(f32[512,128]{1,0:T(8,128)} %get-tuple-element.29.gates, f32[512,128]{1,0:T(8,128)} %get-tuple-element.30.back, bf16[2,512,128]{2,1,0:T(8,128)(2,1)} %copy_bitcast_fusion.filtered, bf16[4,4,4,64,1536]{4,3,2,1,0:T(8,128)(2,1)} %bitcast.94), custom_call_target="tpu_custom_call" | custom-call | tf_op jit(solution)/shard_map/pallas_call | solution.py:237
  239.4 10.1 %all_to_all.22 = bf16[2,4,2,128,512]{4,3,2,1,0:T(8,128)(2,1)S(1)} all-to-all(bf16[2,4,2,128,512]{4,3,2,1,0:T(8,128)(2,1)} %shard_map.104), channel_id=1, replica_groups={{0,1},{2,3},{4,5},{6,7},{8,9},{10,11},{12,13},{14,15},{16,17},{18,19},{..., dimensions={0} | all-to-all | bytes 4194304 | tf_op jit(solution)/shard_map/all_to_all | solution.py:29
  249.5 0.6 convert_element_type.115
  250.1 1.3 fusion.4
  251.5 4.4 %all-to-all-start.3 = ((bf16[4,2,128,512]{3,2,1,0:T(8,128)(2,1)}), bf16[4,2,128,512]{3,2,1,0:T(8,128)(2,1)S(1)}, u32[]{:S(2)}, u32[]{:S(2)}) async-start(bf16[4,2,128,512]{3,2,1,0:T(8,128)(2,1)} %fusion.4), calls=%async_computation.3 | async-start | bytes 2097152 | tf_op jit(solution)/shard_map/all_to_all | solution.py:29
  255.8 0.1 fusion.26
  255.9 0.1 maximum_multiply_fusion
  256.0 0.1 subtract_maximum_fusion
  256.1 0.1 neg.37
  256.2 0.3 fusion.12
  256.6 0.3 fusion.9
  257.0 1.5 multiply_reduce_fusion
  258.5 0.1 reshape.342
  258.6 0.1 reshape.346
  258.6 0.3 convolution_select_fusion
  259.0 1.0 fusion.2
  260.0 1.0 fusion.3
  261.0 0.6 fusion.32
  261.6 19.5 %all-to-all-done.3 = bf16[4,2,128,512]{3,2,1,0:T(8,128)(2,1)S(1)} async-done(((bf16[4,2,128,512]{3,2,1,0:T(8,128)(2,1)}), bf16[4,2,128,512]{3,2,1,0:T(8,128)(2,1)S(1)}, u32[]{:S(2)}, u32[]{:S(2)}) %all-to-all-start.3) | async-done | bytes 1048608 | tf_op jit(solution)/shard_map/all_to_all | solution.py:29
  281.1 0.3 convert_element_type.118
  281.4 0.2 fusion.6
  281.6 0.7 slice_bitcast_fusion
  (25 shorter events, 0.5 us)
Async XLA Ops:
  7.2 146.3 %all-gather.2.cloned.1.call-start = ((), (), s32[]{:S(2)}) async-start(), calls=%async_computation.4 | async-start | bytes 13369344 | tf_op jit(solution)/shard_map/all_gather | solution.py:296
  250.1 6.1 %copy-start.3 = (f32[8,16,128]{2,1,0:T(8,128)S(1)}, f32[8,16,128]{2,1,0:T(8,128)}, u32[]{:S(2)}) copy-start(f32[8,16,128]{2,1,0:T(8,128)} %get-tuple-element.45) | copy-start | bytes 196612
  250.1 6.4 %copy-start.2 = (f32[8,16,128]{2,1,0:T(8,128)S(1)}, f32[8,16,128]{2,1,0:T(8,128)}, u32[]{:S(2)}) copy-start(f32[8,16,128]{2,1,0:T(8,128)} %get-tuple-element.44) | copy-start | bytes 196612
  251.5 7.5 %copy-start = (f32[8,16,128]{2,1,0:T(8,128)S(1)}, f32[8,16,128]{2,1,0:T(8,128)}, u32[]{:S(2)}) copy-start(f32[8,16,128]{2,1,0:T(8,128)} %get-tuple-element.38) | copy-start | bytes 196612
  251.5 7.5 %copy-start.1 = (f32[8,16,128]{2,1,0:T(8,128)S(1)}, f32[8,16,128]{2,1,0:T(8,128)}, u32[]{:S(2)}) copy-start(f32[8,16,128]{2,1,0:T(8,128)} %get-tuple-element.40) | copy-start | bytes 196612
  251.5 9.5 %copy-start.4 = (f32[1,1,8,16]{3,2,1,0:T(8,128)S(1)}, f32[1,1,8,16]{3,2,1,0:T(8,128)}, u32[]{:S(2)}) copy-start(f32[1,1,8,16]{3,2,1,0:T(8,128)} %param.11) | copy-start | bytes 1540
  251.5 29.6 %all-to-all-start.3 = ((bf16[4,2,128,512]{3,2,1,0:T(8,128)(2,1)}), bf16[4,2,128,512]{3,2,1,0:T(8,128)(2,1)S(1)}, u32[]{:S(2)}, u32[]{:S(2)}) async-start(bf16[4,2,128,512]{3,2,1,0:T(8,128)(2,1)} %fusion.4), calls=%async_computation.3 | async-start | bytes 2097152 | tf_op jit(solution)/shard_map/all_to_all | solution.py:29
Sparse Core Ops, SparseCore 0:
  47.4 106.0 all-gather.1

commit v2 on v1

--- a/solution.py
+++ b/solution.py
@@ -29,6 +29,33 @@
     return lax.all_to_all(
         blocks, axis, split_axis=0, concat_axis=0, tiled=True, axis_index_groups=groups
     )
+
+
+def shift_pairs(sizes, axis, step):
+    pairs = []
+    for group in groups_along(sizes, (axis,)):
+        pairs += [(group[i], group[(i + step) % len(group)]) for i in range(len(group))]
+    return pairs
+
+
+def shifted(array, sizes, axis, step):
+    return lax.ppermute(array, "seq", shift_pairs(sizes, axis, step))
+
+
+def gather_blocks(own, sizes, near_axis, far_axis):
+    up = shifted(own, sizes, near_axis, -1)
+    down = shifted(own, sizes, near_axis, 1)
+    across = shifted(own, sizes, near_axis, 2)
+    first, second = jnp.concatenate([own, up]), jnp.concatenate([across, down])
+    first_down = shifted(first, sizes, far_axis, 1)
+    second_up = shifted(second, sizes, far_axis, -1)
+    second_down = shifted(second, sizes, far_axis, 1)
+    first_up = shifted(first, sizes, far_axis, -1)
+    first_across = shifted(first_down, sizes, far_axis, 1)
+    second_across = shifted(second_up, sizes, far_axis, -1)
+    return [
+        first, second, first_up, second_up, first_across, second_across, first_down, second_down
+    ]
 
 
 def batched(spec, left, right):
@@ -136,39 +163,59 @@
     )(signal, tables["high"], tables["low"], tables["hops"])
 
 
-def fetch(weights, held, arrived):
-    side_y, _, side_z = weights.shape[:3]
+SIDE = 4
+COUNT = 4 * SIDE
+
+
+def fetch(blocks, held, arrived):
     copies = [
-        pltpu.make_async_copy(
-            weights.at[i // side_z, :, i % side_z], held.at[i], arrived.at[i]
-        )
-        for i in range(side_y * side_z)
+        pltpu.make_async_copy(blocks[i], held.at[i], arrived.at[i]) for i in range(COUNT)
     ]
     for copy in copies:
         copy.start()
 
     def block(i):
         copies[i].wait()
-        return held[i].reshape(-1, held.shape[3])
+        return held[i]
 
     return block
 
 
-def project_kernel(
-    tokens, cotangent, weights, gates, back, sent, held, arrived, total, back_total
-):
+def split_index(i):
+    return i // (2 * SIDE), i // 2 % SIDE, i % 2
+
+
+def project_kernel(place, tokens, cotangent, turn, *refs):
+    blocks, (gates, back, sent, held, arrived, total, back_total, turned) = refs[:COUNT], refs[COUNT:]
     width = gates.shape[0]
-    block = fetch(weights, held, arrived)
-    depth = held.shape[1] * held.shape[2]
-    for i in range(held.shape[0]):
+    block = fetch(blocks, held, arrived)
+    deep = turn.shape[0]
+    piece = deep // SIDE
+    sources = (tokens, cotangent)
+    for z1 in range(2):
+        for distance in range(SIDE):
+            y = lax.rem(place[0] + distance, SIDE)
+            start = pl.multiple_of(y * (2 * deep) + z1 * deep, deep)
+            for which in range(2):
+                turned[which, z1, distance] = jnp.dot(
+                    sources[which][:, pl.ds(start, deep)],
+                    turn[...],
+                    preferred_element_type=jnp.float32,
+                ).astype(jnp.bfloat16)
+
+    def columns(which, i):
+        z1, far, half = split_index(i)
+        if z1 == 0:
+            return turned[which, 0, far, :, half * 2 * piece : (half + 1) * 2 * piece]
+        lanes = slice(far * piece, (far + 1) * piece)
+        return jnp.concatenate(
+            [turned[which, 1, 2 * half, :, lanes], turned[which, 1, 2 * half + 1, :, lanes]], axis=1
+        )
+
+    for i in range(COUNT):
         rows = block(i)
-        columns = slice(i * depth, (i + 1) * depth)
-        term = jnp.dot(
-            tokens[:, columns], rows[:, : 2 * width], preferred_element_type=jnp.float32
-        )
-        back_term = jnp.dot(
-            cotangent[:, columns], rows[:, 2 * width :], preferred_element_type=jnp.float32
-        )
+        term = jnp.dot(columns(0, i), rows[:, : 2 * width], preferred_element_type=jnp.float32)
+        back_term = jnp.dot(columns(1, i), rows[:, 2 * width :], preferred_element_type=jnp.float32)
         if i == 0:
             total[...] = term
             back_total[...] = back_term
@@ -181,17 +228,16 @@
     sent[1] = (back[...] * gates[...]).astype(jnp.bfloat16)
 
 
-def held_blocks(weights):
-    side_y, side_x, side_z, deep, wide = weights.shape
+def held_blocks(blocks):
     return [
-        pltpu.VMEM((side_y * side_z, side_x, deep, wide), weights.dtype),
-        pltpu.SemaphoreType.DMA((side_y * side_z,)),
+        pltpu.VMEM((COUNT,) + blocks[0].shape, blocks[0].dtype),
+        pltpu.SemaphoreType.DMA((COUNT,)),
     ]
 
 
-def project(tokens, cotangent, weights):
+def project(place, tokens, cotangent, turn, blocks):
     rows = tokens.shape[0]
-    width = weights.shape[4] // 3
+    width = blocks[0].shape[1] // 3
     here = pl.BlockSpec(memory_space=pltpu.VMEM)
     return pl.pallas_call(
         project_kernel,
@@ -200,54 +246,64 @@
             jax.ShapeDtypeStruct((width, rows), jnp.float32),
             jax.ShapeDtypeStruct((2, width, rows), jnp.bfloat16),
         ),
-        in_specs=[here, here, pl.BlockSpec(memory_space=pl.ANY)],
+        in_specs=[pl.BlockSpec(memory_space=pltpu.SMEM), here, here, here]
+        + [pl.BlockSpec(memory_space=pl.ANY)] * COUNT,
         out_specs=(here, here, here),
-        scratch_shapes=held_blocks(weights)
+        scratch_shapes=held_blocks(blocks)
         + [
             pltpu.VMEM((rows, 2 * width), jnp.float32),
             pltpu.VMEM((rows, width), jnp.float32),
+            pltpu.VMEM((2, 2, SIDE, rows, turn.shape[0]), jnp.bfloat16),
         ],
         compiler_params=pltpu.CompilerParams(vmem_limit_bytes=VMEM_GRANT),
-    )(tokens, cotangent, weights)
-
-
-def out_kernel(gates, back, filtered, weights, parts, held, arrived, mixed, grads):
+    )(place, tokens, cotangent, turn, *blocks)
+
+
+def out_kernel(place, gates, back, filtered, *refs):
+    blocks, (parts, held, arrived, mixed, grads) = refs[:COUNT], refs[COUNT:]
     width = gates.shape[0]
-    block = fetch(weights, held, arrived)
+    block = fetch(blocks, held, arrived)
     conv = filtered[0].astype(jnp.float32)
     mixed[...] = (gates[...] * conv).astype(jnp.bfloat16)
     grads[:width] = filtered[1]
     grads[width:] = (back[...] * conv).astype(jnp.bfloat16)
-    side_y, side_z = weights.shape[0], weights.shape[2]
-    depth = held.shape[1] * held.shape[2]
-    for i in range(side_y * side_z):
-        y, z = i // side_z, i % side_z
+    deep = held.shape[1]
+    for i in range(COUNT):
+        z1, far, half = split_index(i)
         rows = block(i)
-        columns = slice(z % 2 * depth, (z % 2 + 1) * depth)
-        out = jnp.dot(rows[:, 2 * width :], mixed[...], preferred_element_type=jnp.float32)
-        parts[z // 2, y, 0, :, columns] = out.T.astype(jnp.bfloat16)
-        out = jnp.dot(rows[:, : 2 * width], grads[...], preferred_element_type=jnp.float32)
-        parts[z // 2, y, 1, :, columns] = out.T.astype(jnp.bfloat16)
-
-
-def project_back(gates, back, filtered, weights):
+        outs = (
+            jnp.dot(rows[:, 2 * width :], mixed[...], preferred_element_type=jnp.float32),
+            jnp.dot(rows[:, : 2 * width], grads[...], preferred_element_type=jnp.float32),
+        )
+        for which in range(2):
+            out = outs[which].T.astype(jnp.bfloat16)
+            if z1 == 0:
+                y = lax.rem(place[0] + far, SIDE)
+                parts[0, y, which, :, half * deep : (half + 1) * deep] = out
+            else:
+                for part in range(2):
+                    y = lax.rem(place[0] + 2 * half + part, SIDE)
+                    piece = slice(far * (deep // 2), (far + 1) * (deep // 2))
+                    parts[1, y, which, :, piece] = out[:, part * (deep // 2) : (part + 1) * (deep // 2)]
+
+
+def project_back(place, gates, back, filtered, blocks):
     width, rows = gates.shape
-    side_y, side_x, side_z, deep, _ = weights.shape
+    deep = blocks[0].shape[0]
     here = pl.BlockSpec(memory_space=pltpu.VMEM)
     return pl.pallas_call(
         out_kernel,
-        out_shape=jax.ShapeDtypeStruct(
-            (side_z // 2, side_y, 2, rows, 2 * side_x * deep), jnp.bfloat16
-        ),
-        in_specs=[here, here, here, pl.BlockSpec(memory_space=pl.ANY)],
+        out_shape=jax.ShapeDtypeStruct((2, SIDE, 2, rows, 2 * deep), jnp.bfloat16),
+        in_specs=[pl.BlockSpec(memory_space=pltpu.SMEM), here, here, here]
+        + [pl.BlockSpec(memory_space=pl.ANY)] * COUNT,
         out_specs=here,
-        scratch_shapes=held_blocks(weights)
+        scratch_shapes=held_blocks(blocks)
         + [
             pltpu.VMEM((width, rows), jnp.bfloat16),
             pltpu.VMEM((2 * width, rows), jnp.bfloat16),
         ],
         compiler_params=pltpu.CompilerParams(vmem_limit_bytes=VMEM_GRANT),
-    )(gates, back, filtered, weights)
+    )(place, gates, back, filtered, *blocks)
 
 
 def by_chunk(states):
@@ -280,40 +336,50 @@
 
 def local(tokens, w_value, w_gate, w_output, residues, log_rates, cotangent):
     seq_devices, tp_devices = lax.axis_size("seq"), lax.axis_size("tp")
-    side = 4
-    sizes, tp_sizes = (side, side, seq_devices // side**2), (tp_devices // 2, 2)
-    z_groups, yx_groups = groups_along(sizes, (1,)), groups_along(sizes, (0, 2))
+    sizes, tp_sizes = (SIDE, SIDE, seq_devices // SIDE**2), (tp_devices // 2, 2)
+    z_groups = groups_along(sizes, (1,))
     core_groups, line_groups = groups_along(tp_sizes, (1,)), groups_along(tp_sizes, (0,))
     rows, model = tokens.shape
     block, width = w_value.shape
     channels = width // seq_devices
     half = jnp.bfloat16
+    me = lax.axis_index("seq")
 
     weights = jnp.concatenate([w_value, w_gate, w_output.T], axis=1)
     along_z = lax.all_gather(weights, "seq", axis=0, tiled=True, axis_index_groups=z_groups)
-
-    along_z, residues, log_rates = lax.optimization_barrier((along_z, residues, log_rates))
-    full = lax.all_gather(along_z, "seq", axis=0, tiled=True, axis_index_groups=yx_groups)
+    along_z = along_z.reshape(2, 2 * block, 3 * width)
+    blocks = gather_blocks(along_z[0], sizes, 2, 0) + gather_blocks(along_z[1], sizes, 0, 2)
+
+    place = (me // SIDE**2).reshape(1)
+    deep = 2 * SIDE * block
+    source, target = jnp.arange(deep)[:, None], jnp.arange(deep)[None, :]
+    x_wanted = (me + target // (2 * block)) % SIDE
+    wanted = target // block % 2 * (SIDE * block) + x_wanted * block + target % block
+    turn = (source == wanted).astype(half)
+    passed_on = [blocks[i] for i in (3, 6, 11, 14)]
+    passed_on, residues, log_rates = lax.optimization_barrier((passed_on, residues, log_rates))
     residue_rows = residues.reshape(channels, residues.shape[3])
     log_rows = log_rates.reshape(channels, log_rates.shape[3])
     tables = mode_tables(residue_rows, log_rows, seq_devices, rows)
-    full, tables = lax.optimization_barrier((full, tables))
-    full = full.reshape(side, side, side, block, 3 * width)
-
-    gates, back, sent = project(tokens, cotangent, full)
+    blocks, tables, turn = lax.optimization_barrier((blocks, tables, turn))
+
+    gates, back, sent = project(place, tokens, cotangent, turn, blocks)
     sent = sent.reshape(2, seq_devices, channels, rows).swapaxes(0, 1)
     got = exchange(sent, "seq").transpose(1, 2, 0, 3)
     filtered, states = filter_both(got, tables)
     got_back = exchange(filtered.transpose(2, 0, 1, 3), "seq")
     got_back = got_back.swapaxes(0, 1).reshape(2, width, rows)
-    parts = project_back(gates, back, got_back, full)
+    parts = project_back(place, gates, back, got_back, blocks)
 
     pair = exchange(parts, "tp", core_groups).astype(jnp.float32)
     pair = (pair[0] + pair[1]).astype(half)
     pair, got, states = lax.optimization_barrier((pair, got, states))
     line = exchange(pair, "tp", line_groups).astype(jnp.float32)
     summed = ((line[0] + line[1]) + (line[2] + line[3])).astype(half)
-    result = summed.reshape(2, rows, model // tp_devices)
+    result = lax.dot_general(
+        summed.reshape(2 * rows, -1), turn, (((1,), (1,)), ((), ())), preferred_element_type=jnp.float32
+    )
+    result = result.astype(half).reshape(2, rows, model // tp_devices)
 
     signal, grad = got[0].astype(jnp.float32), got[1].astype(jnp.float32)
     residue_grad, rate_grad = parameter_grads(

time: 290 us -> 261 us (0.900)
  waiting for transfers between devices: 113 us -> 34.3 us
  starting transfers between devices: 4.4 us -> 64.7 us
  between operations: 14.2 us -> 1.25 us
  blocking collectives: 114 us -> 106 us
  other arithmetic: 15.5 us -> 19.7 us
  local copies, waits for them, and re-layouts: 3.64 us -> 6.84 us
    all_gather x1 -> x0, waiting for transfers between devices: 93.9 us -> none  [local(): lax.all_gather(along_z, 'seq', axis=0, tiled=True, axis_index_groups=yx_g...]
    ppermute x0 -> x18, starting transfers between devices: none -> 61 us  [shifted(): return lax.ppermute(array, 'seq', shift_pairs(sizes, axis, step))]
    ppermute x0 -> x18, waiting for transfers between devices: none -> 14.6 us  [shifted(): return lax.ppermute(array, 'seq', shift_pairs(sizes, axis, step))]
    all_to_all x3, blocking collectives: 74.7 us -> 66.1 us  [exchange(): lax.all_to_all(blocks, axis, split_axis=0, concat_axis=0, tiled=True, axi...]
  transfers between devices with their start and end apart: 2 -> 19, of which waited for: 2 -> 7; matrix products, arithmetic and copies ran while one was open for 6% -> 10% of each run, Pallas kernels for 0% -> 0%
where the time goes in v2:
time: 261 us; the launch traced here: 259 us
  blocking collectives  106 us (41%)
  starting transfers between devices  64.7 us (25%)
  waiting for transfers between devices  34.3 us (13%)
  Pallas kernels  20.3 us (8%)
  other arithmetic  19.7 us (8%)
  local copies, waits for them, and re-layouts  6.84 us (3%)
  matrix products  6.07 us (2%)
    all_to_all x3, blocking collectives, exchange(): lax.all_to_all(blocks, axis, split_axis=0, concat_axis=0, tiled=True, axi...  66.1 us
    ppermute x18, starting transfers between devices, shifted(): return lax.ppermute(array, 'seq', shift_pairs(sizes, axis, step))  61 us
    all_gather x1, blocking collectives, local(): lax.all_gather(weights, 'seq', axis=0, tiled=True, axis_index_groups=z_gr...  40.3 us
    all_to_all x1, waiting for transfers between devices, exchange(): lax.all_to_all(blocks, axis, split_axis=0, concat_axis=0, tiled=True, axi...  19.7 us
    ppermute x18, waiting for transfers between devices, shifted(): return lax.ppermute(array, 'seq', shift_pairs(sizes, axis, step))  14.6 us
    pallas_call x1, Pallas kernels, project_back(): pl.pallas_call(out_kernel, out_shape=jax.ShapeDtypeStruct((2, SIDE, 2, ro...  10.6 us
    pallas_call x1, Pallas kernels, project(): pl.pallas_call(project_kernel, out_shape=(jax.ShapeDtypeStruct((width, ro...  8.41 us
    dot_general x6, matrix products, batched(): jnp.einsum(spec, left, right, precision=EXACT, preferred_element_type=jnp...  5.73 us
  transfers between devices with their start and end apart: 19, of which 7 were waited for; matrix products, arithmetic and copies ran while one was open for 10% of the time, Pallas kernels for 0%

profile of v2, /device:TPU:1, one launch (start us, length us, event | category | flops | bytes accessed | tf_op | source)
XLA Modules:
  0.0 259.4 jit_solution(4999970590244663370)
XLA Ops:
  0.6 0.9 pad_maximum_fusion.2
  1.6 40.3 %all_gather.3 = bf16[256,1536]{1,0:T(8,128)(2,1)S(1)} all-gather(bf16[64,1536]{1,0:T(8,128)(2,1)S(1)} %pad_maximum_fusion.2), channel_id=1, replica_groups={{0,32,64,96},{8,40,72,104},{16,48,80,112},{24,56,88,120},{128,160,192,2..., dimensions={0}, use_global_device_ids=true | all-gather | bytes 983040 | tf_op jit(solution)/shard_map/all_gather | solution.py:349
  41.9 4.8 %collective-permute-start.10 = (bf16[128,1536]{1,0:T(8,128)(2,1)S(1)}, bf16[128,1536]{1,0:T(8,128)(2,1)S(1)}, u32[]{:S(2)}, u32[]{:S(2)}) collective-permute-start(bf16[128,1536]{1,0:T(8,128)(2,1)S(1)} %get-tuple-element.80), channel_id=1, source_target_pairs={{0,256},{128,384},{256,0},{384,128},{8,264},{136,392},{264,8},{392... | collective-permute-start | bytes 1179656 | tf_op jit(solution)/shard_map/ppermute | solution.py:42
  46.7 2.3 collective-permute-start.11
  49.0 4.7 %collective-permute-start.1 = (bf16[128,1536]{1,0:T(8,128)(2,1)S(1)}, bf16[128,1536]{1,0:T(8,128)(2,1)S(1)}, u32[]{:S(2)}, u32[]{:S(2)}) collective-permute-start(bf16[128,1536]{1,0:T(8,128)(2,1)S(1)} %get-tuple-element.81), channel_id=1, source_target_pairs={{0,16},{8,24},{16,0},{24,8},{32,48},{40,56},{48,32},{56,40},{64,80... | collective-permute-start | bytes 1179656 | tf_op jit(solution)/shard_map/ppermute | solution.py:42
  53.7 2.2 collective-permute-start.2
  55.9 4.2 %collective-permute-start.9 = (bf16[128,1536]{1,0:T(8,128)(2,1)S(1)}, bf16[128,1536]{1,0:T(8,128)(2,1)}, u32[]{:S(2)}, u32[]{:S(2)}) collective-permute-start(bf16[128,1536]{1,0:T(8,128)(2,1)S(1)} %get-tuple-element.80), channel_id=1, source_target_pairs={{0,384},{128,0},{256,128},{384,256},{8,392},{136,8},{264,136},{392... | collective-permute-start | bytes 1179656 | tf_op jit(solution)/shard_map/ppermute | solution.py:42
  60.3 4.3 %collective-permute-start = (bf16[128,1536]{1,0:T(8,128)(2,1)S(1)}, bf16[128,1536]{1,0:T(8,128)(2,1)S(1)}, u32[]{:S(2)}, u32[]{:S(2)}) collective-permute-start(bf16[128,1536]{1,0:T(8,128)(2,1)S(1)} %get-tuple-element.81), channel_id=1, source_target_pairs={{0,24},{8,0},{16,8},{24,16},{32,56},{40,32},{48,40},{56,48},{64,88... | collective-permute-start | bytes 1179656 | tf_op jit(solution)/shard_map/ppermute | solution.py:42
  64.7 2.5 collective-permute-start.13
  67.2 2.3 collective-permute-done.2
  69.6 4.3 %collective-permute-start.4 = (bf16[256,1536]{1,0:T(8,128)(2,1)S(1)}, bf16[256,1536]{1,0:T(8,128)(2,1)S(1)}, u32[]{:S(2)}, u32[]{:S(2)}) collective-permute-start(bf16[256,1536]{1,0:T(8,128)(2,1)S(1)} %constant_dynamic-update-slice_fusion.refs_1_), channel_id=1, source_target_pairs={{0,384},{128,0},{256,128},{384,256},{8,392},{136,8},{264,136},{392... | collective-permute-start | bytes 2359304 | tf_op jit(solution)/shard_map/ppermute | solution.py:42
  73.9 1.0 pad_maximum_fusion.1.refs_8_
  74.9 3.5 %collective-permute-start.14 = (bf16[256,1536]{1,0:T(8,128)(2,1)S(1)}, bf16[256,1536]{1,0:T(8,128)(2,1)S(1)}, u32[]{:S(2)}, u32[]{:S(2)}) collective-permute-start(bf16[256,1536]{1,0:T(8,128)(2,1)S(1)} %pad_maximum_fusion.1.refs_8_), channel_id=1, source_target_pairs={{0,8},{8,16},{16,24},{24,0},{32,40},{40,48},{48,56},{56,32},{64,72... | collective-permute-start | bytes 2359304 | tf_op jit(solution)/shard_map/ppermute | solution.py:42
  78.5 1.9 collective-permute-start.5
  81.8 0.9 fusion.5.turn
  82.7 4.1 %collective-permute-start.17 = (bf16[256,1536]{1,0:T(8,128)(2,1)S(1)}, bf16[256,1536]{1,0:T(8,128)(2,1)}, u32[]{:S(2)}, u32[]{:S(2)}) collective-permute-start(bf16[256,1536]{1,0:T(8,128)(2,1)S(1)} %constant_dynamic-update-slice_fusion.2.refs_9_), channel_id=1, source_target_pairs={{0,8},{8,16},{16,24},{24,0},{32,40},{40,48},{48,56},{56,32},{64,72... | collective-permute-start | bytes 2359304 | tf_op jit(solution)/shard_map/ppermute | solution.py:42
  86.9 1.9 collective-permute-start.8
  88.8 5.0 %collective-permute-start.12 = (bf16[256,1536]{1,0:T(8,128)(2,1)S(1)}, bf16[256,1536]{1,0:T(8,128)(2,1)}, u32[]{:S(2)}, u32[]{:S(2)}) collective-permute-start(bf16[256,1536]{1,0:T(8,128)(2,1)S(1)} %pad_maximum_fusion.1.refs_8_), channel_id=1, source_target_pairs={{0,24},{8,0},{16,8},{24,16},{32,56},{40,32},{48,40},{56,48},{64,88... | collective-permute-start | bytes 2359304 | tf_op jit(solution)/shard_map/ppermute | solution.py:42
  93.9 2.8 %collective-permute-start.3 = (bf16[256,1536]{1,0:T(8,128)(2,1)S(1)}, bf16[256,1536]{1,0:T(8,128)(2,1)}, u32[]{:S(2)}, u32[]{:S(2)}) collective-permute-start(bf16[256,1536]{1,0:T(8,128)(2,1)S(1)} %pad_maximum_fusion.refs_0_), channel_id=1, source_target_pairs={{0,384},{128,0},{256,128},{384,256},{8,392},{136,8},{264,136},{392... | collective-permute-start | bytes 2359304 | tf_op jit(solution)/shard_map/ppermute | solution.py:42
  96.8 0.9 collective-permute-done.5.refs_6_
  99.8 0.9 multiply_dynamic-update-slice_fusion.2
  100.7 2.8 %bitcast_dynamic-update-slice_fusion.1 = (f32[6,8,128,128]{3,2,1,0:T(8,128)}, f32[8,128,128]{2,1,0:T(8,128)}) fusion(f32[6,8,128,128]{3,2,1,0:T(8,128)} %multiply_dynamic-update-slice_fusion.2, pred[128,128]{1,0:T(8,128)(4,1)S(1)} %get-tuple-element.101, f32[128]{0:T(128)} %copy-done.15, f32[8,16]{1,0:T(8,128)S(1)} %get-tuple-element.88, ...), kind=kOutput, calls=%fused_computation.23 | convolution fusion | flops 25346048 | bytes 1067520 | tf_op jit(solution)/shard_map/cru,crt->cut/dot_general | solution.py:62
  103.5 2.1 copy.27
  105.6 5.2 %collective-permute-start.16 = (bf16[256,1536]{1,0:T(8,128)(2,1)}, bf16[256,1536]{1,0:T(8,128)(2,1)S(1)}, u32[]{:S(2)}, u32[]{:S(2)}) collective-permute-start(bf16[256,1536]{1,0:T(8,128)(2,1)} %copy-done.5), channel_id=1, source_target_pairs={{0,24},{8,0},{16,8},{24,16},{32,56},{40,32},{48,40},{56,48},{64,88... | collective-permute-start | bytes 2359304 | tf_op jit(solution)/shard_map/ppermute | solution.py:42
  111.6 1.9 bitcast_dynamic-update-slice_fusion
  113.5 1.0 multiply_dynamic-update-slice_fusion.1
  114.5 1.9 collective-permute-start.7
  116.4 3.4 %collective-permute-start.15 = (bf16[256,1536]{1,0:T(8,128)(2,1)}, bf16[256,1536]{1,0:T(8,128)(2,1)S(1)}, u32[]{:S(2)}, u32[]{:S(2)}) collective-permute-start(bf16[256,1536]{1,0:T(8,128)(2,1)} %copy-done.7), channel_id=1, source_target_pairs={{0,8},{8,16},{16,24},{24,0},{32,40},{40,48},{48,56},{56,32},{64,72... | collective-permute-start | bytes 2359304 | tf_op jit(solution)/shard_map/ppermute | solution.py:42
  119.8 1.9 collective-permute-start.6
  122.5 1.0 multiply_dynamic-update-slice_fusion
  123.5 2.8 %fusion = (bf16[6,8,128,128]{3,2,1,0:T(8,128)(2,1)S(1)}, bf16[6,8,128,128]{3,2,1,0:T(8,128)(2,1)S(1)}) fusion(f32[6,8,128,128]{3,2,1,0:T(8,128)} %multiply_dynamic-update-slice_fusion), kind=kLoop, calls=%fused_computation.2 | loop fusion | flops 3145728 | bytes 6291456 | tf_op jit(solution)/shard_map/convert_element_type | solution.py:95
  126.4 3.3 %collective-permute-done.7.refs_5_ = bf16[256,1536]{1,0:T(8,128)(2,1)S(1)} collective-permute-done((bf16[256,1536]{1,0:T(8,128)(2,1)}, bf16[256,1536]{1,0:T(8,128)(2,1)S(1)}, u32[]{:S(2)}, u32[]{:S(2)}) %collective-permute-start.7) | collective-permute-done | bytes 786464 | tf_op jit(solution)/shard_map/ppermute | solution.py:42
  129.7 3.1 %collective-permute-done.15.refs_12_ = bf16[256,1536]{1,0:T(8,128)(2,1)S(1)} collective-permute-done((bf16[256,1536]{1,0:T(8,128)(2,1)}, bf16[256,1536]{1,0:T(8,128)(2,1)S(1)}, u32[]{:S(2)}, u32[]{:S(2)}) %collective-permute-start.15) | collective-permute-done | bytes 786464 | tf_op jit(solution)/shard_map/ppermute | solution.py:42
  132.8 4.8 %collective-permute-done.6.refs_4_ = bf16[256,1536]{1,0:T(8,128)(2,1)S(1)} collective-permute-done((bf16[256,1536]{1,0:T(8,128)(2,1)}, bf16[256,1536]{1,0:T(8,128)(2,1)S(1)}, u32[]{:S(2)}, u32[]{:S(2)}) %collective-permute-start.6) | collective-permute-done | bytes 786464 | tf_op jit(solution)/shard_map/ppermute | solution.py:42
  137.6 0.9 copy-done.12
  138.5 8.4 %shard_map.102 = (f32[512,128]{1,0:T(8,128)}, f32[512,128]{1,0:T(8,128)}, bf16[2,512,128]{2,1,0:T(8,128)(2,1)}) custom-call(s32[1]{0:T(128)} %bitcast.place, bf16[128,4096]{1,0:T(8,128)(2,1)} %tokens.1, bf16[128,4096]{1,0:T(8,128)(2,1)} %cotangent.1, bf16[512,512]{1,0:T(8,128)(2,1)} %fusion.5.turn, bf16[256,1536]{1,0:T(8,128)(2,1)} %copy-done.1, ...), custom_call_target="tpu_custom_call" | custom-call | tf_op jit(solution)/shard_map/pallas_call | solution.py:242
  146.9 1.0 copy.28
  147.9 27.7 %all_to_all.20 = bf16[64,2,8,128]{3,2,1,0:T(8,128)(2,1)S(1)} all-to-all(bf16[64,2,8,128]{3,2,1,0:T(8,128)(2,1)S(1)} %copy.28), channel_id=1, replica_groups=mesh['seq'=64,'tp'=8] {'seq'}, dimensions={0} | all-to-all | bytes 524288 | tf_op jit(solution)/shard_map/all_to_all | solution.py:29
  175.7 1.2 shard_map.103
  177.1 23.8 %all_to_all.21 = bf16[64,2,8,128]{3,2,1,0:T(8,128)(2,1)S(1)} all-to-all(bf16[64,2,8,128]{3,2,1,0:T(8,128)(2,1)S(1)} %copy.30), channel_id=1, replica_groups=mesh['seq'=64,'tp'=8] {'seq'}, dimensions={0} | all-to-all | bytes 524288 | tf_op jit(solution)/shard_map/all_to_all | solution.py:29
  201.6 10.6 %shard_map.104 = bf16[2,4,2,128,512]{4,3,2,1,0:T(8,128)(2,1)} custom-call(s32[1]{0:T(128)} %bitcast.place, f32[512,128]{1,0:T(8,128)} %get-tuple-element.59.gates, f32[512,128]{1,0:T(8,128)} %get-tuple-element.60.back, bf16[2,512,128]{2,1,0:T(8,128)(2,1)} %copy_bitcast_fusion.filtered, bf16[256,1536]{1,0:T(8,128)(2,1)} %copy-done.1, ...), custom_call_target="tpu_custom_call" | custom-call | tf_op jit(solution)/shard_map/pallas_call | solution.py:294
  212.3 14.6 %all_to_all.22 = bf16[2,4,2,128,512]{4,3,2,1,0:T(8,128)(2,1)S(1)} all-to-all(bf16[2,4,2,128,512]{4,3,2,1,0:T(8,128)(2,1)} %shard_map.104), channel_id=1, replica_groups={{0,1},{2,3},{4,5},{6,7},{8,9},{10,11},{12,13},{14,15},{16,17},{18,19},{..., dimensions={0} | all-to-all | bytes 4194304 | tf_op jit(solution)/shard_map/all_to_all | solution.py:29
  227.4 1.3 fusion.4
  228.8 3.7 %all-to-all-start.3 = ((bf16[4,2,128,512]{3,2,1,0:T(8,128)(2,1)}), bf16[4,2,128,512]{3,2,1,0:T(8,128)(2,1)S(1)}, u32[]{:S(2)}, u32[]{:S(2)}) async-start(bf16[4,2,128,512]{3,2,1,0:T(8,128)(2,1)} %fusion.4), calls=%async_computation.3 | async-start | bytes 2097152 | tf_op jit(solution)/shard_map/all_to_all | solution.py:29
  233.6 1.5 multiply_reduce_fusion
  235.6 1.0 fusion.2
  236.6 1.0 fusion.3
  238.2 19.7 %all-to-all-done.3 = bf16[4,2,128,512]{3,2,1,0:T(8,128)(2,1)S(1)} async-done(((bf16[4,2,128,512]{3,2,1,0:T(8,128)(2,1)}), bf16[4,2,128,512]{3,2,1,0:T(8,128)(2,1)S(1)}, u32[]{:S(2)}, u32[]{:S(2)}) %all-to-all-start.3) | async-done | bytes 1048608 | tf_op jit(solution)/shard_map/all_to_all | solution.py:29
  (106 shorter events, 10.7 us)
Async XLA Ops:
  41.9 18.4 %collective-permute-start.10 = (bf16[128,1536]{1,0:T(8,128)(2,1)S(1)}, bf16[128,1536]{1,0:T(8,128)(2,1)S(1)}, u32[]{:S(2)}, u32[]{:S(2)}) collective-permute-start(bf16[128,1536]{1,0:T(8,128)(2,1)S(1)} %get-tuple-element.80), channel_id=1, source_target_pairs={{0,256},{128,384},{256,0},{384,128},{8,264},{136,392},{264,8},{392... | collective-permute-start | bytes 1179656 | tf_op jit(solution)/shard_map/ppermute | solution.py:42
  46.7 17.9 %collective-permute-start.11 = (bf16[128,1536]{1,0:T(8,128)(2,1)S(1)}, bf16[128,1536]{1,0:T(8,128)(2,1)S(1)}, u32[]{:S(2)}, u32[]{:S(2)}) collective-permute-start(bf16[128,1536]{1,0:T(8,128)(2,1)S(1)} %get-tuple-element.80), channel_id=1, source_target_pairs={{0,128},{128,256},{256,384},{384,0},{8,136},{136,264},{264,392},{3... | collective-permute-start | bytes 1179656 | tf_op jit(solution)/shard_map/ppermute | solution.py:42
  49.0 18.1 %collective-permute-start.1 = (bf16[128,1536]{1,0:T(8,128)(2,1)S(1)}, bf16[128,1536]{1,0:T(8,128)(2,1)S(1)}, u32[]{:S(2)}, u32[]{:S(2)}) collective-permute-start(bf16[128,1536]{1,0:T(8,128)(2,1)S(1)} %get-tuple-element.81), channel_id=1, source_target_pairs={{0,16},{8,24},{16,0},{24,8},{32,48},{40,56},{48,32},{56,40},{64,80... | collective-permute-start | bytes 1179656 | tf_op jit(solution)/shard_map/ppermute | solution.py:42
  53.7 15.8 %collective-permute-start.2 = (bf16[128,1536]{1,0:T(8,128)(2,1)S(1)}, bf16[128,1536]{1,0:T(8,128)(2,1)S(1)}, u32[]{:S(2)}, u32[]{:S(2)}) collective-permute-start(bf16[128,1536]{1,0:T(8,128)(2,1)S(1)} %get-tuple-element.81), channel_id=1, source_target_pairs={{0,8},{8,16},{16,24},{24,0},{32,40},{40,48},{48,56},{56,32},{64,72... | collective-permute-start | bytes 1179656 | tf_op jit(solution)/shard_map/ppermute | solution.py:42
  55.9 18.0 %collective-permute-start.9 = (bf16[128,1536]{1,0:T(8,128)(2,1)S(1)}, bf16[128,1536]{1,0:T(8,128)(2,1)}, u32[]{:S(2)}, u32[]{:S(2)}) collective-permute-start(bf16[128,1536]{1,0:T(8,128)(2,1)S(1)} %get-tuple-element.80), channel_id=1, source_target_pairs={{0,384},{128,0},{256,128},{384,256},{8,392},{136,8},{264,136},{392... | collective-permute-start | bytes 1179656 | tf_op jit(solution)/shard_map/ppermute | solution.py:42
  60.3 20.8 %copy-start.15 = (f32[128]{0:T(128)}, f32[128]{0:T(128)S(1)}, u32[]{:S(2)}) copy-start(f32[128]{0:T(128)S(1)} %iota_convert_fusion.1) | copy-start | bytes 1540
  60.3 18.2 %collective-permute-start = (bf16[128,1536]{1,0:T(8,128)(2,1)S(1)}, bf16[128,1536]{1,0:T(8,128)(2,1)S(1)}, u32[]{:S(2)}, u32[]{:S(2)}) collective-permute-start(bf16[128,1536]{1,0:T(8,128)(2,1)S(1)} %get-tuple-element.81), channel_id=1, source_target_pairs={{0,24},{8,0},{16,8},{24,16},{32,56},{40,32},{48,40},{56,48},{64,88... | collective-permute-start | bytes 1179656 | tf_op jit(solution)/shard_map/ppermute | solution.py:42
  64.7 18.1 %copy-start.2 = (bf16[256,1536]{1,0:T(8,128)(2,1)}, bf16[256,1536]{1,0:T(8,128)(2,1)S(1)}, u32[]{:S(2)}) copy-start(bf16[256,1536]{1,0:T(8,128)(2,1)S(1)} %constant_dynamic-update-slice_fusion.2.refs_9_) | copy-start | bytes 2359300
  64.7 22.2 %collective-permute-start.13 = (bf16[256,1536]{1,0:T(8,128)(2,1)S(1)}, bf16[256,1536]{1,0:T(8,128)(2,1)S(1)}, u32[]{:S(2)}, u32[]{:S(2)}) collective-permute-start(bf16[256,1536]{1,0:T(8,128)(2,1)S(1)} %constant_dynamic-update-slice_fusion.2.refs_9_), channel_id=1, source_target_pairs={{0,24},{8,0},{16,8},{24,16},{32,56},{40,32},{48,40},{56,48},{64,88... | collective-permute-start | bytes 2359304 | tf_op jit(solution)/shard_map/ppermute | solution.py:42
  67.2 30.5 %copy-start.14 = (f32[1,1,8,16]{3,2,1,0:T(8,128)S(1)}, f32[1,1,8,16]{3,2,1,0:T(8,128)}, u32[]{:S(2)}) copy-start(f32[1,1,8,16]{3,2,1,0:T(8,128)} %param.11) | copy-start | bytes 1540
  67.2 30.5 %copy-start.17 = (f32[1,1,8,16]{3,2,1,0:T(8,128)S(1)}, f32[1,1,8,16]{3,2,1,0:T(8,128)}, u32[]{:S(2)}) copy-start(f32[1,1,8,16]{3,2,1,0:T(8,128)} %param.12) | copy-start | bytes 1540
  69.6 30.2 %copy-start.3 = (bf16[256,1536]{1,0:T(8,128)(2,1)}, bf16[256,1536]{1,0:T(8,128)(2,1)S(1)}, u32[]{:S(2)}) copy-start(bf16[256,1536]{1,0:T(8,128)(2,1)S(1)} %constant_dynamic-update-slice_fusion.refs_1_) | copy-start | bytes 2359300
  69.6 19.2 %collective-permute-start.4 = (bf16[256,1536]{1,0:T(8,128)(2,1)S(1)}, bf16[256,1536]{1,0:T(8,128)(2,1)S(1)}, u32[]{:S(2)}, u32[]{:S(2)}) collective-permute-start(bf16[256,1536]{1,0:T(8,128)(2,1)S(1)} %constant_dynamic-update-slice_fusion.refs_1_), channel_id=1, source_target_pairs={{0,384},{128,0},{256,128},{384,256},{8,392},{136,8},{264,136},{392... | collective-permute-start | bytes 2359304 | tf_op jit(solution)/shard_map/ppermute | solution.py:42
  74.9 28.6 %copy-start = (bf16[256,1536]{1,0:T(8,128)(2,1)}, bf16[256,1536]{1,0:T(8,128)(2,1)S(1)}, u32[]{:S(2)}) copy-start(bf16[256,1536]{1,0:T(8,128)(2,1)S(1)} %pad_maximum_fusion.1.refs_8_) | copy-start | bytes 2359300
  74.9 19.0 %collective-permute-start.14 = (bf16[256,1536]{1,0:T(8,128)(2,1)S(1)}, bf16[256,1536]{1,0:T(8,128)(2,1)S(1)}, u32[]{:S(2)}, u32[]{:S(2)}) collective-permute-start(bf16[256,1536]{1,0:T(8,128)(2,1)S(1)} %pad_maximum_fusion.1.refs_8_), channel_id=1, source_target_pairs={{0,8},{8,16},{16,24},{24,0},{32,40},{40,48},{48,56},{56,32},{64,72... | collective-permute-start | bytes 2359304 | tf_op jit(solution)/shard_map/ppermute | solution.py:42
  78.5 27.0 %copy-start.1 = (bf16[256,1536]{1,0:T(8,128)(2,1)}, bf16[256,1536]{1,0:T(8,128)(2,1)S(1)}, u32[]{:S(2)}) copy-start(bf16[256,1536]{1,0:T(8,128)(2,1)S(1)} %pad_maximum_fusion.refs_0_) | copy-start | bytes 2359300
  78.5 19.2 %collective-permute-start.5 = (bf16[256,1536]{1,0:T(8,128)(2,1)S(1)}, bf16[256,1536]{1,0:T(8,128)(2,1)S(1)}, u32[]{:S(2)}, u32[]{:S(2)}) collective-permute-start(bf16[256,1536]{1,0:T(8,128)(2,1)S(1)} %pad_maximum_fusion.refs_0_), channel_id=1, source_target_pairs={{0,128},{128,256},{256,384},{384,0},{8,136},{136,264},{264,392},{3... | collective-permute-start | bytes 2359304 | tf_op jit(solution)/shard_map/ppermute | solution.py:42
  81.0 24.5 %copy-start.19 = (f32[128]{0:T(128)}, f32[128]{0:T(128)S(1)}, u32[]{:S(2)}) copy-start(f32[128]{0:T(128)S(1)} %get-tuple-element.105) | copy-start | bytes 1540
  81.0 24.5 %copy-start.21 = (f32[128]{0:T(128)}, f32[128]{0:T(128)S(1)}, u32[]{:S(2)}) copy-start(f32[128]{0:T(128)S(1)} %get-tuple-element.106) | copy-start | bytes 1540
  82.7 31.7 %collective-permute-start.17 = (bf16[256,1536]{1,0:T(8,128)(2,1)S(1)}, bf16[256,1536]{1,0:T(8,128)(2,1)}, u32[]{:S(2)}, u32[]{:S(2)}) collective-permute-start(bf16[256,1536]{1,0:T(8,128)(2,1)S(1)} %constant_dynamic-update-slice_fusion.2.refs_9_), channel_id=1, source_target_pairs={{0,8},{8,16},{16,24},{24,0},{32,40},{40,48},{48,56},{56,32},{64,72... | collective-permute-start | bytes 2359304 | tf_op jit(solution)/shard_map/ppermute | solution.py:42
  86.8 10.9 %copy-start.5 = (bf16[256,1536]{1,0:T(8,128)(2,1)}, bf16[256,1536]{1,0:T(8,128)(2,1)S(1)}, u32[]{:S(2)}) copy-start(bf16[256,1536]{1,0:T(8,128)(2,1)S(1)} %collective-permute-done.13.refs_11_) | copy-start | bytes 2359300
  86.9 29.5 %collective-permute-start.8 = (bf16[256,1536]{1,0:T(8,128)(2,1)S(1)}, bf16[256,1536]{1,0:T(8,128)(2,1)}, u32[]{:S(2)}, u32[]{:S(2)}) collective-permute-start(bf16[256,1536]{1,0:T(8,128)(2,1)S(1)} %constant_dynamic-update-slice_fusion.refs_1_), channel_id=1, source_target_pairs={{0,128},{128,256},{256,384},{384,0},{8,136},{136,264},{264,392},{3... | collective-permute-start | bytes 2359304 | tf_op jit(solution)/shard_map/ppermute | solution.py:42
  88.8 9.0 %copy-start.6 = (bf16[256,1536]{1,0:T(8,128)(2,1)}, bf16[256,1536]{1,0:T(8,128)(2,1)S(1)}, u32[]{:S(2)}) copy-start(bf16[256,1536]{1,0:T(8,128)(2,1)S(1)} %collective-permute-done.4.refs_3_) | copy-start | bytes 2359300
  88.8 31.0 %collective-permute-start.12 = (bf16[256,1536]{1,0:T(8,128)(2,1)S(1)}, bf16[256,1536]{1,0:T(8,128)(2,1)}, u32[]{:S(2)}, u32[]{:S(2)}) collective-permute-start(bf16[256,1536]{1,0:T(8,128)(2,1)S(1)} %pad_maximum_fusion.1.refs_8_), channel_id=1, source_target_pairs={{0,24},{8,0},{16,8},{24,16},{32,56},{40,32},{48,40},{56,48},{64,88... | collective-permute-start | bytes 2359304 | tf_op jit(solution)/shard_map/ppermute | solution.py:42
  93.9 4.5 %copy-start.7 = (bf16[256,1536]{1,0:T(8,128)(2,1)}, bf16[256,1536]{1,0:T(8,128)(2,1)S(1)}, u32[]{:S(2)}) copy-start(bf16[256,1536]{1,0:T(8,128)(2,1)S(1)} %collective-permute-done.14.refs_14_) | copy-start | bytes 2359300
  93.9 32.4 %collective-permute-start.3 = (bf16[256,1536]{1,0:T(8,128)(2,1)S(1)}, bf16[256,1536]{1,0:T(8,128)(2,1)}, u32[]{:S(2)}, u32[]{:S(2)}) collective-permute-start(bf16[256,1536]{1,0:T(8,128)(2,1)S(1)} %pad_maximum_fusion.refs_0_), channel_id=1, source_target_pairs={{0,384},{128,0},{256,128},{384,256},{8,392},{136,8},{264,136},{392... | collective-permute-start | bytes 2359304 | tf_op jit(solution)/shard_map/ppermute | solution.py:42
  97.7 1.0 copy-start.8
  98.7 6.8 %copy-start.23 = (f32[128]{0:T(128)}, f32[128]{0:T(128)S(1)}, u32[]{:S(2)}) copy-start(f32[128]{0:T(128)S(1)} %neg.35) | copy-start | bytes 1540
  105.6 20.8 %collective-permute-start.16 = (bf16[256,1536]{1,0:T(8,128)(2,1)}, bf16[256,1536]{1,0:T(8,128)(2,1)S(1)}, u32[]{:S(2)}, u32[]{:S(2)}) collective-permute-start(bf16[256,1536]{1,0:T(8,128)(2,1)} %copy-done.5), channel_id=1, source_target_pairs={{0,24},{8,0},{16,8},{24,16},{32,56},{40,32},{48,40},{56,48},{64,88... | collective-permute-start | bytes 2359304 | tf_op jit(solution)/shard_map/ppermute | solution.py:42
  114.5 15.2 %collective-permute-start.7 = (bf16[256,1536]{1,0:T(8,128)(2,1)}, bf16[256,1536]{1,0:T(8,128)(2,1)S(1)}, u32[]{:S(2)}, u32[]{:S(2)}) collective-permute-start(bf16[256,1536]{1,0:T(8,128)(2,1)} %copy-done.6), channel_id=1, source_target_pairs={{0,384},{128,0},{256,128},{384,256},{8,392},{136,8},{264,136},{392... | collective-permute-start | bytes 2359304 | tf_op jit(solution)/shard_map/ppermute | solution.py:42
  116.4 16.4 %collective-permute-start.15 = (bf16[256,1536]{1,0:T(8,128)(2,1)}, bf16[256,1536]{1,0:T(8,128)(2,1)S(1)}, u32[]{:S(2)}, u32[]{:S(2)}) collective-permute-start(bf16[256,1536]{1,0:T(8,128)(2,1)} %copy-done.7), channel_id=1, source_target_pairs={{0,8},{8,16},{16,24},{24,0},{32,40},{40,48},{48,56},{56,32},{64,72... | collective-permute-start | bytes 2359304 | tf_op jit(solution)/shard_map/ppermute | solution.py:42
  119.8 17.8 %collective-permute-start.6 = (bf16[256,1536]{1,0:T(8,128)(2,1)}, bf16[256,1536]{1,0:T(8,128)(2,1)S(1)}, u32[]{:S(2)}, u32[]{:S(2)}) collective-permute-start(bf16[256,1536]{1,0:T(8,128)(2,1)} %copy-done.8), channel_id=1, source_target_pairs={{0,128},{128,256},{256,384},{384,0},{8,136},{136,264},{264,392},{3... | collective-permute-start | bytes 2359304 | tf_op jit(solution)/shard_map/ppermute | solution.py:42
  126.3 11.3 %copy-start.9 = (bf16[256,1536]{1,0:T(8,128)(2,1)}, bf16[256,1536]{1,0:T(8,128)(2,1)S(1)}, u32[]{:S(2)}) copy-start(bf16[256,1536]{1,0:T(8,128)(2,1)S(1)} %collective-permute-done.16.refs_13_) | copy-start | bytes 2359300
  129.7 7.9 %copy-start.10 = (bf16[256,1536]{1,0:T(8,128)(2,1)}, bf16[256,1536]{1,0:T(8,128)(2,1)S(1)}, u32[]{:S(2)}) copy-start(bf16[256,1536]{1,0:T(8,128)(2,1)S(1)} %collective-permute-done.7.refs_5_) | copy-start | bytes 2359300
  132.8 4.8 %copy-start.11 = (bf16[256,1536]{1,0:T(8,128)(2,1)}, bf16[256,1536]{1,0:T(8,128)(2,1)S(1)}, u32[]{:S(2)}) copy-start(bf16[256,1536]{1,0:T(8,128)(2,1)S(1)} %collective-permute-done.15.refs_12_) | copy-start | bytes 2359300
  137.6 0.9 copy-start.12
  228.8 3.9 %copy-start.16 = (f32[128]{0:T(128)S(1)}, f32[128]{0:T(128)}, u32[]{:S(2)}) copy-start(f32[128]{0:T(128)} %copy-done.15) | copy-start | bytes 1540
  228.8 4.0 %copy-start.22 = (f32[128]{0:T(128)S(1)}, f32[128]{0:T(128)}, u32[]{:S(2)}) copy-start(f32[128]{0:T(128)} %copy-done.21) | copy-start | bytes 1540
  228.8 4.4 %copy-start.20 = (f32[128]{0:T(128)S(1)}, f32[128]{0:T(128)}, u32[]{:S(2)}) copy-start(f32[128]{0:T(128)} %copy-done.19) | copy-start | bytes 1540
  228.8 6.5 %copy-start.13 = (pred[128,128]{1,0:T(8,128)(4,1)S(1)}, pred[128,128]{1,0:T(8,128)(4,1)}, u32[]{:S(2)}) copy-start(pred[128,128]{1,0:T(8,128)(4,1)} %get-tuple-element.100) | copy-start | bytes 49156
  228.8 29.1 %all-to-all-start.3 = ((bf16[4,2,128,512]{3,2,1,0:T(8,128)(2,1)}), bf16[4,2,128,512]{3,2,1,0:T(8,128)(2,1)S(1)}, u32[]{:S(2)}, u32[]{:S(2)}) async-start(bf16[4,2,128,512]{3,2,1,0:T(8,128)(2,1)} %fusion.4), calls=%async_computation.3 | async-start | bytes 2097152 | tf_op jit(solution)/shard_map/all_to_all | solution.py:29
  232.6 5.0 %copy-start.18 = (f32[8,16]{1,0:T(8,128)S(1)}, f32[8,16]{1,0:T(8,128)}, u32[]{:S(2)}) copy-start(f32[8,16]{1,0:T(8,128)} %get-tuple-element.72) | copy-start | bytes 1540
  238.2 20.1 %copy-start.4 = (bf16[512,512]{1,0:T(8,128)(2,1)S(1)}, bf16[512,512]{1,0:T(8,128)(2,1)}, u32[]{:S(2)}) copy-start(bf16[512,512]{1,0:T(8,128)(2,1)} %fusion.5.turn) | copy-start | bytes 1572868

commit v3 on v2

--- a/solution.py
+++ b/solution.py
@@ -42,17 +42,20 @@
     return lax.ppermute(array, "seq", shift_pairs(sizes, axis, step))
 
 
-def gather_blocks(own, sizes, near_axis, far_axis):
-    up = shifted(own, sizes, near_axis, -1)
-    down = shifted(own, sizes, near_axis, 1)
-    across = shifted(own, sizes, near_axis, 2)
-    first, second = jnp.concatenate([own, up]), jnp.concatenate([across, down])
-    first_down = shifted(first, sizes, far_axis, 1)
-    second_up = shifted(second, sizes, far_axis, -1)
-    second_down = shifted(second, sizes, far_axis, 1)
-    first_up = shifted(first, sizes, far_axis, -1)
-    first_across = shifted(first_down, sizes, far_axis, 1)
-    second_across = shifted(second_up, sizes, far_axis, -1)
+def near_blocks(own, sizes, axis):
+    across = shifted(own, sizes, axis, 2)
+    up = shifted(own, sizes, axis, -1)
+    down = shifted(own, sizes, axis, 1)
+    return jnp.concatenate([own, up]), jnp.concatenate([across, down])
+
+
+def far_blocks(first, second, sizes, axis):
+    first_down = shifted(first, sizes, axis, 1)
+    second_up = shifted(second, sizes, axis, -1)
+    second_down = shifted(second, sizes, axis, 1)
+    first_up = shifted(first, sizes, axis, -1)
+    first_across = shifted(first_down, sizes, axis, 1)
+    second_across = shifted(second_up, sizes, axis, -1)
     return [
         first, second, first_up, second_up, first_across, second_across, first_down, second_down
     ]
@@ -62,50 +65,60 @@
     return jnp.einsum(spec, left, right, precision=EXACT, preferred_element_type=jnp.float32)
 
 
-def mode_tables(residue_rows, log_rows, chunks, width):
-    rates = jnp.exp(log_rows)
-    root = jnp.sqrt(2.0 * rates)
-    amplitude = residue_rows * root
-    channels, modes = rates.shape
-    steps = jnp.arange(width).astype(jnp.float32)
-    lag = steps[None, :] - steps[:, None]
-    to_end = width - 1.0 - steps
-    grow = jnp.exp(rates[:, :, None] * steps[None, None, :])
-    fade = jnp.exp(-rates[:, :, None] * steps[None, None, :])
-    near = batched("cru,crt->cut", amplitude[:, :, None] * grow, fade)
-    near = jnp.where((lag >= 0.0)[None], near, 0.0)
-    into = jnp.exp(-rates[:, :, None] * to_end[None, None, :])
-    out_of = jnp.exp(-rates[:, :, None] * (steps + 1.0)[None, None, :])
-
-    def wide(table):
-        own = jnp.eye(channels, dtype=jnp.float32)[:, :, None, None]
-        return (own * table[None]).reshape(channels, channels * modes, width)
-
-    filters = jnp.stack(
-        [
-            wide(into).swapaxes(1, 2),
-            wide(out_of).swapaxes(1, 2),
-            near,
-            near.swapaxes(1, 2),
-            wide(amplitude[:, :, None] * out_of),
-            wide(amplitude[:, :, None] * into),
-        ]
-    )
-    high = lax.reduce_precision(filters, 8, 7)
-    low = (filters - high).astype(jnp.bfloat16)
-    spans = width * 2.0 ** jnp.arange(8).astype(jnp.float32)
-    hops = jnp.exp(-rates.reshape(1, -1) * spans[:, None])
-    return {
-        "rates": rates,
-        "root": root,
-        "grow": grow,
-        "fade": fade,
-        "into": into,
-        "out_of": out_of,
-        "high": high.astype(jnp.bfloat16),
-        "low": low,
-        "hops": hops,
-    }
+def table_kernel(log_row, log_col, residue_row, residue_col, high, low, hops):
+    channels, width = high.shape[1:3]
+    modes = width // channels
+    rate_row, rate_col = jnp.exp(log_row[...]), jnp.exp(log_col[...])
+    amp_row = residue_row[...] * jnp.sqrt(2.0 * rate_row)
+    amp_col = residue_col[...] * jnp.sqrt(2.0 * rate_col)
+    row = lax.broadcasted_iota(jnp.int32, (width, width), 0)
+    col = lax.broadcasted_iota(jnp.int32, (width, width), 1)
+    row_step, col_step = row.astype(jnp.float32), col.astype(jnp.float32)
+    into = jnp.exp(-rate_row * (width - 1.0 - row_step))
+    out_of = jnp.exp(-rate_row * (row_step + 1.0))
+    into_amp = amp_col * jnp.exp(-rate_col * (width - 1.0 - col_step))
+    out_amp = amp_col * jnp.exp(-rate_col * (col_step + 1.0))
+    grow = amp_row * jnp.exp(rate_row * row_step)
+    fade = jnp.exp(-rate_col * col_step)
+
+    def put(table, c, value):
+        rough = value.astype(jnp.bfloat16)
+        high[table, c] = rough
+        low[table, c] = (value - rough.astype(jnp.float32)).astype(jnp.bfloat16)
+
+    for c in range(channels):
+        own_col = (col >= c * modes) & (col < (c + 1) * modes)
+        own_row = (row >= c * modes) & (row < (c + 1) * modes)
+        near = jnp.dot(
+            jnp.where(own_col, grow, 0.0), fade, precision=EXACT, preferred_element_type=jnp.float32
+        )
+        near = jnp.where(col >= row, near, 0.0)
+        put(0, c, jnp.where(own_col, into, 0.0))
+        put(1, c, jnp.where(own_col, out_of, 0.0))
+        put(2, c, near)
+        put(3, c, near.T)
+        put(4, c, jnp.where(own_row, out_amp, 0.0))
+        put(5, c, jnp.where(own_row, into_amp, 0.0))
+    for level in range(hops.shape[0]):
+        hops[level : level + 1, :] = jnp.exp(-rate_row * (width * 2.0**level))
+
+
+def mode_tables(residue_rows, log_rows, width):
+    channels, modes = log_rows.shape
+    here = pl.BlockSpec(memory_space=pltpu.VMEM)
+    tables = jax.ShapeDtypeStruct((6, channels, width, width), jnp.bfloat16)
+    return pl.pallas_call(
+        table_kernel,
+        out_shape=(tables, tables, jax.ShapeDtypeStruct((8, channels * modes), jnp.float32)),
+        in_specs=[here] * 4,
+        out_specs=(here,) * 3,
+        compiler_params=pltpu.CompilerParams(vmem_limit_bytes=24 * 2**20),
+    )(
+        log_rows.reshape(1, -1),
+        log_rows.reshape(-1, 1),
+        residue_rows.reshape(1, -1),
+        residue_rows.reshape(-1, 1),
+    )
 
 
 def filter_kernel(signal, high, low, hops, filtered, states):
@@ -148,8 +161,7 @@
 
 
 def filter_both(signal, tables):
-    channels, chunks = signal.shape[1:3]
-    modes = tables["hops"].shape[1]
+    chunks, modes = signal.shape[2], tables[2].shape[1]
     return pl.pallas_call(
         filter_kernel,
         out_shape=(
@@ -160,16 +172,18 @@
         out_specs=(pl.BlockSpec(memory_space=pltpu.VMEM),) * 2,
         compiler_params=pltpu.CompilerParams(vmem_limit_bytes=24 * 2**20),
         cost_estimate=pl.CostEstimate(flops=200_000_000, bytes_accessed=4_000_000, transcendentals=0),
-    )(signal, tables["high"], tables["low"], tables["hops"])
+    )(signal, *tables)
 
 
 SIDE = 4
 COUNT = 4 * SIDE
+FLIGHT = (3, 11, 6, 14, 2, 10, 7, 15, 4, 12, 5, 13, 0, 8, 1, 9)
 
 
 def fetch(blocks, held, arrived):
     copies = [
-        pltpu.make_async_copy(blocks[i], held.at[i], arrived.at[i]) for i in range(COUNT)
+        pltpu.make_async_copy(blocks[FLIGHT.index(i)], held.at[i], arrived.at[i])
+        for i in range(COUNT)
     ]
     for copy in copies:
         copy.start()
@@ -310,28 +324,32 @@
     return states.reshape(-1, states.shape[2]).T
 
 
-def parameter_grads(signal, grad, head, tail, ahead, residue_rows, tables):
+def parameter_grads(signal, grad, head, tail, ahead, residue_rows, log_rows):
     chunks, width = signal.shape[1:]
+    rates = jnp.exp(log_rows)
+    root = jnp.sqrt(2.0 * rates)
     steps = jnp.arange(width).astype(jnp.float32)
     lag = jnp.maximum(steps[None, :] - steps[:, None], -1.0)[None]
     overlap = jnp.where(lag >= 0.0, batched("cku,ckt->cut", signal, grad), 0.0)
-    grow, fade = tables["grow"], tables["fade"]
+    grow = jnp.exp(rates[:, :, None] * steps[None, None, :])
+    fade = jnp.exp(-rates[:, :, None] * steps[None, None, :])
     shape = residue_rows.shape
     plain = jnp.sum(batched("cut,crt->cru", overlap, fade) * grow, axis=2)
     plain = plain + jnp.sum(ahead * tail, axis=0).reshape(shape)
-    into_moment = tables["into"] * (width - 1.0 - steps)[None, None, :]
-    out_moment = tables["out_of"] * (steps + 1.0)[None, None, :]
+    to_end = (width - 1.0 - steps)[None, None, :]
+    from_start = (steps + 1.0)[None, None, :]
+    into_moment = jnp.exp(-rates[:, :, None] * to_end) * to_end
+    out_moment = jnp.exp(-rates[:, :, None] * from_start) * from_start
     head_moment = by_chunk(batched("cku,cru->crk", signal, into_moment))
     tail_moment = by_chunk(batched("ckt,crt->crk", grad, out_moment))
     blocks = jnp.arange(chunks).astype(jnp.float32)
     gap = (blocks[:, None] - blocks[None, :] - 1.0)[:, :, None]
     hop = width * jnp.maximum(gap, 0.0)
-    carry = jnp.where(gap >= 0.0, jnp.exp(-tables["rates"].reshape(1, 1, -1) * hop), 0.0)
+    carry = jnp.where(gap >= 0.0, jnp.exp(-rates.reshape(1, 1, -1) * hop), 0.0)
     ahead_moment = jnp.sum(carry * (head_moment[None] + hop * head[None]), axis=1)
     far = jnp.sum(ahead * tail_moment + ahead_moment * tail, axis=0).reshape(shape)
     moment = jnp.sum(batched("cut,crt->cru", overlap * lag, fade) * grow, axis=2) + far
-    root = tables["root"]
-    return plain * root, residue_rows * root * (0.5 * plain - tables["rates"] * moment)
+    return plain * root, residue_rows * root * (0.5 * plain - rates * moment)
 
 
 def local(tokens, w_value, w_gate, w_output, residues, log_rates, cotangent):
@@ -348,7 +366,9 @@
     weights = jnp.concatenate([w_value, w_gate, w_output.T], axis=1)
     along_z = lax.all_gather(weights, "seq", axis=0, tiled=True, axis_index_groups=z_groups)
     along_z = along_z.reshape(2, 2 * block, 3 * width)
-    blocks = gather_blocks(along_z[0], sizes, 2, 0) + gather_blocks(along_z[1], sizes, 0, 2)
+    near = near_blocks(along_z[0], sizes, 2), near_blocks(along_z[1], sizes, 0)
+    near = lax.optimization_barrier(near)
+    blocks = far_blocks(*near[0], sizes, 0) + far_blocks(*near[1], sizes, 2)
 
     place = (me // SIDE**2).reshape(1)
     deep = 2 * SIDE * block
@@ -356,11 +376,12 @@
     x_wanted = (me + target // (2 * block)) % SIDE
     wanted = target // block % 2 * (SIDE * block) + x_wanted * block + target % block
     turn = (source == wanted).astype(half)
-    passed_on = [blocks[i] for i in (3, 6, 11, 14)]
+    passed_on = [blocks[i] for i in FLIGHT[:4]]
     passed_on, residues, log_rates = lax.optimization_barrier((passed_on, residues, log_rates))
     residue_rows = residues.reshape(channels, residues.shape[3])
     log_rows = log_rates.reshape(channels, log_rates.shape[3])
-    tables = mode_tables(residue_rows, log_rows, seq_devices, rows)
+    tables = mode_tables(residue_rows, log_rows, rows)
+    blocks = [blocks[i] for i in FLIGHT]
     blocks, tables, turn = lax.optimization_barrier((blocks, tables, turn))
 
     gates, back, sent = project(place, tokens, cotangent, turn, blocks)
@@ -373,7 +394,7 @@
 
     pair = exchange(parts, "tp", core_groups).astype(jnp.float32)
     pair = (pair[0] + pair[1]).astype(half)
-    pair, got, states = lax.optimization_barrier((pair, got, states))
+    pair, got, states, log_rows = lax.optimization_barrier((pair, got, states, log_rows))
     line = exchange(pair, "tp", line_groups).astype(jnp.float32)
     summed = ((line[0] + line[1]) + (line[2] + line[3])).astype(half)
     result = lax.dot_general(
@@ -383,7 +404,7 @@
 
     signal, grad = got[0].astype(jnp.float32), got[1].astype(jnp.float32)
     residue_grad, rate_grad = parameter_grads(
-        signal, grad, states[0], states[1], states[2], residue_rows, tables
+        signal, grad, states[0], states[1], states[2], residue_rows, log_rows
     )
     scale = (rows * seq_devices) ** (-0.5)
     return (

time: 261 us -> 258 us (0.989)
  waiting for transfers between devices: 34.3 us -> 66.6 us
  blocking collectives: 106 us -> 86.8 us
  other arithmetic: 19.7 us -> 6.92 us
    all_to_all x3 -> x2, blocking collectives: 66.1 us -> 46.5 us  [exchange(): lax.all_to_all(blocks, axis, split_axis=0, concat_axis=0, tiled=True, axi...]
    all_to_all x1 -> x2, waiting for transfers between devices: 19.7 us -> 37.9 us  [exchange(): lax.all_to_all(blocks, axis, split_axis=0, concat_axis=0, tiled=True, axi...]
    ppermute x18, waiting for transfers between devices: 14.6 us -> 28.7 us  [shifted(): return lax.ppermute(array, 'seq', shift_pairs(sizes, axis, step))]
    all_to_all x1 -> x2, starting transfers between devices: 3.66 us -> 9.46 us  [exchange(): lax.all_to_all(blocks, axis, split_axis=0, concat_axis=0, tiled=True, axi...]
    ppermute x18, starting transfers between devices: 61 us -> 56.3 us  [shifted(): return lax.ppermute(array, 'seq', shift_pairs(sizes, axis, step))]
    unnamed x4 -> x0, other arithmetic: 4.56 us -> none
    convert_element_type x3 -> x1, other arithmetic: 2.78 us -> 0.01 us  [parameter_grads(): steps = jnp.arange(width).astype(jnp.float32)]
    dot_general x6 -> x5, matrix products: 5.73 us -> 3.17 us  [batched(): jnp.einsum(spec, left, right, precision=EXACT, preferred_element_type=jnp...]
  transfers between devices with their start and end apart: 19 -> 20, of which waited for: 7 -> 10; matrix products, arithmetic and copies ran while one was open for 10% -> 3% of each run, Pallas kernels for 0% -> 0%
where the time goes in v3:
time: 258 us; the launch traced here: 257 us
  blocking collectives  86.8 us (34%)
  waiting for transfers between devices  66.6 us (26%)
  starting transfers between devices  65.8 us (26%)
  Pallas kernels  21.3 us (8%)
  other arithmetic  6.92 us (3%)
  local copies, waits for them, and re-layouts  5.08 us (2%)
  matrix products  3.51 us (1%)
    ppermute x18, starting transfers between devices, shifted(): return lax.ppermute(array, 'seq', shift_pairs(sizes, axis, step))  56.3 us
    all_to_all x2, blocking collectives, exchange(): lax.all_to_all(blocks, axis, split_axis=0, concat_axis=0, tiled=True, axi...  46.5 us
    all_gather x1, blocking collectives, local(): lax.all_gather(weights, 'seq', axis=0, tiled=True, axis_index_groups=z_gr...  40.3 us
    all_to_all x2, waiting for transfers between devices, exchange(): lax.all_to_all(blocks, axis, split_axis=0, concat_axis=0, tiled=True, axi...  37.9 us
    ppermute x18, waiting for transfers between devices, shifted(): return lax.ppermute(array, 'seq', shift_pairs(sizes, axis, step))  28.7 us
    pallas_call x1, Pallas kernels, project_back(): pl.pallas_call(out_kernel, out_shape=jax.ShapeDtypeStruct((2, SIDE, 2, ro...  10.6 us
    all_to_all x2, starting transfers between devices, exchange(): lax.all_to_all(blocks, axis, split_axis=0, concat_axis=0, tiled=True, axi...  9.46 us
    pallas_call x1, Pallas kernels, project(): pl.pallas_call(project_kernel, out_shape=(jax.ShapeDtypeStruct((width, ro...  8.45 us
  transfers between devices with their start and end apart: 20, of which 10 were waited for; matrix products, arithmetic and copies ran while one was open for 3% of the time, Pallas kernels for 0%

profile of v3, /device:TPU:1, one launch (start us, length us, event | category | flops | bytes accessed | tf_op | source)
XLA Modules:
  0.0 257.1 jit_solution(8792975907738901241)
XLA Ops:
  0.6 0.9 pad_maximum_fusion.4
  1.6 40.3 %all_gather.3 = bf16[256,1536]{1,0:T(8,128)(2,1)S(1)} all-gather(bf16[64,1536]{1,0:T(8,128)(2,1)S(1)} %pad_maximum_fusion.4), channel_id=1, replica_groups={{0,32,64,96},{8,40,72,104},{16,48,80,112},{24,56,88,120},{128,160,192,2..., dimensions={0}, use_global_device_ids=true | all-gather | bytes 983040 | tf_op jit(solution)/shard_map/all_gather | solution.py:367
  41.9 4.4 %collective-permute-start = (bf16[128,1536]{1,0:T(8,128)(2,1)S(1)}, bf16[128,1536]{1,0:T(8,128)(2,1)S(1)}, u32[]{:S(2)}, u32[]{:S(2)}) collective-permute-start(bf16[128,1536]{1,0:T(8,128)(2,1)S(1)} %get-tuple-element.83), channel_id=1, source_target_pairs={{0,24},{8,0},{16,8},{24,16},{32,56},{40,32},{48,40},{56,48},{64,88... | collective-permute-start | bytes 1179656 | tf_op jit(solution)/shard_map/ppermute | solution.py:42
  46.3 4.6 %collective-permute-start.3 = (bf16[128,1536]{1,0:T(8,128)(2,1)S(1)}, bf16[128,1536]{1,0:T(8,128)(2,1)S(1)}, u32[]{:S(2)}, u32[]{:S(2)}) collective-permute-start(bf16[128,1536]{1,0:T(8,128)(2,1)S(1)} %get-tuple-element.82), channel_id=1, source_target_pairs={{0,384},{128,0},{256,128},{384,256},{8,392},{136,8},{264,136},{392... | collective-permute-start | bytes 1179656 | tf_op jit(solution)/shard_map/ppermute | solution.py:42
  50.9 1.9 collective-permute-start.2
  52.8 3.6 %collective-permute-start.1 = (bf16[128,1536]{1,0:T(8,128)(2,1)S(1)}, bf16[128,1536]{1,0:T(8,128)(2,1)S(1)}, u32[]{:S(2)}, u32[]{:S(2)}) collective-permute-start(bf16[128,1536]{1,0:T(8,128)(2,1)S(1)} %get-tuple-element.83), channel_id=1, source_target_pairs={{0,16},{8,24},{16,0},{24,8},{32,48},{40,56},{48,32},{56,40},{64,80... | collective-permute-start | bytes 1179656 | tf_op jit(solution)/shard_map/ppermute | solution.py:42
  56.5 1.9 collective-permute-start.5
  58.4 3.5 %collective-permute-start.4 = (bf16[128,1536]{1,0:T(8,128)(2,1)S(1)}, bf16[128,1536]{1,0:T(8,128)(2,1)S(1)}, u32[]{:S(2)}, u32[]{:S(2)}) collective-permute-start(bf16[128,1536]{1,0:T(8,128)(2,1)S(1)} %get-tuple-element.82), channel_id=1, source_target_pairs={{0,256},{128,384},{256,0},{384,128},{8,264},{136,392},{264,8},{392... | collective-permute-start | bytes 1179656 | tf_op jit(solution)/shard_map/ppermute | solution.py:42
  62.1 1.0 collective-permute-done.2
  63.2 4.6 %collective-permute-done.1 = bf16[128,1536]{1,0:T(8,128)(2,1)S(1)} collective-permute-done((bf16[128,1536]{1,0:T(8,128)(2,1)S(1)}, bf16[128,1536]{1,0:T(8,128)(2,1)S(1)}, u32[]{:S(2)}, u32[]{:S(2)}) %collective-permute-start.1) | collective-permute-done | bytes 393248 | tf_op jit(solution)/shard_map/ppermute | solution.py:42
  67.8 1.6 collective-permute-done.5
  69.4 3.3 %collective-permute-done.4 = bf16[128,1536]{1,0:T(8,128)(2,1)S(1)} collective-permute-done((bf16[128,1536]{1,0:T(8,128)(2,1)S(1)}, bf16[128,1536]{1,0:T(8,128)(2,1)S(1)}, u32[]{:S(2)}, u32[]{:S(2)}) %collective-permute-start.4) | collective-permute-done | bytes 393248 | tf_op jit(solution)/shard_map/ppermute | solution.py:42
  72.8 1.9 collective-permute-start.6
  74.7 2.9 %collective-permute-start.7 = (bf16[256,1536]{1,0:T(8,128)(2,1)S(1)}, bf16[256,1536]{1,0:T(8,128)(2,1)}, u32[]{:S(2)}, u32[]{:S(2)}) collective-permute-start(bf16[256,1536]{1,0:T(8,128)(2,1)S(1)} %pad_maximum_fusion.3.refs_15_), channel_id=1, source_target_pairs={{0,24},{8,0},{16,8},{24,16},{32,56},{40,32},{48,40},{56,48},{64,88... | collective-permute-start | bytes 2359304 | tf_op jit(solution)/shard_map/ppermute | solution.py:42
  77.6 3.4 %collective-permute-start.8 = (bf16[256,1536]{1,0:T(8,128)(2,1)S(1)}, bf16[256,1536]{1,0:T(8,128)(2,1)}, u32[]{:S(2)}, u32[]{:S(2)}) collective-permute-start(bf16[256,1536]{1,0:T(8,128)(2,1)S(1)} %pad_maximum_fusion.refs_12_), channel_id=1, source_target_pairs={{0,128},{128,256},{256,384},{384,0},{8,136},{136,264},{264,392},{3... | collective-permute-start | bytes 2359304 | tf_op jit(solution)/shard_map/ppermute | solution.py:42
  81.0 2.4 collective-permute-start.9
  83.4 3.1 %collective-permute-start.10 = (bf16[256,1536]{1,0:T(8,128)(2,1)S(1)}, bf16[256,1536]{1,0:T(8,128)(2,1)S(1)}, u32[]{:S(2)}, u32[]{:S(2)}) collective-permute-start(bf16[256,1536]{1,0:T(8,128)(2,1)S(1)} %pad_maximum_fusion.refs_12_), channel_id=1, source_target_pairs={{0,384},{128,0},{256,128},{384,256},{8,392},{136,8},{264,136},{392... | collective-permute-start | bytes 2359304 | tf_op jit(solution)/shard_map/ppermute | solution.py:42
  86.9 3.7 %collective-permute-start.11 = (bf16[256,1536]{1,0:T(8,128)(2,1)S(1)}, bf16[256,1536]{1,0:T(8,128)(2,1)S(1)}, u32[]{:S(2)}, u32[]{:S(2)}) collective-permute-start(bf16[256,1536]{1,0:T(8,128)(2,1)S(1)} %pad_maximum_fusion.2.refs_13_), channel_id=1, source_target_pairs={{0,24},{8,0},{16,8},{24,16},{32,56},{40,32},{48,40},{56,48},{64,88... | collective-permute-start | bytes 2359304 | tf_op jit(solution)/shard_map/ppermute | solution.py:42
  90.7 2.6 %collective-permute-start.12 = (bf16[256,1536]{1,0:T(8,128)(2,1)S(1)}, bf16[256,1536]{1,0:T(8,128)(2,1)S(1)}, u32[]{:S(2)}, u32[]{:S(2)}) collective-permute-start(bf16[256,1536]{1,0:T(8,128)(2,1)S(1)} %pad_maximum_fusion.1.refs_14_), channel_id=1, source_target_pairs={{0,128},{128,256},{256,384},{384,0},{8,136},{136,264},{264,392},{3... | collective-permute-start | bytes 2359304 | tf_op jit(solution)/shard_map/ppermute | solution.py:42
  93.3 2.3 collective-permute-start.13
  95.6 3.1 %collective-permute-start.14 = (bf16[256,1536]{1,0:T(8,128)(2,1)}, bf16[256,1536]{1,0:T(8,128)(2,1)}, u32[]{:S(2)}, u32[]{:S(2)}) collective-permute-start(bf16[256,1536]{1,0:T(8,128)(2,1)} %collective-permute-done.8.refs_2_), channel_id=1, source_target_pairs={{0,128},{128,256},{256,384},{384,0},{8,136},{136,264},{264,392},{3... | collective-permute-start | bytes 2359304 | tf_op jit(solution)/shard_map/ppermute | solution.py:42
  98.7 6.4 %collective-permute-done.10.refs_4_ = bf16[256,1536]{1,0:T(8,128)(2,1)S(1)} collective-permute-done((bf16[256,1536]{1,0:T(8,128)(2,1)S(1)}, bf16[256,1536]{1,0:T(8,128)(2,1)S(1)}, u32[]{:S(2)}, u32[]{:S(2)}) %collective-permute-start.10) | collective-permute-done | bytes 786464 | tf_op jit(solution)/shard_map/ppermute | solution.py:42
  105.1 3.4 %collective-permute-start.15 = (bf16[256,1536]{1,0:T(8,128)(2,1)}, bf16[256,1536]{1,0:T(8,128)(2,1)S(1)}, u32[]{:S(2)}, u32[]{:S(2)}) collective-permute-start(bf16[256,1536]{1,0:T(8,128)(2,1)} %collective-permute-done.9.refs_3_), channel_id=1, source_target_pairs={{0,8},{8,16},{16,24},{24,0},{32,40},{40,48},{48,56},{56,32},{64,72... | collective-permute-start | bytes 2359304 | tf_op jit(solution)/shard_map/ppermute | solution.py:42
  108.4 4.2 %collective-permute-start.16 = (bf16[256,1536]{1,0:T(8,128)(2,1)}, bf16[256,1536]{1,0:T(8,128)(2,1)}, u32[]{:S(2)}, u32[]{:S(2)}) collective-permute-start(bf16[256,1536]{1,0:T(8,128)(2,1)} %collective-permute-done.6.refs_0_), channel_id=1, source_target_pairs={{0,384},{128,0},{256,128},{384,256},{8,392},{136,8},{264,136},{392... | collective-permute-start | bytes 2359304 | tf_op jit(solution)/shard_map/ppermute | solution.py:42
  112.7 3.2 %collective-permute-start.17 = (bf16[256,1536]{1,0:T(8,128)(2,1)}, bf16[256,1536]{1,0:T(8,128)(2,1)}, u32[]{:S(2)}, u32[]{:S(2)}) collective-permute-start(bf16[256,1536]{1,0:T(8,128)(2,1)} %collective-permute-done.7.refs_1_), channel_id=1, source_target_pairs={{0,24},{8,0},{16,8},{24,16},{32,56},{40,32},{48,40},{56,48},{64,88... | collective-permute-start | bytes 2359304 | tf_op jit(solution)/shard_map/ppermute | solution.py:42
  116.0 0.9 fusion.4.turn
  117.3 1.0 shard_map.102
  118.3 6.8 %collective-permute-done.14.refs_8_ = bf16[256,1536]{1,0:T(8,128)(2,1)} collective-permute-done((bf16[256,1536]{1,0:T(8,128)(2,1)}, bf16[256,1536]{1,0:T(8,128)(2,1)}, u32[]{:S(2)}, u32[]{:S(2)}) %collective-permute-start.14) | collective-permute-done | bytes 786464 | tf_op jit(solution)/shard_map/ppermute | solution.py:42
  125.1 4.6 %collective-permute-done.15.refs_9_ = bf16[256,1536]{1,0:T(8,128)(2,1)S(1)} collective-permute-done((bf16[256,1536]{1,0:T(8,128)(2,1)}, bf16[256,1536]{1,0:T(8,128)(2,1)S(1)}, u32[]{:S(2)}, u32[]{:S(2)}) %collective-permute-start.15) | collective-permute-done | bytes 786464 | tf_op jit(solution)/shard_map/ppermute | solution.py:42
  129.8 0.9 copy-done.8
  130.7 8.4 %shard_map.103 = (f32[512,128]{1,0:T(8,128)}, f32[512,128]{1,0:T(8,128)}, bf16[2,512,128]{2,1,0:T(8,128)(2,1)}) custom-call(s32[1]{0:T(128)} %bitcast.place, bf16[128,4096]{1,0:T(8,128)(2,1)} %tokens.1, bf16[128,4096]{1,0:T(8,128)(2,1)} %cotangent.1, bf16[512,512]{1,0:T(8,128)(2,1)} %fusion.4.turn, bf16[256,1536]{1,0:T(8,128)(2,1)} %collective-permute-done.6.refs_0_, ...), custom_call_target="tpu_custom_call" | custom-call | tf_op jit(solution)/shard_map/pallas_call | solution.py:256
  139.1 1.0 copy.32
  140.1 27.1 %all_to_all.20 = bf16[64,2,8,128]{3,2,1,0:T(8,128)(2,1)S(1)} all-to-all(bf16[64,2,8,128]{3,2,1,0:T(8,128)(2,1)S(1)} %copy.32), channel_id=1, replica_groups=mesh['seq'=64,'tp'=8] {'seq'}, dimensions={0} | all-to-all | bytes 524288 | tf_op jit(solution)/shard_map/all_to_all | solution.py:29
  167.3 1.2 shard_map.104
  168.5 0.9 copy.34
  169.4 5.5 %all-to-all-start.1 = ((bf16[64,2,8,128]{3,2,1,0:T(8,128)(2,1)}), bf16[64,2,8,128]{3,2,1,0:T(8,128)(2,1)S(1)}, u32[]{:S(2)}, u32[]{:S(2)}) async-start(bf16[64,2,8,128]{3,2,1,0:T(8,128)(2,1)} %copy.34), calls=%async_computation.1 | async-start | bytes 524288 | tf_op jit(solution)/shard_map/all_to_all | solution.py:29
  174.9 18.7 %all-to-all-done.1 = bf16[64,2,8,128]{3,2,1,0:T(8,128)(2,1)S(1)} async-done(((bf16[64,2,8,128]{3,2,1,0:T(8,128)(2,1)}), bf16[64,2,8,128]{3,2,1,0:T(8,128)(2,1)S(1)}, u32[]{:S(2)}, u32[]{:S(2)}) %all-to-all-start.1) | async-done | bytes 262176 | tf_op jit(solution)/shard_map/all_to_all | solution.py:29
  193.6 0.7 copy_bitcast_fusion.filtered
  194.3 10.6 %shard_map.105 = bf16[2,4,2,128,512]{4,3,2,1,0:T(8,128)(2,1)} custom-call(s32[1]{0:T(128)} %bitcast.place, f32[512,128]{1,0:T(8,128)} %get-tuple-element.68.gates, f32[512,128]{1,0:T(8,128)} %get-tuple-element.69.back, bf16[2,512,128]{2,1,0:T(8,128)(2,1)} %copy_bitcast_fusion.filtered, bf16[256,1536]{1,0:T(8,128)(2,1)} %collective-permute-done.6.refs_0_, ...), custom_call_target="tpu_custom_call" | custom-call | tf_op jit(solution)/shard_map/pallas_call | solution.py:308
  204.9 19.4 %all_to_all.21 = bf16[2,4,2,128,512]{4,3,2,1,0:T(8,128)(2,1)S(1)} all-to-all(bf16[2,4,2,128,512]{4,3,2,1,0:T(8,128)(2,1)} %shard_map.105), channel_id=1, replica_groups={{0,1},{2,3},{4,5},{6,7},{8,9},{10,11},{12,13},{14,15},{16,17},{18,19},{..., dimensions={0} | all-to-all | bytes 4194304 | tf_op jit(solution)/shard_map/all_to_all | solution.py:29
  224.9 1.4 fusion.3
  226.3 4.0 %all-to-all-start.3 = ((bf16[4,2,128,512]{3,2,1,0:T(8,128)(2,1)}), bf16[4,2,128,512]{3,2,1,0:T(8,128)(2,1)S(1)}, u32[]{:S(2)}, u32[]{:S(2)}) async-start(bf16[4,2,128,512]{3,2,1,0:T(8,128)(2,1)} %fusion.3), calls=%async_computation.3 | async-start | bytes 2097152 | tf_op jit(solution)/shard_map/all_to_all | solution.py:29
  231.7 1.5 multiply_reduce_fusion
  233.7 1.0 fusion.1
  234.7 1.1 fusion.2
  235.8 0.6 fusion.39
  236.4 19.2 %all-to-all-done.3 = bf16[4,2,128,512]{3,2,1,0:T(8,128)(2,1)S(1)} async-done(((bf16[4,2,128,512]{3,2,1,0:T(8,128)(2,1)}), bf16[4,2,128,512]{3,2,1,0:T(8,128)(2,1)S(1)}, u32[]{:S(2)}, u32[]{:S(2)}) %all-to-all-start.3) | async-done | bytes 1048608 | tf_op jit(solution)/shard_map/all_to_all | solution.py:29
  256.4 0.7 fusion.56
  (66 shorter events, 4.3 us)
Async XLA Ops:
  41.9 16.5 %collective-permute-start = (bf16[128,1536]{1,0:T(8,128)(2,1)S(1)}, bf16[128,1536]{1,0:T(8,128)(2,1)S(1)}, u32[]{:S(2)}, u32[]{:S(2)}) collective-permute-start(bf16[128,1536]{1,0:T(8,128)(2,1)S(1)} %get-tuple-element.83), channel_id=1, source_target_pairs={{0,24},{8,0},{16,8},{24,16},{32,56},{40,32},{48,40},{56,48},{64,88... | collective-permute-start | bytes 1179656 | tf_op jit(solution)/shard_map/ppermute | solution.py:42
  46.3 15.8 %collective-permute-start.3 = (bf16[128,1536]{1,0:T(8,128)(2,1)S(1)}, bf16[128,1536]{1,0:T(8,128)(2,1)S(1)}, u32[]{:S(2)}, u32[]{:S(2)}) collective-permute-start(bf16[128,1536]{1,0:T(8,128)(2,1)S(1)} %get-tuple-element.82), channel_id=1, source_target_pairs={{0,384},{128,0},{256,128},{384,256},{8,392},{136,8},{264,136},{392... | collective-permute-start | bytes 1179656 | tf_op jit(solution)/shard_map/ppermute | solution.py:42
  50.9 12.2 %collective-permute-start.2 = (bf16[128,1536]{1,0:T(8,128)(2,1)S(1)}, bf16[128,1536]{1,0:T(8,128)(2,1)S(1)}, u32[]{:S(2)}, u32[]{:S(2)}) collective-permute-start(bf16[128,1536]{1,0:T(8,128)(2,1)S(1)} %get-tuple-element.83), channel_id=1, source_target_pairs={{0,8},{8,16},{16,24},{24,0},{32,40},{40,48},{48,56},{56,32},{64,72... | collective-permute-start | bytes 1179656 | tf_op jit(solution)/shard_map/ppermute | solution.py:42
  52.8 14.9 %collective-permute-start.1 = (bf16[128,1536]{1,0:T(8,128)(2,1)S(1)}, bf16[128,1536]{1,0:T(8,128)(2,1)S(1)}, u32[]{:S(2)}, u32[]{:S(2)}) collective-permute-start(bf16[128,1536]{1,0:T(8,128)(2,1)S(1)} %get-tuple-element.83), channel_id=1, source_target_pairs={{0,16},{8,24},{16,0},{24,8},{32,48},{40,56},{48,32},{56,40},{64,80... | collective-permute-start | bytes 1179656 | tf_op jit(solution)/shard_map/ppermute | solution.py:42
  56.5 12.9 %collective-permute-start.5 = (bf16[128,1536]{1,0:T(8,128)(2,1)S(1)}, bf16[128,1536]{1,0:T(8,128)(2,1)S(1)}, u32[]{:S(2)}, u32[]{:S(2)}) collective-permute-start(bf16[128,1536]{1,0:T(8,128)(2,1)S(1)} %get-tuple-element.82), channel_id=1, source_target_pairs={{0,128},{128,256},{256,384},{384,0},{8,136},{136,264},{264,392},{3... | collective-permute-start | bytes 1179656 | tf_op jit(solution)/shard_map/ppermute | solution.py:42
  58.4 14.3 %collective-permute-start.4 = (bf16[128,1536]{1,0:T(8,128)(2,1)S(1)}, bf16[128,1536]{1,0:T(8,128)(2,1)S(1)}, u32[]{:S(2)}, u32[]{:S(2)}) collective-permute-start(bf16[128,1536]{1,0:T(8,128)(2,1)S(1)} %get-tuple-element.82), channel_id=1, source_target_pairs={{0,256},{128,384},{256,0},{384,128},{8,264},{136,392},{264,8},{392... | collective-permute-start | bytes 1179656 | tf_op jit(solution)/shard_map/ppermute | solution.py:42
  62.0 21.4 %copy-start = (bf16[256,1536]{1,0:T(8,128)(2,1)}, bf16[256,1536]{1,0:T(8,128)(2,1)S(1)}, u32[]{:S(2)}) copy-start(bf16[256,1536]{1,0:T(8,128)(2,1)S(1)} %pad_maximum_fusion.refs_12_) | copy-start | bytes 2359300
  62.1 67.7 %copy-start.1 = (bf16[256,1536]{1,0:T(8,128)(2,1)}, bf16[256,1536]{1,0:T(8,128)(2,1)S(1)}, u32[]{:S(2)}) copy-start(bf16[256,1536]{1,0:T(8,128)(2,1)S(1)} %pad_maximum_fusion.2.refs_13_) | copy-start | bytes 2359300
  62.1 54.8 %copy-start.9 = (f32[1,1,8,16]{3,2,1,0:T(8,128)S(1)}, f32[1,1,8,16]{3,2,1,0:T(8,128)}, u32[]{:S(2)}) copy-start(f32[1,1,8,16]{3,2,1,0:T(8,128)} %param.12) | copy-start | bytes 1540
  62.1 55.0 %copy-start.10 = (f32[1,1,8,16]{3,2,1,0:T(8,128)S(1)}, f32[1,1,8,16]{3,2,1,0:T(8,128)}, u32[]{:S(2)}) copy-start(f32[1,1,8,16]{3,2,1,0:T(8,128)} %param.11) | copy-start | bytes 1540
  67.8 62.0 %copy-start.2 = (bf16[256,1536]{1,0:T(8,128)(2,1)}, bf16[256,1536]{1,0:T(8,128)(2,1)S(1)}, u32[]{:S(2)}) copy-start(bf16[256,1536]{1,0:T(8,128)(2,1)S(1)} %pad_maximum_fusion.1.refs_14_) | copy-start | bytes 2359300
  72.7 57.1 %copy-start.3 = (bf16[256,1536]{1,0:T(8,128)(2,1)}, bf16[256,1536]{1,0:T(8,128)(2,1)S(1)}, u32[]{:S(2)}) copy-start(bf16[256,1536]{1,0:T(8,128)(2,1)S(1)} %pad_maximum_fusion.3.refs_15_) | copy-start | bytes 2359300
  72.8 14.2 %collective-permute-start.6 = (bf16[256,1536]{1,0:T(8,128)(2,1)S(1)}, bf16[256,1536]{1,0:T(8,128)(2,1)}, u32[]{:S(2)}, u32[]{:S(2)}) collective-permute-start(bf16[256,1536]{1,0:T(8,128)(2,1)S(1)} %pad_maximum_fusion.1.refs_14_), channel_id=1, source_target_pairs={{0,384},{128,0},{256,128},{384,256},{8,392},{136,8},{264,136},{392... | collective-permute-start | bytes 2359304 | tf_op jit(solution)/shard_map/ppermute | solution.py:42
  74.7 16.0 %collective-permute-start.7 = (bf16[256,1536]{1,0:T(8,128)(2,1)S(1)}, bf16[256,1536]{1,0:T(8,128)(2,1)}, u32[]{:S(2)}, u32[]{:S(2)}) collective-permute-start(bf16[256,1536]{1,0:T(8,128)(2,1)S(1)} %pad_maximum_fusion.3.refs_15_), channel_id=1, source_target_pairs={{0,24},{8,0},{16,8},{24,16},{32,56},{40,32},{48,40},{56,48},{64,88... | collective-permute-start | bytes 2359304 | tf_op jit(solution)/shard_map/ppermute | solution.py:42
  77.6 15.7 %collective-permute-start.8 = (bf16[256,1536]{1,0:T(8,128)(2,1)S(1)}, bf16[256,1536]{1,0:T(8,128)(2,1)}, u32[]{:S(2)}, u32[]{:S(2)}) collective-permute-start(bf16[256,1536]{1,0:T(8,128)(2,1)S(1)} %pad_maximum_fusion.refs_12_), channel_id=1, source_target_pairs={{0,128},{128,256},{256,384},{384,0},{8,136},{136,264},{264,392},{3... | collective-permute-start | bytes 2359304 | tf_op jit(solution)/shard_map/ppermute | solution.py:42
  81.0 14.6 %collective-permute-start.9 = (bf16[256,1536]{1,0:T(8,128)(2,1)S(1)}, bf16[256,1536]{1,0:T(8,128)(2,1)}, u32[]{:S(2)}, u32[]{:S(2)}) collective-permute-start(bf16[256,1536]{1,0:T(8,128)(2,1)S(1)} %pad_maximum_fusion.2.refs_13_), channel_id=1, source_target_pairs={{0,8},{8,16},{16,24},{24,0},{32,40},{40,48},{48,56},{56,32},{64,72... | collective-permute-start | bytes 2359304 | tf_op jit(solution)/shard_map/ppermute | solution.py:42
  83.4 21.6 %collective-permute-start.10 = (bf16[256,1536]{1,0:T(8,128)(2,1)S(1)}, bf16[256,1536]{1,0:T(8,128)(2,1)S(1)}, u32[]{:S(2)}, u32[]{:S(2)}) collective-permute-start(bf16[256,1536]{1,0:T(8,128)(2,1)S(1)} %pad_maximum_fusion.refs_12_), channel_id=1, source_target_pairs={{0,384},{128,0},{256,128},{384,256},{8,392},{136,8},{264,136},{392... | collective-permute-start | bytes 2359304 | tf_op jit(solution)/shard_map/ppermute | solution.py:42
  86.9 21.5 %collective-permute-start.11 = (bf16[256,1536]{1,0:T(8,128)(2,1)S(1)}, bf16[256,1536]{1,0:T(8,128)(2,1)S(1)}, u32[]{:S(2)}, u32[]{:S(2)}) collective-permute-start(bf16[256,1536]{1,0:T(8,128)(2,1)S(1)} %pad_maximum_fusion.2.refs_13_), channel_id=1, source_target_pairs={{0,24},{8,0},{16,8},{24,16},{32,56},{40,32},{48,40},{56,48},{64,88... | collective-permute-start | bytes 2359304 | tf_op jit(solution)/shard_map/ppermute | solution.py:42
  90.7 22.0 %collective-permute-start.12 = (bf16[256,1536]{1,0:T(8,128)(2,1)S(1)}, bf16[256,1536]{1,0:T(8,128)(2,1)S(1)}, u32[]{:S(2)}, u32[]{:S(2)}) collective-permute-start(bf16[256,1536]{1,0:T(8,128)(2,1)S(1)} %pad_maximum_fusion.1.refs_14_), channel_id=1, source_target_pairs={{0,128},{128,256},{256,384},{384,0},{8,136},{136,264},{264,392},{3... | collective-permute-start | bytes 2359304 | tf_op jit(solution)/shard_map/ppermute | solution.py:42
  93.3 25.0 %collective-permute-start.13 = (bf16[256,1536]{1,0:T(8,128)(2,1)S(1)}, bf16[256,1536]{1,0:T(8,128)(2,1)}, u32[]{:S(2)}, u32[]{:S(2)}) collective-permute-start(bf16[256,1536]{1,0:T(8,128)(2,1)S(1)} %pad_maximum_fusion.3.refs_15_), channel_id=1, source_target_pairs={{0,8},{8,16},{16,24},{24,0},{32,40},{40,48},{48,56},{56,32},{64,72... | collective-permute-start | bytes 2359304 | tf_op jit(solution)/shard_map/ppermute | solution.py:42
  95.6 29.6 %collective-permute-start.14 = (bf16[256,1536]{1,0:T(8,128)(2,1)}, bf16[256,1536]{1,0:T(8,128)(2,1)}, u32[]{:S(2)}, u32[]{:S(2)}) collective-permute-start(bf16[256,1536]{1,0:T(8,128)(2,1)} %collective-permute-done.8.refs_2_), channel_id=1, source_target_pairs={{0,128},{128,256},{256,384},{384,0},{8,136},{136,264},{264,392},{3... | collective-permute-start | bytes 2359304 | tf_op jit(solution)/shard_map/ppermute | solution.py:42
  105.1 7.6 %copy-start.5 = (bf16[256,1536]{1,0:T(8,128)(2,1)}, bf16[256,1536]{1,0:T(8,128)(2,1)S(1)}, u32[]{:S(2)}) copy-start(bf16[256,1536]{1,0:T(8,128)(2,1)S(1)} %collective-permute-done.10.refs_4_) | copy-start | bytes 2359300
  105.1 24.7 %collective-permute-start.15 = (bf16[256,1536]{1,0:T(8,128)(2,1)}, bf16[256,1536]{1,0:T(8,128)(2,1)S(1)}, u32[]{:S(2)}, u32[]{:S(2)}) collective-permute-start(bf16[256,1536]{1,0:T(8,128)(2,1)} %collective-permute-done.9.refs_3_), channel_id=1, source_target_pairs={{0,8},{8,16},{16,24},{24,0},{32,40},{40,48},{48,56},{56,32},{64,72... | collective-permute-start | bytes 2359304 | tf_op jit(solution)/shard_map/ppermute | solution.py:42
  108.4 7.5 %copy-start.6 = (bf16[256,1536]{1,0:T(8,128)(2,1)}, bf16[256,1536]{1,0:T(8,128)(2,1)S(1)}, u32[]{:S(2)}) copy-start(bf16[256,1536]{1,0:T(8,128)(2,1)S(1)} %collective-permute-done.11.refs_5_) | copy-start | bytes 2359300
  108.4 21.3 %collective-permute-start.16 = (bf16[256,1536]{1,0:T(8,128)(2,1)}, bf16[256,1536]{1,0:T(8,128)(2,1)}, u32[]{:S(2)}, u32[]{:S(2)}) collective-permute-start(bf16[256,1536]{1,0:T(8,128)(2,1)} %collective-permute-done.6.refs_0_), channel_id=1, source_target_pairs={{0,384},{128,0},{256,128},{384,256},{8,392},{136,8},{264,136},{392... | collective-permute-start | bytes 2359304 | tf_op jit(solution)/shard_map/ppermute | solution.py:42
  112.7 3.3 %copy-start.7 = (bf16[256,1536]{1,0:T(8,128)(2,1)}, bf16[256,1536]{1,0:T(8,128)(2,1)S(1)}, u32[]{:S(2)}) copy-start(bf16[256,1536]{1,0:T(8,128)(2,1)S(1)} %collective-permute-done.12.refs_6_) | copy-start | bytes 2359300
  112.7 17.1 %collective-permute-start.17 = (bf16[256,1536]{1,0:T(8,128)(2,1)}, bf16[256,1536]{1,0:T(8,128)(2,1)}, u32[]{:S(2)}, u32[]{:S(2)}) collective-permute-start(bf16[256,1536]{1,0:T(8,128)(2,1)} %collective-permute-done.7.refs_1_), channel_id=1, source_target_pairs={{0,24},{8,0},{16,8},{24,16},{32,56},{40,32},{48,40},{56,48},{64,88... | collective-permute-start | bytes 2359304 | tf_op jit(solution)/shard_map/ppermute | solution.py:42
  129.8 0.9 copy-start.8
  169.4 24.2 %all-to-all-start.1 = ((bf16[64,2,8,128]{3,2,1,0:T(8,128)(2,1)}), bf16[64,2,8,128]{3,2,1,0:T(8,128)(2,1)S(1)}, u32[]{:S(2)}, u32[]{:S(2)}) async-start(bf16[64,2,8,128]{3,2,1,0:T(8,128)(2,1)} %copy.34), calls=%async_computation.1 | async-start | bytes 524288 | tf_op jit(solution)/shard_map/all_to_all | solution.py:29
  226.3 29.3 %all-to-all-start.3 = ((bf16[4,2,128,512]{3,2,1,0:T(8,128)(2,1)}), bf16[4,2,128,512]{3,2,1,0:T(8,128)(2,1)S(1)}, u32[]{:S(2)}, u32[]{:S(2)}) async-start(bf16[4,2,128,512]{3,2,1,0:T(8,128)(2,1)} %fusion.3), calls=%async_computation.3 | async-start | bytes 2097152 | tf_op jit(solution)/shard_map/all_to_all | solution.py:29
  236.4 19.7 %copy-start.4 = (bf16[512,512]{1,0:T(8,128)(2,1)S(1)}, bf16[512,512]{1,0:T(8,128)(2,1)}, u32[]{:S(2)}) copy-start(bf16[512,512]{1,0:T(8,128)(2,1)} %fusion.4.turn) | copy-start | bytes 1572868

commit v4 on v3

--- a/solution.py
+++ b/solution.py
@@ -43,9 +43,9 @@
 
 
 def near_blocks(own, sizes, axis):
-    across = shifted(own, sizes, axis, 2)
     up = shifted(own, sizes, axis, -1)
     down = shifted(own, sizes, axis, 1)
+    across = shifted(up, sizes, axis, -1)
     return jnp.concatenate([own, up]), jnp.concatenate([across, down])
 
 

time: 258 us -> 254 us (0.984)
  waiting for transfers between devices: 66.6 us -> 59.2 us
  starting transfers between devices: 65.8 us -> 69.5 us
    ppermute x18, waiting for transfers between devices: 28.7 us -> 21.3 us  [shifted(): return lax.ppermute(array, 'seq', shift_pairs(sizes, axis, step))]
    ppermute x18, starting transfers between devices: 56.3 us -> 59.7 us  [shifted(): return lax.ppermute(array, 'seq', shift_pairs(sizes, axis, step))]
  transfers between devices with their start and end apart: 20 -> 20, of which waited for: 10 -> 8; matrix products, arithmetic and copies ran while one was open for 3% -> 3% of each run, Pallas kernels for 0% -> 0%
where the time goes in v4:
time: 254 us; the launch traced here: 253 us
  blocking collectives  85.8 us (34%)
  starting transfers between devices  69.5 us (27%)
  waiting for transfers between devices  59.2 us (23%)
  Pallas kernels  21.3 us (8%)
  other arithmetic  6.93 us (3%)
  local copies, waits for them, and re-layouts  5.08 us (2%)
  matrix products  3.51 us (1%)
    ppermute x18, starting transfers between devices, shifted(): return lax.ppermute(array, 'seq', shift_pairs(sizes, axis, step))  59.7 us
    all_to_all x2, blocking collectives, exchange(): lax.all_to_all(blocks, axis, split_axis=0, concat_axis=0, tiled=True, axi...  45.6 us
    all_gather x1, blocking collectives, local(): lax.all_gather(weights, 'seq', axis=0, tiled=True, axis_index_groups=z_gr...  40.3 us
    all_to_all x2, waiting for transfers between devices, exchange(): lax.all_to_all(blocks, axis, split_axis=0, concat_axis=0, tiled=True, axi...  38 us
    ppermute x18, waiting for transfers between devices, shifted(): return lax.ppermute(array, 'seq', shift_pairs(sizes, axis, step))  21.3 us
    pallas_call x1, Pallas kernels, project_back(): pl.pallas_call(out_kernel, out_shape=jax.ShapeDtypeStruct((2, SIDE, 2, ro...  10.6 us
    all_to_all x2, starting transfers between devices, exchange(): lax.all_to_all(blocks, axis, split_axis=0, concat_axis=0, tiled=True, axi...  9.78 us
    pallas_call x1, Pallas kernels, project(): pl.pallas_call(project_kernel, out_shape=(jax.ShapeDtypeStruct((width, ro...  8.45 us
  transfers between devices with their start and end apart: 20, of which 8 were waited for; matrix products, arithmetic and copies ran while one was open for 3% of the time, Pallas kernels for 0%

profile of v4, /device:TPU:1, one launch (start us, length us, event | category | flops | bytes accessed | tf_op | source)
XLA Modules:
  0.0 252.5 jit_solution(8172593321125384386)
XLA Ops:
  0.6 0.9 pad_maximum_fusion.4
  1.6 40.3 %all_gather.3 = bf16[256,1536]{1,0:T(8,128)(2,1)S(1)} all-gather(bf16[64,1536]{1,0:T(8,128)(2,1)S(1)} %pad_maximum_fusion.4), channel_id=1, replica_groups={{0,32,64,96},{8,40,72,104},{16,48,80,112},{24,56,88,120},{128,160,192,2..., dimensions={0}, use_global_device_ids=true | all-gather | bytes 983040 | tf_op jit(solution)/shard_map/all_gather | solution.py:367
  41.9 4.4 %collective-permute-start = (bf16[128,1536]{1,0:T(8,128)(2,1)S(1)}, bf16[128,1536]{1,0:T(8,128)(2,1)S(1)}, u32[]{:S(2)}, u32[]{:S(2)}) collective-permute-start(bf16[128,1536]{1,0:T(8,128)(2,1)S(1)} %get-tuple-element.83), channel_id=1, source_target_pairs={{0,24},{8,0},{16,8},{24,16},{32,56},{40,32},{48,40},{56,48},{64,88... | collective-permute-start | bytes 1179656 | tf_op jit(solution)/shard_map/ppermute | solution.py:42
  46.3 4.6 %collective-permute-start.3 = (bf16[128,1536]{1,0:T(8,128)(2,1)S(1)}, bf16[128,1536]{1,0:T(8,128)(2,1)S(1)}, u32[]{:S(2)}, u32[]{:S(2)}) collective-permute-start(bf16[128,1536]{1,0:T(8,128)(2,1)S(1)} %get-tuple-element.82), channel_id=1, source_target_pairs={{0,384},{128,0},{256,128},{384,256},{8,392},{136,8},{264,136},{392... | collective-permute-start | bytes 1179656 | tf_op jit(solution)/shard_map/ppermute | solution.py:42
  50.9 1.9 collective-permute-start.2
  52.8 1.9 collective-permute-start.5
  54.8 4.6 %collective-permute-start.1 = (bf16[128,1536]{1,0:T(8,128)(2,1)S(1)}, bf16[128,1536]{1,0:T(8,128)(2,1)S(1)}, u32[]{:S(2)}, u32[]{:S(2)}) collective-permute-start(bf16[128,1536]{1,0:T(8,128)(2,1)S(1)} %collective-permute-done), channel_id=1, source_target_pairs={{0,24},{8,0},{16,8},{24,16},{32,56},{40,32},{48,40},{56,48},{64,88... | collective-permute-start | bytes 1179656 | tf_op jit(solution)/shard_map/ppermute | solution.py:42
  59.4 4.6 %collective-permute-start.4 = (bf16[128,1536]{1,0:T(8,128)(2,1)S(1)}, bf16[128,1536]{1,0:T(8,128)(2,1)S(1)}, u32[]{:S(2)}, u32[]{:S(2)}) collective-permute-start(bf16[128,1536]{1,0:T(8,128)(2,1)S(1)} %collective-permute-done.3), channel_id=1, source_target_pairs={{0,384},{128,0},{256,128},{384,256},{8,392},{136,8},{264,136},{392... | collective-permute-start | bytes 1179656 | tf_op jit(solution)/shard_map/ppermute | solution.py:42
  64.2 4.4 %collective-permute-done.4 = bf16[128,1536]{1,0:T(8,128)(2,1)S(1)} collective-permute-done((bf16[128,1536]{1,0:T(8,128)(2,1)S(1)}, bf16[128,1536]{1,0:T(8,128)(2,1)S(1)}, u32[]{:S(2)}, u32[]{:S(2)}) %collective-permute-start.4) | collective-permute-done | bytes 393248 | tf_op jit(solution)/shard_map/ppermute | solution.py:42
  68.7 5.0 %collective-permute-start.6 = (bf16[256,1536]{1,0:T(8,128)(2,1)S(1)}, bf16[256,1536]{1,0:T(8,128)(2,1)}, u32[]{:S(2)}, u32[]{:S(2)}) collective-permute-start(bf16[256,1536]{1,0:T(8,128)(2,1)S(1)} %pad_maximum_fusion.1.refs_14_), channel_id=1, source_target_pairs={{0,384},{128,0},{256,128},{384,256},{8,392},{136,8},{264,136},{392... | collective-permute-start | bytes 2359304 | tf_op jit(solution)/shard_map/ppermute | solution.py:42
  73.8 2.2 collective-permute-start.7
  76.0 1.9 collective-permute-start.8
  77.9 3.1 %collective-permute-start.9 = (bf16[256,1536]{1,0:T(8,128)(2,1)S(1)}, bf16[256,1536]{1,0:T(8,128)(2,1)}, u32[]{:S(2)}, u32[]{:S(2)}) collective-permute-start(bf16[256,1536]{1,0:T(8,128)(2,1)S(1)} %pad_maximum_fusion.2.refs_13_), channel_id=1, source_target_pairs={{0,8},{8,16},{16,24},{24,0},{32,40},{40,48},{48,56},{56,32},{64,72... | collective-permute-start | bytes 2359304 | tf_op jit(solution)/shard_map/ppermute | solution.py:42
  81.0 4.6 %collective-permute-start.10 = (bf16[256,1536]{1,0:T(8,128)(2,1)S(1)}, bf16[256,1536]{1,0:T(8,128)(2,1)S(1)}, u32[]{:S(2)}, u32[]{:S(2)}) collective-permute-start(bf16[256,1536]{1,0:T(8,128)(2,1)S(1)} %pad_maximum_fusion.refs_12_), channel_id=1, source_target_pairs={{0,384},{128,0},{256,128},{384,256},{8,392},{136,8},{264,136},{392... | collective-permute-start | bytes 2359304 | tf_op jit(solution)/shard_map/ppermute | solution.py:42
  85.6 3.4 %collective-permute-start.11 = (bf16[256,1536]{1,0:T(8,128)(2,1)S(1)}, bf16[256,1536]{1,0:T(8,128)(2,1)S(1)}, u32[]{:S(2)}, u32[]{:S(2)}) collective-permute-start(bf16[256,1536]{1,0:T(8,128)(2,1)S(1)} %pad_maximum_fusion.2.refs_13_), channel_id=1, source_target_pairs={{0,24},{8,0},{16,8},{24,16},{32,56},{40,32},{48,40},{56,48},{64,88... | collective-permute-start | bytes 2359304 | tf_op jit(solution)/shard_map/ppermute | solution.py:42
  89.0 1.9 collective-permute-start.12
  91.0 1.2 collective-permute-done.8.refs_2_
  92.2 2.5 collective-permute-start.13
  94.7 1.9 collective-permute-start.14
  96.6 6.4 %collective-permute-done.10.refs_4_ = bf16[256,1536]{1,0:T(8,128)(2,1)S(1)} collective-permute-done((bf16[256,1536]{1,0:T(8,128)(2,1)S(1)}, bf16[256,1536]{1,0:T(8,128)(2,1)S(1)}, u32[]{:S(2)}, u32[]{:S(2)}) %collective-permute-start.10) | collective-permute-done | bytes 786464 | tf_op jit(solution)/shard_map/ppermute | solution.py:42
  103.0 1.9 collective-permute-start.15
  104.9 0.8 collective-permute-done.11.refs_5_
  105.7 4.6 %collective-permute-start.16 = (bf16[256,1536]{1,0:T(8,128)(2,1)}, bf16[256,1536]{1,0:T(8,128)(2,1)}, u32[]{:S(2)}, u32[]{:S(2)}) collective-permute-start(bf16[256,1536]{1,0:T(8,128)(2,1)} %collective-permute-done.6.refs_0_), channel_id=1, source_target_pairs={{0,384},{128,0},{256,128},{384,256},{8,392},{136,8},{264,136},{392... | collective-permute-start | bytes 2359304 | tf_op jit(solution)/shard_map/ppermute | solution.py:42
  110.4 4.6 %collective-permute-start.17 = (bf16[256,1536]{1,0:T(8,128)(2,1)}, bf16[256,1536]{1,0:T(8,128)(2,1)}, u32[]{:S(2)}, u32[]{:S(2)}) collective-permute-start(bf16[256,1536]{1,0:T(8,128)(2,1)} %collective-permute-done.7.refs_1_), channel_id=1, source_target_pairs={{0,24},{8,0},{16,8},{24,16},{32,56},{40,32},{48,40},{56,48},{64,88... | collective-permute-start | bytes 2359304 | tf_op jit(solution)/shard_map/ppermute | solution.py:42
  115.0 0.9 fusion.4.turn
  116.3 1.0 shard_map.102
  117.3 6.8 %collective-permute-done.14.refs_8_ = bf16[256,1536]{1,0:T(8,128)(2,1)} collective-permute-done((bf16[256,1536]{1,0:T(8,128)(2,1)}, bf16[256,1536]{1,0:T(8,128)(2,1)}, u32[]{:S(2)}, u32[]{:S(2)}) %collective-permute-start.14) | collective-permute-done | bytes 786464 | tf_op jit(solution)/shard_map/ppermute | solution.py:42
  124.1 1.6 collective-permute-done.15.refs_9_
  125.8 0.9 copy-done.8
  126.6 8.4 %shard_map.103 = (f32[512,128]{1,0:T(8,128)}, f32[512,128]{1,0:T(8,128)}, bf16[2,512,128]{2,1,0:T(8,128)(2,1)}) custom-call(s32[1]{0:T(128)} %bitcast.place, bf16[128,4096]{1,0:T(8,128)(2,1)} %tokens.1, bf16[128,4096]{1,0:T(8,128)(2,1)} %cotangent.1, bf16[512,512]{1,0:T(8,128)(2,1)} %fusion.4.turn, bf16[256,1536]{1,0:T(8,128)(2,1)} %collective-permute-done.6.refs_0_, ...), custom_call_target="tpu_custom_call" | custom-call | tf_op jit(solution)/shard_map/pallas_call | solution.py:256
  135.1 1.0 copy.32
  136.1 28.5 %all_to_all.20 = bf16[64,2,8,128]{3,2,1,0:T(8,128)(2,1)S(1)} all-to-all(bf16[64,2,8,128]{3,2,1,0:T(8,128)(2,1)S(1)} %copy.32), channel_id=1, replica_groups=mesh['seq'=64,'tp'=8] {'seq'}, dimensions={0} | all-to-all | bytes 524288 | tf_op jit(solution)/shard_map/all_to_all | solution.py:29
  164.7 1.2 shard_map.104
  165.9 0.9 copy.34
  166.8 5.8 %all-to-all-start.1 = ((bf16[64,2,8,128]{3,2,1,0:T(8,128)(2,1)}), bf16[64,2,8,128]{3,2,1,0:T(8,128)(2,1)S(1)}, u32[]{:S(2)}, u32[]{:S(2)}) async-start(bf16[64,2,8,128]{3,2,1,0:T(8,128)(2,1)} %copy.34), calls=%async_computation.1 | async-start | bytes 524288 | tf_op jit(solution)/shard_map/all_to_all | solution.py:29
  172.6 18.8 %all-to-all-done.1 = bf16[64,2,8,128]{3,2,1,0:T(8,128)(2,1)S(1)} async-done(((bf16[64,2,8,128]{3,2,1,0:T(8,128)(2,1)}), bf16[64,2,8,128]{3,2,1,0:T(8,128)(2,1)S(1)}, u32[]{:S(2)}, u32[]{:S(2)}) %all-to-all-start.1) | async-done | bytes 262176 | tf_op jit(solution)/shard_map/all_to_all | solution.py:29
  191.4 0.7 copy_bitcast_fusion.filtered
  192.1 10.6 %shard_map.105 = bf16[2,4,2,128,512]{4,3,2,1,0:T(8,128)(2,1)} custom-call(s32[1]{0:T(128)} %bitcast.place, f32[512,128]{1,0:T(8,128)} %get-tuple-element.68.gates, f32[512,128]{1,0:T(8,128)} %get-tuple-element.69.back, bf16[2,512,128]{2,1,0:T(8,128)(2,1)} %copy_bitcast_fusion.filtered, bf16[256,1536]{1,0:T(8,128)(2,1)} %collective-permute-done.6.refs_0_, ...), custom_call_target="tpu_custom_call" | custom-call | tf_op jit(solution)/shard_map/pallas_call | solution.py:308
  202.7 17.1 %all_to_all.21 = bf16[2,4,2,128,512]{4,3,2,1,0:T(8,128)(2,1)S(1)} all-to-all(bf16[2,4,2,128,512]{4,3,2,1,0:T(8,128)(2,1)} %shard_map.105), channel_id=1, replica_groups={{0,1},{2,3},{4,5},{6,7},{8,9},{10,11},{12,13},{14,15},{16,17},{18,19},{..., dimensions={0} | all-to-all | bytes 4194304 | tf_op jit(solution)/shard_map/all_to_all | solution.py:29
  219.8 0.6 convert_element_type.78
  220.3 1.4 fusion.3
  221.7 4.0 %all-to-all-start.3 = ((bf16[4,2,128,512]{3,2,1,0:T(8,128)(2,1)}), bf16[4,2,128,512]{3,2,1,0:T(8,128)(2,1)S(1)}, u32[]{:S(2)}, u32[]{:S(2)}) async-start(bf16[4,2,128,512]{3,2,1,0:T(8,128)(2,1)} %fusion.3), calls=%async_computation.3 | async-start | bytes 2097152 | tf_op jit(solution)/shard_map/all_to_all | solution.py:29
  227.1 1.5 multiply_reduce_fusion
  229.1 1.0 fusion.1
  230.1 1.1 fusion.2
  231.2 0.6 fusion.39
  231.8 19.2 %all-to-all-done.3 = bf16[4,2,128,512]{3,2,1,0:T(8,128)(2,1)S(1)} async-done(((bf16[4,2,128,512]{3,2,1,0:T(8,128)(2,1)}), bf16[4,2,128,512]{3,2,1,0:T(8,128)(2,1)S(1)}, u32[]{:S(2)}, u32[]{:S(2)}) %all-to-all-start.3) | async-done | bytes 1048608 | tf_op jit(solution)/shard_map/all_to_all | solution.py:29
  251.8 0.7 fusion.56
  (66 shorter events, 3.4 us)
Async XLA Ops:
  41.9 12.9 %collective-permute-start = (bf16[128,1536]{1,0:T(8,128)(2,1)S(1)}, bf16[128,1536]{1,0:T(8,128)(2,1)S(1)}, u32[]{:S(2)}, u32[]{:S(2)}) collective-permute-start(bf16[128,1536]{1,0:T(8,128)(2,1)S(1)} %get-tuple-element.83), channel_id=1, source_target_pairs={{0,24},{8,0},{16,8},{24,16},{32,56},{40,32},{48,40},{56,48},{64,88... | collective-permute-start | bytes 1179656 | tf_op jit(solution)/shard_map/ppermute | solution.py:42
  46.3 13.1 %collective-permute-start.3 = (bf16[128,1536]{1,0:T(8,128)(2,1)S(1)}, bf16[128,1536]{1,0:T(8,128)(2,1)S(1)}, u32[]{:S(2)}, u32[]{:S(2)}) collective-permute-start(bf16[128,1536]{1,0:T(8,128)(2,1)S(1)} %get-tuple-element.82), channel_id=1, source_target_pairs={{0,384},{128,0},{256,128},{384,256},{8,392},{136,8},{264,136},{392... | collective-permute-start | bytes 1179656 | tf_op jit(solution)/shard_map/ppermute | solution.py:42
  50.9 13.2 %collective-permute-start.2 = (bf16[128,1536]{1,0:T(8,128)(2,1)S(1)}, bf16[128,1536]{1,0:T(8,128)(2,1)S(1)}, u32[]{:S(2)}, u32[]{:S(2)}) collective-permute-start(bf16[128,1536]{1,0:T(8,128)(2,1)S(1)} %get-tuple-element.83), channel_id=1, source_target_pairs={{0,8},{8,16},{16,24},{24,0},{32,40},{40,48},{48,56},{56,32},{64,72... | collective-permute-start | bytes 1179656 | tf_op jit(solution)/shard_map/ppermute | solution.py:42
  52.8 11.4 %collective-permute-start.5 = (bf16[128,1536]{1,0:T(8,128)(2,1)S(1)}, bf16[128,1536]{1,0:T(8,128)(2,1)S(1)}, u32[]{:S(2)}, u32[]{:S(2)}) collective-permute-start(bf16[128,1536]{1,0:T(8,128)(2,1)S(1)} %get-tuple-element.82), channel_id=1, source_target_pairs={{0,128},{128,256},{256,384},{384,0},{8,136},{136,264},{264,392},{3... | collective-permute-start | bytes 1179656 | tf_op jit(solution)/shard_map/ppermute | solution.py:42
  54.8 9.4 %collective-permute-start.1 = (bf16[128,1536]{1,0:T(8,128)(2,1)S(1)}, bf16[128,1536]{1,0:T(8,128)(2,1)S(1)}, u32[]{:S(2)}, u32[]{:S(2)}) collective-permute-start(bf16[128,1536]{1,0:T(8,128)(2,1)S(1)} %collective-permute-done), channel_id=1, source_target_pairs={{0,24},{8,0},{16,8},{24,16},{32,56},{40,32},{48,40},{56,48},{64,88... | collective-permute-start | bytes 1179656 | tf_op jit(solution)/shard_map/ppermute | solution.py:42
  59.4 9.3 %collective-permute-start.4 = (bf16[128,1536]{1,0:T(8,128)(2,1)S(1)}, bf16[128,1536]{1,0:T(8,128)(2,1)S(1)}, u32[]{:S(2)}, u32[]{:S(2)}) collective-permute-start(bf16[128,1536]{1,0:T(8,128)(2,1)S(1)} %collective-permute-done.3), channel_id=1, source_target_pairs={{0,384},{128,0},{256,128},{384,256},{8,392},{136,8},{264,136},{392... | collective-permute-start | bytes 1179656 | tf_op jit(solution)/shard_map/ppermute | solution.py:42
  64.0 17.0 %copy-start = (bf16[256,1536]{1,0:T(8,128)(2,1)}, bf16[256,1536]{1,0:T(8,128)(2,1)S(1)}, u32[]{:S(2)}) copy-start(bf16[256,1536]{1,0:T(8,128)(2,1)S(1)} %pad_maximum_fusion.refs_12_) | copy-start | bytes 2359300
  64.1 61.7 %copy-start.1 = (bf16[256,1536]{1,0:T(8,128)(2,1)}, bf16[256,1536]{1,0:T(8,128)(2,1)S(1)}, u32[]{:S(2)}) copy-start(bf16[256,1536]{1,0:T(8,128)(2,1)S(1)} %pad_maximum_fusion.2.refs_13_) | copy-start | bytes 2359300
  64.1 51.9 %copy-start.9 = (f32[1,1,8,16]{3,2,1,0:T(8,128)S(1)}, f32[1,1,8,16]{3,2,1,0:T(8,128)}, u32[]{:S(2)}) copy-start(f32[1,1,8,16]{3,2,1,0:T(8,128)} %param.12) | copy-start | bytes 1540
  64.1 52.0 %copy-start.10 = (f32[1,1,8,16]{3,2,1,0:T(8,128)S(1)}, f32[1,1,8,16]{3,2,1,0:T(8,128)}, u32[]{:S(2)}) copy-start(f32[1,1,8,16]{3,2,1,0:T(8,128)} %param.11) | copy-start | bytes 1540
  64.2 61.6 %copy-start.2 = (bf16[256,1536]{1,0:T(8,128)(2,1)}, bf16[256,1536]{1,0:T(8,128)(2,1)S(1)}, u32[]{:S(2)}) copy-start(bf16[256,1536]{1,0:T(8,128)(2,1)S(1)} %pad_maximum_fusion.1.refs_14_) | copy-start | bytes 2359300
  68.7 57.1 %copy-start.3 = (bf16[256,1536]{1,0:T(8,128)(2,1)}, bf16[256,1536]{1,0:T(8,128)(2,1)S(1)}, u32[]{:S(2)}) copy-start(bf16[256,1536]{1,0:T(8,128)(2,1)S(1)} %pad_maximum_fusion.3.refs_15_) | copy-start | bytes 2359300
  68.7 16.9 %collective-permute-start.6 = (bf16[256,1536]{1,0:T(8,128)(2,1)S(1)}, bf16[256,1536]{1,0:T(8,128)(2,1)}, u32[]{:S(2)}, u32[]{:S(2)}) collective-permute-start(bf16[256,1536]{1,0:T(8,128)(2,1)S(1)} %pad_maximum_fusion.1.refs_14_), channel_id=1, source_target_pairs={{0,384},{128,0},{256,128},{384,256},{8,392},{136,8},{264,136},{392... | collective-permute-start | bytes 2359304 | tf_op jit(solution)/shard_map/ppermute | solution.py:42
  73.8 15.3 %collective-permute-start.7 = (bf16[256,1536]{1,0:T(8,128)(2,1)S(1)}, bf16[256,1536]{1,0:T(8,128)(2,1)}, u32[]{:S(2)}, u32[]{:S(2)}) collective-permute-start(bf16[256,1536]{1,0:T(8,128)(2,1)S(1)} %pad_maximum_fusion.3.refs_15_), channel_id=1, source_target_pairs={{0,24},{8,0},{16,8},{24,16},{32,56},{40,32},{48,40},{56,48},{64,88... | collective-permute-start | bytes 2359304 | tf_op jit(solution)/shard_map/ppermute | solution.py:42
  76.0 16.2 %collective-permute-start.8 = (bf16[256,1536]{1,0:T(8,128)(2,1)S(1)}, bf16[256,1536]{1,0:T(8,128)(2,1)}, u32[]{:S(2)}, u32[]{:S(2)}) collective-permute-start(bf16[256,1536]{1,0:T(8,128)(2,1)S(1)} %pad_maximum_fusion.refs_12_), channel_id=1, source_target_pairs={{0,128},{128,256},{256,384},{384,0},{8,136},{136,264},{264,392},{3... | collective-permute-start | bytes 2359304 | tf_op jit(solution)/shard_map/ppermute | solution.py:42
  77.9 16.7 %collective-permute-start.9 = (bf16[256,1536]{1,0:T(8,128)(2,1)S(1)}, bf16[256,1536]{1,0:T(8,128)(2,1)}, u32[]{:S(2)}, u32[]{:S(2)}) collective-permute-start(bf16[256,1536]{1,0:T(8,128)(2,1)S(1)} %pad_maximum_fusion.2.refs_13_), channel_id=1, source_target_pairs={{0,8},{8,16},{16,24},{24,0},{32,40},{40,48},{48,56},{56,32},{64,72... | collective-permute-start | bytes 2359304 | tf_op jit(solution)/shard_map/ppermute | solution.py:42
  81.0 22.0 %collective-permute-start.10 = (bf16[256,1536]{1,0:T(8,128)(2,1)S(1)}, bf16[256,1536]{1,0:T(8,128)(2,1)S(1)}, u32[]{:S(2)}, u32[]{:S(2)}) collective-permute-start(bf16[256,1536]{1,0:T(8,128)(2,1)S(1)} %pad_maximum_fusion.refs_12_), channel_id=1, source_target_pairs={{0,384},{128,0},{256,128},{384,256},{8,392},{136,8},{264,136},{392... | collective-permute-start | bytes 2359304 | tf_op jit(solution)/shard_map/ppermute | solution.py:42
  85.6 20.1 %collective-permute-start.11 = (bf16[256,1536]{1,0:T(8,128)(2,1)S(1)}, bf16[256,1536]{1,0:T(8,128)(2,1)S(1)}, u32[]{:S(2)}, u32[]{:S(2)}) collective-permute-start(bf16[256,1536]{1,0:T(8,128)(2,1)S(1)} %pad_maximum_fusion.2.refs_13_), channel_id=1, source_target_pairs={{0,24},{8,0},{16,8},{24,16},{32,56},{40,32},{48,40},{56,48},{64,88... | collective-permute-start | bytes 2359304 | tf_op jit(solution)/shard_map/ppermute | solution.py:42
  89.0 21.3 %collective-permute-start.12 = (bf16[256,1536]{1,0:T(8,128)(2,1)S(1)}, bf16[256,1536]{1,0:T(8,128)(2,1)S(1)}, u32[]{:S(2)}, u32[]{:S(2)}) collective-permute-start(bf16[256,1536]{1,0:T(8,128)(2,1)S(1)} %pad_maximum_fusion.1.refs_14_), channel_id=1, source_target_pairs={{0,128},{128,256},{256,384},{384,0},{8,136},{136,264},{264,392},{3... | collective-permute-start | bytes 2359304 | tf_op jit(solution)/shard_map/ppermute | solution.py:42
  92.2 25.2 %collective-permute-start.13 = (bf16[256,1536]{1,0:T(8,128)(2,1)S(1)}, bf16[256,1536]{1,0:T(8,128)(2,1)}, u32[]{:S(2)}, u32[]{:S(2)}) collective-permute-start(bf16[256,1536]{1,0:T(8,128)(2,1)S(1)} %pad_maximum_fusion.3.refs_15_), channel_id=1, source_target_pairs={{0,8},{8,16},{16,24},{24,0},{32,40},{40,48},{48,56},{56,32},{64,72... | collective-permute-start | bytes 2359304 | tf_op jit(solution)/shard_map/ppermute | solution.py:42
  94.7 29.4 %collective-permute-start.14 = (bf16[256,1536]{1,0:T(8,128)(2,1)}, bf16[256,1536]{1,0:T(8,128)(2,1)}, u32[]{:S(2)}, u32[]{:S(2)}) collective-permute-start(bf16[256,1536]{1,0:T(8,128)(2,1)} %collective-permute-done.8.refs_2_), channel_id=1, source_target_pairs={{0,128},{128,256},{256,384},{384,0},{8,136},{136,264},{264,392},{3... | collective-permute-start | bytes 2359304 | tf_op jit(solution)/shard_map/ppermute | solution.py:42
  103.0 7.4 %copy-start.5 = (bf16[256,1536]{1,0:T(8,128)(2,1)}, bf16[256,1536]{1,0:T(8,128)(2,1)S(1)}, u32[]{:S(2)}) copy-start(bf16[256,1536]{1,0:T(8,128)(2,1)S(1)} %collective-permute-done.10.refs_4_) | copy-start | bytes 2359300
  103.0 22.8 %collective-permute-start.15 = (bf16[256,1536]{1,0:T(8,128)(2,1)}, bf16[256,1536]{1,0:T(8,128)(2,1)S(1)}, u32[]{:S(2)}, u32[]{:S(2)}) collective-permute-start(bf16[256,1536]{1,0:T(8,128)(2,1)} %collective-permute-done.9.refs_3_), channel_id=1, source_target_pairs={{0,8},{8,16},{16,24},{24,0},{32,40},{40,48},{48,56},{56,32},{64,72... | collective-permute-start | bytes 2359304 | tf_op jit(solution)/shard_map/ppermute | solution.py:42
  105.7 9.3 %copy-start.6 = (bf16[256,1536]{1,0:T(8,128)(2,1)}, bf16[256,1536]{1,0:T(8,128)(2,1)S(1)}, u32[]{:S(2)}) copy-start(bf16[256,1536]{1,0:T(8,128)(2,1)S(1)} %collective-permute-done.11.refs_5_) | copy-start | bytes 2359300
  105.7 20.0 %collective-permute-start.16 = (bf16[256,1536]{1,0:T(8,128)(2,1)}, bf16[256,1536]{1,0:T(8,128)(2,1)}, u32[]{:S(2)}, u32[]{:S(2)}) collective-permute-start(bf16[256,1536]{1,0:T(8,128)(2,1)} %collective-permute-done.6.refs_0_), channel_id=1, source_target_pairs={{0,384},{128,0},{256,128},{384,256},{8,392},{136,8},{264,136},{392... | collective-permute-start | bytes 2359304 | tf_op jit(solution)/shard_map/ppermute | solution.py:42
  110.4 4.6 %copy-start.7 = (bf16[256,1536]{1,0:T(8,128)(2,1)}, bf16[256,1536]{1,0:T(8,128)(2,1)S(1)}, u32[]{:S(2)}) copy-start(bf16[256,1536]{1,0:T(8,128)(2,1)S(1)} %collective-permute-done.12.refs_6_) | copy-start | bytes 2359300
  110.4 15.4 %collective-permute-start.17 = (bf16[256,1536]{1,0:T(8,128)(2,1)}, bf16[256,1536]{1,0:T(8,128)(2,1)}, u32[]{:S(2)}, u32[]{:S(2)}) collective-permute-start(bf16[256,1536]{1,0:T(8,128)(2,1)} %collective-permute-done.7.refs_1_), channel_id=1, source_target_pairs={{0,24},{8,0},{16,8},{24,16},{32,56},{40,32},{48,40},{56,48},{64,88... | collective-permute-start | bytes 2359304 | tf_op jit(solution)/shard_map/ppermute | solution.py:42
  125.7 0.9 copy-start.8
  166.8 24.6 %all-to-all-start.1 = ((bf16[64,2,8,128]{3,2,1,0:T(8,128)(2,1)}), bf16[64,2,8,128]{3,2,1,0:T(8,128)(2,1)S(1)}, u32[]{:S(2)}, u32[]{:S(2)}) async-start(bf16[64,2,8,128]{3,2,1,0:T(8,128)(2,1)} %copy.34), calls=%async_computation.1 | async-start | bytes 524288 | tf_op jit(solution)/shard_map/all_to_all | solution.py:29
  221.7 29.3 %all-to-all-start.3 = ((bf16[4,2,128,512]{3,2,1,0:T(8,128)(2,1)}), bf16[4,2,128,512]{3,2,1,0:T(8,128)(2,1)S(1)}, u32[]{:S(2)}, u32[]{:S(2)}) async-start(bf16[4,2,128,512]{3,2,1,0:T(8,128)(2,1)} %fusion.3), calls=%async_computation.3 | async-start | bytes 2097152 | tf_op jit(solution)/shard_map/all_to_all | solution.py:29
  231.8 19.7 %copy-start.4 = (bf16[512,512]{1,0:T(8,128)(2,1)S(1)}, bf16[512,512]{1,0:T(8,128)(2,1)}, u32[]{:S(2)}) copy-start(bf16[512,512]{1,0:T(8,128)(2,1)} %fusion.4.turn) | copy-start | bytes 1572868

commit v5 on v4

--- a/solution.py
+++ b/solution.py
@@ -367,7 +367,7 @@
     along_z = lax.all_gather(weights, "seq", axis=0, tiled=True, axis_index_groups=z_groups)
     along_z = along_z.reshape(2, 2 * block, 3 * width)
     near = near_blocks(along_z[0], sizes, 2), near_blocks(along_z[1], sizes, 0)
-    near = lax.optimization_barrier(near)
+    near = [lax.optimization_barrier(pair) for pair in near]
     blocks = far_blocks(*near[0], sizes, 0) + far_blocks(*near[1], sizes, 2)
 
     place = (me // SIDE**2).reshape(1)

time: 254 us -> 253 us (level)
  starting transfers between devices: 69.5 us -> 73.8 us
  waiting for transfers between devices: 59.2 us -> 55.4 us
    ppermute x18, waiting for transfers between devices: 21.3 us -> 17.7 us  [shifted(): return lax.ppermute(array, 'seq', shift_pairs(sizes, axis, step))]
    ppermute x18, starting transfers between devices: 59.7 us -> 62.8 us  [shifted(): return lax.ppermute(array, 'seq', shift_pairs(sizes, axis, step))]
  transfers between devices with their start and end apart: 20 -> 20, of which waited for: 8 -> 6; matrix products, arithmetic and copies ran while one was open for 3% -> 3% of each run, Pallas kernels for 0% -> 0%
where the time goes in v5:
time: 253 us; the launch traced here: 252 us
  blocking collectives  84.7 us (33%)
  starting transfers between devices  73.8 us (29%)
  waiting for transfers between devices  55.4 us (22%)
  Pallas kernels  21.3 us (8%)
  other arithmetic  6.93 us (3%)
  local copies, waits for them, and re-layouts  5.08 us (2%)
  matrix products  3.51 us (1%)
    ppermute x18, starting transfers between devices, shifted(): return lax.ppermute(array, 'seq', shift_pairs(sizes, axis, step))  62.8 us
    all_to_all x2, blocking collectives, exchange(): lax.all_to_all(blocks, axis, split_axis=0, concat_axis=0, tiled=True, axi...  44.4 us
    all_gather x1, blocking collectives, local(): lax.all_gather(weights, 'seq', axis=0, tiled=True, axis_index_groups=z_gr...  40.3 us
    all_to_all x2, waiting for transfers between devices, exchange(): lax.all_to_all(blocks, axis, split_axis=0, concat_axis=0, tiled=True, axi...  37.7 us
    ppermute x18, waiting for transfers between devices, shifted(): return lax.ppermute(array, 'seq', shift_pairs(sizes, axis, step))  17.7 us
    all_to_all x2, starting transfers between devices, exchange(): lax.all_to_all(blocks, axis, split_axis=0, concat_axis=0, tiled=True, axi...  11 us
    pallas_call x1, Pallas kernels, project_back(): pl.pallas_call(out_kernel, out_shape=jax.ShapeDtypeStruct((2, SIDE, 2, ro...  10.6 us
    pallas_call x1, Pallas kernels, project(): pl.pallas_call(project_kernel, out_shape=(jax.ShapeDtypeStruct((width, ro...  8.45 us
  transfers between devices with their start and end apart: 20, of which 6 were waited for; matrix products, arithmetic and copies ran while one was open for 3% of the time, Pallas kernels for 0%

profile of v5, /device:TPU:1, one launch (start us, length us, event | category | flops | bytes accessed | tf_op | source)
XLA Modules:
  0.0 252.0 jit_solution(16116686870209956013)
XLA Ops:
  0.6 0.9 pad_maximum_fusion.4
  1.6 40.3 %all_gather.3 = bf16[256,1536]{1,0:T(8,128)(2,1)S(1)} all-gather(bf16[64,1536]{1,0:T(8,128)(2,1)S(1)} %pad_maximum_fusion.4), channel_id=1, replica_groups={{0,32,64,96},{8,40,72,104},{16,48,80,112},{24,56,88,120},{128,160,192,2..., dimensions={0}, use_global_device_ids=true | all-gather | bytes 983040 | tf_op jit(solution)/shard_map/all_gather | solution.py:367
  41.9 4.4 %collective-permute-start = (bf16[128,1536]{1,0:T(8,128)(2,1)S(1)}, bf16[128,1536]{1,0:T(8,128)(2,1)S(1)}, u32[]{:S(2)}, u32[]{:S(2)}) collective-permute-start(bf16[128,1536]{1,0:T(8,128)(2,1)S(1)} %get-tuple-element.83), channel_id=1, source_target_pairs={{0,24},{8,0},{16,8},{24,16},{32,56},{40,32},{48,40},{56,48},{64,88... | collective-permute-start | bytes 1179656 | tf_op jit(solution)/shard_map/ppermute | solution.py:42
  46.3 4.6 %collective-permute-start.4 = (bf16[128,1536]{1,0:T(8,128)(2,1)S(1)}, bf16[128,1536]{1,0:T(8,128)(2,1)S(1)}, u32[]{:S(2)}, u32[]{:S(2)}) collective-permute-start(bf16[128,1536]{1,0:T(8,128)(2,1)S(1)} %get-tuple-element.82), channel_id=1, source_target_pairs={{0,384},{128,0},{256,128},{384,256},{8,392},{136,8},{264,136},{392... | collective-permute-start | bytes 1179656 | tf_op jit(solution)/shard_map/ppermute | solution.py:42
  50.9 1.9 collective-permute-start.2
  52.8 1.9 collective-permute-start.6
  54.8 4.6 %collective-permute-start.1 = (bf16[128,1536]{1,0:T(8,128)(2,1)S(1)}, bf16[128,1536]{1,0:T(8,128)(2,1)S(1)}, u32[]{:S(2)}, u32[]{:S(2)}) collective-permute-start(bf16[128,1536]{1,0:T(8,128)(2,1)S(1)} %collective-permute-done), channel_id=1, source_target_pairs={{0,24},{8,0},{16,8},{24,16},{32,56},{40,32},{48,40},{56,48},{64,88... | collective-permute-start | bytes 1179656 | tf_op jit(solution)/shard_map/ppermute | solution.py:42
  59.4 4.6 %collective-permute-start.5 = (bf16[128,1536]{1,0:T(8,128)(2,1)S(1)}, bf16[128,1536]{1,0:T(8,128)(2,1)S(1)}, u32[]{:S(2)}, u32[]{:S(2)}) collective-permute-start(bf16[128,1536]{1,0:T(8,128)(2,1)S(1)} %collective-permute-done.4), channel_id=1, source_target_pairs={{0,384},{128,0},{256,128},{384,256},{8,392},{136,8},{264,136},{392... | collective-permute-start | bytes 1179656 | tf_op jit(solution)/shard_map/ppermute | solution.py:42
  64.2 4.5 %collective-permute-start.3 = (bf16[256,1536]{1,0:T(8,128)(2,1)S(1)}, bf16[256,1536]{1,0:T(8,128)(2,1)}, u32[]{:S(2)}, u32[]{:S(2)}) collective-permute-start(bf16[256,1536]{1,0:T(8,128)(2,1)S(1)} %pad_maximum_fusion.1.refs_14_), channel_id=1, source_target_pairs={{0,384},{128,0},{256,128},{384,256},{8,392},{136,8},{264,136},{392... | collective-permute-start | bytes 2359304 | tf_op jit(solution)/shard_map/ppermute | solution.py:42
  68.8 5.0 %collective-permute-start.7 = (bf16[256,1536]{1,0:T(8,128)(2,1)S(1)}, bf16[256,1536]{1,0:T(8,128)(2,1)}, u32[]{:S(2)}, u32[]{:S(2)}) collective-permute-start(bf16[256,1536]{1,0:T(8,128)(2,1)S(1)} %pad_maximum_fusion.3.refs_15_), channel_id=1, source_target_pairs={{0,24},{8,0},{16,8},{24,16},{32,56},{40,32},{48,40},{56,48},{64,88... | collective-permute-start | bytes 2359304 | tf_op jit(solution)/shard_map/ppermute | solution.py:42
  73.8 1.9 collective-permute-start.8
  75.8 1.9 collective-permute-start.9
  77.7 4.6 %collective-permute-start.10 = (bf16[256,1536]{1,0:T(8,128)(2,1)S(1)}, bf16[256,1536]{1,0:T(8,128)(2,1)S(1)}, u32[]{:S(2)}, u32[]{:S(2)}) collective-permute-start(bf16[256,1536]{1,0:T(8,128)(2,1)S(1)} %pad_maximum_fusion.refs_12_), channel_id=1, source_target_pairs={{0,384},{128,0},{256,128},{384,256},{8,392},{136,8},{264,136},{392... | collective-permute-start | bytes 2359304 | tf_op jit(solution)/shard_map/ppermute | solution.py:42
  82.3 3.2 %collective-permute-done.3.refs_0_ = bf16[256,1536]{1,0:T(8,128)(2,1)} collective-permute-done((bf16[256,1536]{1,0:T(8,128)(2,1)S(1)}, bf16[256,1536]{1,0:T(8,128)(2,1)}, u32[]{:S(2)}, u32[]{:S(2)}) %collective-permute-start.3) | collective-permute-done | bytes 786464 | tf_op jit(solution)/shard_map/ppermute | solution.py:42
  85.5 2.1 collective-permute-start.11
  87.7 1.9 collective-permute-start.12
  89.6 3.1 %collective-permute-start.13 = (bf16[256,1536]{1,0:T(8,128)(2,1)S(1)}, bf16[256,1536]{1,0:T(8,128)(2,1)}, u32[]{:S(2)}, u32[]{:S(2)}) collective-permute-start(bf16[256,1536]{1,0:T(8,128)(2,1)S(1)} %pad_maximum_fusion.3.refs_15_), channel_id=1, source_target_pairs={{0,8},{8,16},{16,24},{24,0},{32,40},{40,48},{48,56},{56,32},{64,72... | collective-permute-start | bytes 2359304 | tf_op jit(solution)/shard_map/ppermute | solution.py:42
  92.8 3.9 %collective-permute-start.14 = (bf16[256,1536]{1,0:T(8,128)(2,1)}, bf16[256,1536]{1,0:T(8,128)(2,1)}, u32[]{:S(2)}, u32[]{:S(2)}) collective-permute-start(bf16[256,1536]{1,0:T(8,128)(2,1)} %collective-permute-done.8.refs_2_), channel_id=1, source_target_pairs={{0,128},{128,256},{256,384},{384,0},{8,136},{136,264},{264,392},{3... | collective-permute-start | bytes 2359304 | tf_op jit(solution)/shard_map/ppermute | solution.py:42
  96.7 5.7 %collective-permute-done.10.refs_4_ = bf16[256,1536]{1,0:T(8,128)(2,1)S(1)} collective-permute-done((bf16[256,1536]{1,0:T(8,128)(2,1)S(1)}, bf16[256,1536]{1,0:T(8,128)(2,1)S(1)}, u32[]{:S(2)}, u32[]{:S(2)}) %collective-permute-start.10) | collective-permute-done | bytes 786464 | tf_op jit(solution)/shard_map/ppermute | solution.py:42
  102.3 2.1 collective-permute-start.15
  104.5 5.3 %collective-permute-start.16 = (bf16[256,1536]{1,0:T(8,128)(2,1)}, bf16[256,1536]{1,0:T(8,128)(2,1)}, u32[]{:S(2)}, u32[]{:S(2)}) collective-permute-start(bf16[256,1536]{1,0:T(8,128)(2,1)} %collective-permute-done.3.refs_0_), channel_id=1, source_target_pairs={{0,384},{128,0},{256,128},{384,256},{8,392},{136,8},{264,136},{392... | collective-permute-start | bytes 2359304 | tf_op jit(solution)/shard_map/ppermute | solution.py:42
  109.8 4.3 %collective-permute-start.17 = (bf16[256,1536]{1,0:T(8,128)(2,1)}, bf16[256,1536]{1,0:T(8,128)(2,1)}, u32[]{:S(2)}, u32[]{:S(2)}) collective-permute-start(bf16[256,1536]{1,0:T(8,128)(2,1)} %collective-permute-done.7.refs_1_), channel_id=1, source_target_pairs={{0,24},{8,0},{16,8},{24,16},{32,56},{40,32},{48,40},{56,48},{64,88... | collective-permute-start | bytes 2359304 | tf_op jit(solution)/shard_map/ppermute | solution.py:42
  114.3 0.9 fusion.4.turn
  115.5 1.0 shard_map.102
  116.6 5.2 %collective-permute-done.14.refs_8_ = bf16[256,1536]{1,0:T(8,128)(2,1)} collective-permute-done((bf16[256,1536]{1,0:T(8,128)(2,1)}, bf16[256,1536]{1,0:T(8,128)(2,1)}, u32[]{:S(2)}, u32[]{:S(2)}) %collective-permute-start.14) | collective-permute-done | bytes 786464 | tf_op jit(solution)/shard_map/ppermute | solution.py:42
  121.8 3.5 %collective-permute-done.15.refs_9_ = bf16[256,1536]{1,0:T(8,128)(2,1)S(1)} collective-permute-done((bf16[256,1536]{1,0:T(8,128)(2,1)}, bf16[256,1536]{1,0:T(8,128)(2,1)S(1)}, u32[]{:S(2)}, u32[]{:S(2)}) %collective-permute-start.15) | collective-permute-done | bytes 786464 | tf_op jit(solution)/shard_map/ppermute | solution.py:42
  125.4 0.9 copy-done.8
  126.3 8.5 %shard_map.103 = (f32[512,128]{1,0:T(8,128)}, f32[512,128]{1,0:T(8,128)}, bf16[2,512,128]{2,1,0:T(8,128)(2,1)}) custom-call(s32[1]{0:T(128)} %bitcast.place, bf16[128,4096]{1,0:T(8,128)(2,1)} %tokens.1, bf16[128,4096]{1,0:T(8,128)(2,1)} %cotangent.1, bf16[512,512]{1,0:T(8,128)(2,1)} %fusion.4.turn, bf16[256,1536]{1,0:T(8,128)(2,1)} %collective-permute-done.3.refs_0_, ...), custom_call_target="tpu_custom_call" | custom-call | tf_op jit(solution)/shard_map/pallas_call | solution.py:256
  134.7 1.0 copy.32
  135.7 28.6 %all_to_all.20 = bf16[64,2,8,128]{3,2,1,0:T(8,128)(2,1)S(1)} all-to-all(bf16[64,2,8,128]{3,2,1,0:T(8,128)(2,1)S(1)} %copy.32), channel_id=1, replica_groups=mesh['seq'=64,'tp'=8] {'seq'}, dimensions={0} | all-to-all | bytes 524288 | tf_op jit(solution)/shard_map/all_to_all | solution.py:29
  164.4 1.2 shard_map.104
  165.6 0.9 copy.34
  166.5 5.6 %all-to-all-start.1 = ((bf16[64,2,8,128]{3,2,1,0:T(8,128)(2,1)}), bf16[64,2,8,128]{3,2,1,0:T(8,128)(2,1)S(1)}, u32[]{:S(2)}, u32[]{:S(2)}) async-start(bf16[64,2,8,128]{3,2,1,0:T(8,128)(2,1)} %copy.34), calls=%async_computation.1 | async-start | bytes 524288 | tf_op jit(solution)/shard_map/all_to_all | solution.py:29
  172.1 18.5 %all-to-all-done.1 = bf16[64,2,8,128]{3,2,1,0:T(8,128)(2,1)S(1)} async-done(((bf16[64,2,8,128]{3,2,1,0:T(8,128)(2,1)}), bf16[64,2,8,128]{3,2,1,0:T(8,128)(2,1)S(1)}, u32[]{:S(2)}, u32[]{:S(2)}) %all-to-all-start.1) | async-done | bytes 262176 | tf_op jit(solution)/shard_map/all_to_all | solution.py:29
  190.6 0.7 copy_bitcast_fusion.filtered
  191.3 10.6 %shard_map.105 = bf16[2,4,2,128,512]{4,3,2,1,0:T(8,128)(2,1)} custom-call(s32[1]{0:T(128)} %bitcast.place, f32[512,128]{1,0:T(8,128)} %get-tuple-element.68.gates, f32[512,128]{1,0:T(8,128)} %get-tuple-element.69.back, bf16[2,512,128]{2,1,0:T(8,128)(2,1)} %copy_bitcast_fusion.filtered, bf16[256,1536]{1,0:T(8,128)(2,1)} %collective-permute-done.3.refs_0_, ...), custom_call_target="tpu_custom_call" | custom-call | tf_op jit(solution)/shard_map/pallas_call | solution.py:308
  201.9 15.9 %all_to_all.21 = bf16[2,4,2,128,512]{4,3,2,1,0:T(8,128)(2,1)S(1)} all-to-all(bf16[2,4,2,128,512]{4,3,2,1,0:T(8,128)(2,1)} %shard_map.105), channel_id=1, replica_groups={{0,1},{2,3},{4,5},{6,7},{8,9},{10,11},{12,13},{14,15},{16,17},{18,19},{..., dimensions={0} | all-to-all | bytes 4194304 | tf_op jit(solution)/shard_map/all_to_all | solution.py:29
  217.8 0.6 convert_element_type.78
  218.3 1.4 fusion.3
  219.7 5.4 %all-to-all-start.3 = ((bf16[4,2,128,512]{3,2,1,0:T(8,128)(2,1)}), bf16[4,2,128,512]{3,2,1,0:T(8,128)(2,1)S(1)}, u32[]{:S(2)}, u32[]{:S(2)}) async-start(bf16[4,2,128,512]{3,2,1,0:T(8,128)(2,1)} %fusion.3), calls=%async_computation.3 | async-start | bytes 2097152 | tf_op jit(solution)/shard_map/all_to_all | solution.py:29
  225.6 0.4 fusion.9
  226.1 0.4 fusion.12
  226.6 1.5 multiply_reduce_fusion
  228.5 1.0 fusion.1
  229.6 1.1 fusion.2
  230.6 0.6 fusion.39
  231.2 19.2 %all-to-all-done.3 = bf16[4,2,128,512]{3,2,1,0:T(8,128)(2,1)S(1)} async-done(((bf16[4,2,128,512]{3,2,1,0:T(8,128)(2,1)}), bf16[4,2,128,512]{3,2,1,0:T(8,128)(2,1)S(1)}, u32[]{:S(2)}, u32[]{:S(2)}) %all-to-all-start.3) | async-done | bytes 1048608 | tf_op jit(solution)/shard_map/all_to_all | solution.py:29
  251.2 0.7 fusion.56
  (66 shorter events, 2.6 us)
Async XLA Ops:
  41.9 12.9 %collective-permute-start = (bf16[128,1536]{1,0:T(8,128)(2,1)S(1)}, bf16[128,1536]{1,0:T(8,128)(2,1)S(1)}, u32[]{:S(2)}, u32[]{:S(2)}) collective-permute-start(bf16[128,1536]{1,0:T(8,128)(2,1)S(1)} %get-tuple-element.83), channel_id=1, source_target_pairs={{0,24},{8,0},{16,8},{24,16},{32,56},{40,32},{48,40},{56,48},{64,88... | collective-permute-start | bytes 1179656 | tf_op jit(solution)/shard_map/ppermute | solution.py:42
  46.3 13.1 %collective-permute-start.4 = (bf16[128,1536]{1,0:T(8,128)(2,1)S(1)}, bf16[128,1536]{1,0:T(8,128)(2,1)S(1)}, u32[]{:S(2)}, u32[]{:S(2)}) collective-permute-start(bf16[128,1536]{1,0:T(8,128)(2,1)S(1)} %get-tuple-element.82), channel_id=1, source_target_pairs={{0,384},{128,0},{256,128},{384,256},{8,392},{136,8},{264,136},{392... | collective-permute-start | bytes 1179656 | tf_op jit(solution)/shard_map/ppermute | solution.py:42
  50.9 13.2 %collective-permute-start.2 = (bf16[128,1536]{1,0:T(8,128)(2,1)S(1)}, bf16[128,1536]{1,0:T(8,128)(2,1)S(1)}, u32[]{:S(2)}, u32[]{:S(2)}) collective-permute-start(bf16[128,1536]{1,0:T(8,128)(2,1)S(1)} %get-tuple-element.83), channel_id=1, source_target_pairs={{0,8},{8,16},{16,24},{24,0},{32,40},{40,48},{48,56},{56,32},{64,72... | collective-permute-start | bytes 1179656 | tf_op jit(solution)/shard_map/ppermute | solution.py:42
  52.8 15.9 %collective-permute-start.6 = (bf16[128,1536]{1,0:T(8,128)(2,1)S(1)}, bf16[128,1536]{1,0:T(8,128)(2,1)S(1)}, u32[]{:S(2)}, u32[]{:S(2)}) collective-permute-start(bf16[128,1536]{1,0:T(8,128)(2,1)S(1)} %get-tuple-element.82), channel_id=1, source_target_pairs={{0,128},{128,256},{256,384},{384,0},{8,136},{136,264},{264,392},{3... | collective-permute-start | bytes 1179656 | tf_op jit(solution)/shard_map/ppermute | solution.py:42
  54.8 9.4 %collective-permute-start.1 = (bf16[128,1536]{1,0:T(8,128)(2,1)S(1)}, bf16[128,1536]{1,0:T(8,128)(2,1)S(1)}, u32[]{:S(2)}, u32[]{:S(2)}) collective-permute-start(bf16[128,1536]{1,0:T(8,128)(2,1)S(1)} %collective-permute-done), channel_id=1, source_target_pairs={{0,24},{8,0},{16,8},{24,16},{32,56},{40,32},{48,40},{56,48},{64,88... | collective-permute-start | bytes 1179656 | tf_op jit(solution)/shard_map/ppermute | solution.py:42
  59.4 9.3 %collective-permute-start.5 = (bf16[128,1536]{1,0:T(8,128)(2,1)S(1)}, bf16[128,1536]{1,0:T(8,128)(2,1)S(1)}, u32[]{:S(2)}, u32[]{:S(2)}) collective-permute-start(bf16[128,1536]{1,0:T(8,128)(2,1)S(1)} %collective-permute-done.4), channel_id=1, source_target_pairs={{0,384},{128,0},{256,128},{384,256},{8,392},{136,8},{264,136},{392... | collective-permute-start | bytes 1179656 | tf_op jit(solution)/shard_map/ppermute | solution.py:42
  64.0 13.7 %copy-start = (bf16[256,1536]{1,0:T(8,128)(2,1)}, bf16[256,1536]{1,0:T(8,128)(2,1)S(1)}, u32[]{:S(2)}) copy-start(bf16[256,1536]{1,0:T(8,128)(2,1)S(1)} %pad_maximum_fusion.refs_12_) | copy-start | bytes 2359300
  64.1 61.3 %copy-start.1 = (bf16[256,1536]{1,0:T(8,128)(2,1)}, bf16[256,1536]{1,0:T(8,128)(2,1)S(1)}, u32[]{:S(2)}) copy-start(bf16[256,1536]{1,0:T(8,128)(2,1)S(1)} %pad_maximum_fusion.2.refs_13_) | copy-start | bytes 2359300
  64.1 51.1 %copy-start.9 = (f32[1,1,8,16]{3,2,1,0:T(8,128)S(1)}, f32[1,1,8,16]{3,2,1,0:T(8,128)}, u32[]{:S(2)}) copy-start(f32[1,1,8,16]{3,2,1,0:T(8,128)} %param.12) | copy-start | bytes 1540
  64.1 51.3 %copy-start.10 = (f32[1,1,8,16]{3,2,1,0:T(8,128)S(1)}, f32[1,1,8,16]{3,2,1,0:T(8,128)}, u32[]{:S(2)}) copy-start(f32[1,1,8,16]{3,2,1,0:T(8,128)} %param.11) | copy-start | bytes 1540
  64.2 61.2 %copy-start.2 = (bf16[256,1536]{1,0:T(8,128)(2,1)}, bf16[256,1536]{1,0:T(8,128)(2,1)S(1)}, u32[]{:S(2)}) copy-start(bf16[256,1536]{1,0:T(8,128)(2,1)S(1)} %pad_maximum_fusion.1.refs_14_) | copy-start | bytes 2359300
  64.2 21.3 %collective-permute-start.3 = (bf16[256,1536]{1,0:T(8,128)(2,1)S(1)}, bf16[256,1536]{1,0:T(8,128)(2,1)}, u32[]{:S(2)}, u32[]{:S(2)}) collective-permute-start(bf16[256,1536]{1,0:T(8,128)(2,1)S(1)} %pad_maximum_fusion.1.refs_14_), channel_id=1, source_target_pairs={{0,384},{128,0},{256,128},{384,256},{8,392},{136,8},{264,136},{392... | collective-permute-start | bytes 2359304 | tf_op jit(solution)/shard_map/ppermute | solution.py:42
  68.8 56.6 %copy-start.3 = (bf16[256,1536]{1,0:T(8,128)(2,1)}, bf16[256,1536]{1,0:T(8,128)(2,1)S(1)}, u32[]{:S(2)}) copy-start(bf16[256,1536]{1,0:T(8,128)(2,1)S(1)} %pad_maximum_fusion.3.refs_15_) | copy-start | bytes 2359300
  68.8 18.9 %collective-permute-start.7 = (bf16[256,1536]{1,0:T(8,128)(2,1)S(1)}, bf16[256,1536]{1,0:T(8,128)(2,1)}, u32[]{:S(2)}, u32[]{:S(2)}) collective-permute-start(bf16[256,1536]{1,0:T(8,128)(2,1)S(1)} %pad_maximum_fusion.3.refs_15_), channel_id=1, source_target_pairs={{0,24},{8,0},{16,8},{24,16},{32,56},{40,32},{48,40},{56,48},{64,88... | collective-permute-start | bytes 2359304 | tf_op jit(solution)/shard_map/ppermute | solution.py:42
  73.8 15.8 %collective-permute-start.8 = (bf16[256,1536]{1,0:T(8,128)(2,1)S(1)}, bf16[256,1536]{1,0:T(8,128)(2,1)}, u32[]{:S(2)}, u32[]{:S(2)}) collective-permute-start(bf16[256,1536]{1,0:T(8,128)(2,1)S(1)} %pad_maximum_fusion.refs_12_), channel_id=1, source_target_pairs={{0,128},{128,256},{256,384},{384,0},{8,136},{136,264},{264,392},{3... | collective-permute-start | bytes 2359304 | tf_op jit(solution)/shard_map/ppermute | solution.py:42
  75.8 17.0 %collective-permute-start.9 = (bf16[256,1536]{1,0:T(8,128)(2,1)S(1)}, bf16[256,1536]{1,0:T(8,128)(2,1)}, u32[]{:S(2)}, u32[]{:S(2)}) collective-permute-start(bf16[256,1536]{1,0:T(8,128)(2,1)S(1)} %pad_maximum_fusion.2.refs_13_), channel_id=1, source_target_pairs={{0,8},{8,16},{16,24},{24,0},{32,40},{40,48},{48,56},{56,32},{64,72... | collective-permute-start | bytes 2359304 | tf_op jit(solution)/shard_map/ppermute | solution.py:42
  77.7 24.6 %collective-permute-start.10 = (bf16[256,1536]{1,0:T(8,128)(2,1)S(1)}, bf16[256,1536]{1,0:T(8,128)(2,1)S(1)}, u32[]{:S(2)}, u32[]{:S(2)}) collective-permute-start(bf16[256,1536]{1,0:T(8,128)(2,1)S(1)} %pad_maximum_fusion.refs_12_), channel_id=1, source_target_pairs={{0,384},{128,0},{256,128},{384,256},{8,392},{136,8},{264,136},{392... | collective-permute-start | bytes 2359304 | tf_op jit(solution)/shard_map/ppermute | solution.py:42
  85.5 19.0 %collective-permute-start.11 = (bf16[256,1536]{1,0:T(8,128)(2,1)S(1)}, bf16[256,1536]{1,0:T(8,128)(2,1)S(1)}, u32[]{:S(2)}, u32[]{:S(2)}) collective-permute-start(bf16[256,1536]{1,0:T(8,128)(2,1)S(1)} %pad_maximum_fusion.2.refs_13_), channel_id=1, source_target_pairs={{0,24},{8,0},{16,8},{24,16},{32,56},{40,32},{48,40},{56,48},{64,88... | collective-permute-start | bytes 2359304 | tf_op jit(solution)/shard_map/ppermute | solution.py:42
  87.7 22.1 %collective-permute-start.12 = (bf16[256,1536]{1,0:T(8,128)(2,1)S(1)}, bf16[256,1536]{1,0:T(8,128)(2,1)S(1)}, u32[]{:S(2)}, u32[]{:S(2)}) collective-permute-start(bf16[256,1536]{1,0:T(8,128)(2,1)S(1)} %pad_maximum_fusion.1.refs_14_), channel_id=1, source_target_pairs={{0,128},{128,256},{256,384},{384,0},{8,136},{136,264},{264,392},{3... | collective-permute-start | bytes 2359304 | tf_op jit(solution)/shard_map/ppermute | solution.py:42
  89.6 27.0 %collective-permute-start.13 = (bf16[256,1536]{1,0:T(8,128)(2,1)S(1)}, bf16[256,1536]{1,0:T(8,128)(2,1)}, u32[]{:S(2)}, u32[]{:S(2)}) collective-permute-start(bf16[256,1536]{1,0:T(8,128)(2,1)S(1)} %pad_maximum_fusion.3.refs_15_), channel_id=1, source_target_pairs={{0,8},{8,16},{16,24},{24,0},{32,40},{40,48},{48,56},{56,32},{64,72... | collective-permute-start | bytes 2359304 | tf_op jit(solution)/shard_map/ppermute | solution.py:42
  92.8 29.1 %collective-permute-start.14 = (bf16[256,1536]{1,0:T(8,128)(2,1)}, bf16[256,1536]{1,0:T(8,128)(2,1)}, u32[]{:S(2)}, u32[]{:S(2)}) collective-permute-start(bf16[256,1536]{1,0:T(8,128)(2,1)} %collective-permute-done.8.refs_2_), channel_id=1, source_target_pairs={{0,128},{128,256},{256,384},{384,0},{8,136},{136,264},{264,392},{3... | collective-permute-start | bytes 2359304 | tf_op jit(solution)/shard_map/ppermute | solution.py:42
  102.3 7.5 %copy-start.5 = (bf16[256,1536]{1,0:T(8,128)(2,1)}, bf16[256,1536]{1,0:T(8,128)(2,1)S(1)}, u32[]{:S(2)}) copy-start(bf16[256,1536]{1,0:T(8,128)(2,1)S(1)} %collective-permute-done.10.refs_4_) | copy-start | bytes 2359300
  102.3 23.0 %collective-permute-start.15 = (bf16[256,1536]{1,0:T(8,128)(2,1)}, bf16[256,1536]{1,0:T(8,128)(2,1)S(1)}, u32[]{:S(2)}, u32[]{:S(2)}) collective-permute-start(bf16[256,1536]{1,0:T(8,128)(2,1)} %collective-permute-done.9.refs_3_), channel_id=1, source_target_pairs={{0,8},{8,16},{16,24},{24,0},{32,40},{40,48},{48,56},{56,32},{64,72... | collective-permute-start | bytes 2359304 | tf_op jit(solution)/shard_map/ppermute | solution.py:42
  104.5 9.7 %copy-start.6 = (bf16[256,1536]{1,0:T(8,128)(2,1)}, bf16[256,1536]{1,0:T(8,128)(2,1)S(1)}, u32[]{:S(2)}) copy-start(bf16[256,1536]{1,0:T(8,128)(2,1)S(1)} %collective-permute-done.11.refs_5_) | copy-start | bytes 2359300
  104.5 20.9 %collective-permute-start.16 = (bf16[256,1536]{1,0:T(8,128)(2,1)}, bf16[256,1536]{1,0:T(8,128)(2,1)}, u32[]{:S(2)}, u32[]{:S(2)}) collective-permute-start(bf16[256,1536]{1,0:T(8,128)(2,1)} %collective-permute-done.3.refs_0_), channel_id=1, source_target_pairs={{0,384},{128,0},{256,128},{384,256},{8,392},{136,8},{264,136},{392... | collective-permute-start | bytes 2359304 | tf_op jit(solution)/shard_map/ppermute | solution.py:42
  109.8 4.4 %copy-start.7 = (bf16[256,1536]{1,0:T(8,128)(2,1)}, bf16[256,1536]{1,0:T(8,128)(2,1)S(1)}, u32[]{:S(2)}) copy-start(bf16[256,1536]{1,0:T(8,128)(2,1)S(1)} %collective-permute-done.12.refs_6_) | copy-start | bytes 2359300
  109.8 15.5 %collective-permute-start.17 = (bf16[256,1536]{1,0:T(8,128)(2,1)}, bf16[256,1536]{1,0:T(8,128)(2,1)}, u32[]{:S(2)}, u32[]{:S(2)}) collective-permute-start(bf16[256,1536]{1,0:T(8,128)(2,1)} %collective-permute-done.7.refs_1_), channel_id=1, source_target_pairs={{0,24},{8,0},{16,8},{24,16},{32,56},{40,32},{48,40},{56,48},{64,88... | collective-permute-start | bytes 2359304 | tf_op jit(solution)/shard_map/ppermute | solution.py:42
  125.4 0.9 copy-start.8
  166.5 24.1 %all-to-all-start.1 = ((bf16[64,2,8,128]{3,2,1,0:T(8,128)(2,1)}), bf16[64,2,8,128]{3,2,1,0:T(8,128)(2,1)S(1)}, u32[]{:S(2)}, u32[]{:S(2)}) async-start(bf16[64,2,8,128]{3,2,1,0:T(8,128)(2,1)} %copy.34), calls=%async_computation.1 | async-start | bytes 524288 | tf_op jit(solution)/shard_map/all_to_all | solution.py:29
  219.7 30.7 %all-to-all-start.3 = ((bf16[4,2,128,512]{3,2,1,0:T(8,128)(2,1)}), bf16[4,2,128,512]{3,2,1,0:T(8,128)(2,1)S(1)}, u32[]{:S(2)}, u32[]{:S(2)}) async-start(bf16[4,2,128,512]{3,2,1,0:T(8,128)(2,1)} %fusion.3), calls=%async_computation.3 | async-start | bytes 2097152 | tf_op jit(solution)/shard_map/all_to_all | solution.py:29
  231.2 19.7 %copy-start.4 = (bf16[512,512]{1,0:T(8,128)(2,1)S(1)}, bf16[512,512]{1,0:T(8,128)(2,1)}, u32[]{:S(2)}) copy-start(bf16[512,512]{1,0:T(8,128)(2,1)} %fusion.4.turn) | copy-start | bytes 1572868
